TPU v7x, 256 devices: a whole 4x4x8 slice. The times are simulated.
256 devices in a mesh: chan: 64 (over z, y, core), row: 4 (over x).
Axes of the slice: x: 4, y: 4, z: 8, core: 2. Of those that a mesh axis runs over, the one named last changes fastest.
Arguments:
- counts: int32 [4, 64, 2048, 512], P('row', None, 'chan'), may hold values from 1 to 109, as said below
- template_mask: int32 [32, 2048], replicated, may hold values from 0 to 1, as said below
- weights_init: float32 [4, 64, 128, 512], P('row', 'chan'), may hold values from 0.05 to 0.5
- spectra_init: float32 [96, 2048], replicated, may hold values from 0.02 to 0.2
Outputs:
- weights: float32 [4, 64, 128, 512], P('row', 'chan')
- free_spectra: float32 [96, 2048], replicated
Inputs may be any that keep to these rules, and one draw needn't show every extreme that they name: `counts`: some entries reach the largest value. Every row of template_mask holds at least one 1.
All inputs are finite; a program needn't handle non-finite values.
Results may differ from a plain program's by a relative error of at most 0.00105.
Values may be sent and summed in bfloat16 or wider, within the bound.
No kernel may reach another device: no remote copies, remote signals or barrier semaphores. Data moves between devices by JAX's collectives and lax.ppermute only.
A program may use at most 64 MiB of HBM per device.

v0:
```python
import jax
import jax.numpy as jnp
from jax import lax
from jax.sharding import PartitionSpec as P

FIXED = 32
PASSES = 3
ITERS = 4


def padded_2(x, sides, width):
    for axis, dim in sides:
        size, length = (lax.axis_size(axis), x.shape[dim])
        up = [(i, (i + 1) % size) for i in range(size - 1)]
        down = [(j, i) for i, j in up]
        last = lax.slice_in_dim(x, length - width, length, axis=dim)
        first = lax.slice_in_dim(x, 0, width, axis=dim)
        before = lax.ppermute(last, axis, up)
        after = lax.ppermute(first, axis, down)
        x = jnp.concatenate([before, x, after], axis=dim)
    return x


def smooth_rows(padded):
    center = padded[:, 1:-1]
    side_cols = jnp.pad(center, ((0, 0), (0, 0), (0, 0), (1, 1)))
    beside = padded[:, 2:] + padded[:, :-2] + side_cols[..., 2:] + side_cols[..., :-2]
    return 0.4 * center + 0.15 * beside


def shards(counts, template_mask, weights_init, spectra_init):
    slab_field = counts.astype(jnp.float32)
    for repeat in range(PASSES):
        slab_field = smooth_rows(padded_2(slab_field, (("row", 1),), 1))
    smoothed = slab_field.astype(jnp.bfloat16)
    pixel_data = lax.all_to_all(smoothed, "chan", split_axis=1, concat_axis=2, tiled=True)[0]
    pixel_wide = pixel_data.astype(jnp.float32)
    weights = weights_init[0]
    template = template_mask.astype(jnp.float32)
    free_spectra = spectra_init
    for iteration in range(ITERS):
        spectra = jnp.concatenate([template, free_spectra], axis=0)
        spectra_low = spectra.astype(jnp.bfloat16)
        weight_den = jnp.sum(spectra, axis=1)
        weight_low = weights.astype(jnp.bfloat16)
        intensity = jnp.einsum(
            "kc,lkp->lcp", spectra_low, weight_low, preferred_element_type=jnp.float32
        )
        ratios = (pixel_wide / intensity).astype(jnp.bfloat16)
        numerator = jnp.einsum(
            "kc,lcp->lkp", spectra_low, ratios, preferred_element_type=jnp.float32
        )
        weights = weights * numerator / weight_den[None, :, None]
        new_low = weights.astype(jnp.bfloat16)
        new_intensity = jnp.einsum(
            "kc,lkp->lcp", spectra_low, new_low, preferred_element_type=jnp.float32
        )
        new_ratios = (pixel_wide / new_intensity).astype(jnp.bfloat16)
        spec_num = jnp.einsum(
            "lkp,lcp->kc", new_low[:, FIXED:], new_ratios, preferred_element_type=jnp.float32
        )
        spec_den = jnp.sum(weights[:, FIXED:], axis=(0, 2))
        spec_num, spec_den = lax.psum((spec_num, spec_den), ("chan", "row"))
        free_spectra = free_spectra * spec_num / spec_den[:, None]
    return (weights[None], free_spectra)


def solution(mesh):
    placed = (P("row", None, "chan", None), P(), P("row", "chan", None, None), P())
    return jax.shard_map(
        shards,
        mesh=mesh,
        in_specs=placed,
        out_specs=(P("row", "chan", None, None), P()),
        check_vma=False,
    )
```

profile of v0, /device:TPU:1, one launch (start us, length us, event | category | flops | bytes accessed | tf_op | source)
XLA Modules:
  0.0 1158.9 jit_solution(8989174163527005638)
XLA Ops:
  7.2 2.7 bitcast_convert_fusion
  9.9 1.3 collective-permute-start
  11.2 4.6 collective-permute-start.1
  15.8 0.0 collective-permute-done
  15.8 1.3 collective-permute-done.1
  17.1 3.1 fusion.3
  20.2 1.3 collective-permute-start.2
  21.5 4.3 collective-permute-start.3
  25.9 0.0 collective-permute-done.2
  25.9 1.3 collective-permute-done.3
  27.2 3.1 fusion.7
  30.3 1.3 collective-permute-start.4
  31.6 0.0 copy-start.1
  31.6 0.0 copy-start
  31.6 4.5 collective-permute-start.5
  36.1 0.0 collective-permute-done.4
  36.1 1.3 collective-permute-done.5
  37.4 4.2 fusion.12
  41.6 0.0 copy-start.3
  41.6 16.3 %all-to-all-start = ((bf16[1,64,32,512]{3,2,0,1:T(8,128)(2,1)}), bf16[1,64,32,512]{3,2,0,1:T(8,128)(2,1)}, u32[]{:S(2)}, u32[]{:S(2)}) async-start(bf16[1,64,32,512]{3,2,0,1:T(8,128)(2,1)} %fusion.12), calls=%async_computation | async-start | bytes 4194304 | tf_op jit(solution)/shard_map/all_to_all | solution.py:36
  57.9 0.0 all-reduce.8.cloned.1.call-start
  58.0 0.0 copy-done.1
  58.0 0.0 copy-done
  58.0 0.1 fusion.52
  58.1 49.4 %all-to-all-done = bf16[1,64,32,512]{3,2,0,1:T(8,128)(2,1)} async-done(((bf16[1,64,32,512]{3,2,0,1:T(8,128)(2,1)}), bf16[1,64,32,512]{3,2,0,1:T(8,128)(2,1)}, u32[]{:S(2)}, u32[]{:S(2)}) %all-to-all-start) | async-done | bytes 2097184 | tf_op jit(solution)/shard_map/all_to_all | solution.py:36
  107.5 0.0 copy-done.3
  107.5 2.6 fusion.119
  110.1 3.9 fusion.32
  114.0 0.0 all-reduce.8.cloned.1.call-update
  114.0 0.0 all-reduce.10.cloned.1.call-start
  114.1 0.1 slice_reduce_fusion.3
  114.2 79.2 %psum.57 = f32[96]{0:T(128)S(1)} all-reduce(f32[96]{0:T(128)S(1)} %slice_reduce_fusion.3), channel_id=1, replica_groups=mesh['chan'=64,'row'=4] {'chan','row'}, use_global_device_ids=true, to_apply=%region_3.4 | all-reduce | flops 96 | bytes 768 | tf_op jit(solution)/shard_map/psum | solution.py:63
  193.4 173.4 %all-reduce.8.cloned.1.call-done = f32[96,2048]{1,0:T(8,128)} async-done(((f32[96,2048]{1,0:T(8,128)}), f32[96,2048]{1,0:T(8,128)}) %all-reduce.8.cloned.1.call-update) | async-done | bytes 786448 | tf_op jit(solution)/shard_map/psum | solution.py:63
  366.8 1.3 multiply_divide_fusion.3
  368.1 0.1 fusion.54
  368.2 2.7 fusion.124
  370.9 3.9 fusion.33
  374.8 0.0 all-reduce.10.cloned.1.call-update
  374.8 0.0 all-reduce.12.cloned.1.call-start
  374.9 0.1 slice_reduce_fusion.2
  375.0 78.1 %psum.59 = f32[96]{0:T(128)S(1)} all-reduce(f32[96]{0:T(128)S(1)} %slice_reduce_fusion.2), channel_id=1, replica_groups=mesh['chan'=64,'row'=4] {'chan','row'}, use_global_device_ids=true, to_apply=%region_7.8 | all-reduce | flops 96 | bytes 768 | tf_op jit(solution)/shard_map/psum | solution.py:63
  453.1 175.0 %all-reduce.10.cloned.1.call-done = f32[96,2048]{1,0:T(8,128)} async-done(((f32[96,2048]{1,0:T(8,128)}), f32[96,2048]{1,0:T(8,128)}) %all-reduce.10.cloned.1.call-update) | async-done | bytes 786448 | tf_op jit(solution)/shard_map/psum | solution.py:63
  628.1 1.3 multiply_divide_fusion.2
  629.3 0.1 fusion.56
  629.5 2.7 fusion.129
  632.2 3.9 fusion.34
  636.0 0.0 all-reduce.12.cloned.1.call-update
  636.1 0.0 all-reduce.14.cloned.1.call-start
  636.1 0.1 slice_reduce_fusion.1
  636.2 78.1 %psum.61 = f32[96]{0:T(128)S(1)} all-reduce(f32[96]{0:T(128)S(1)} %slice_reduce_fusion.1), channel_id=1, replica_groups=mesh['chan'=64,'row'=4] {'chan','row'}, use_global_device_ids=true, to_apply=%region_11.12 | all-reduce | flops 96 | bytes 768 | tf_op jit(solution)/shard_map/psum | solution.py:63
  714.3 174.9 %all-reduce.12.cloned.1.call-done = f32[96,2048]{1,0:T(8,128)} async-done(((f32[96,2048]{1,0:T(8,128)}), f32[96,2048]{1,0:T(8,128)}) %all-reduce.12.cloned.1.call-update) | async-done | bytes 786448 | tf_op jit(solution)/shard_map/psum | solution.py:63
  889.2 1.3 multiply_divide_fusion.1
  890.4 0.1 fusion.58
  890.6 2.7 fusion.134
  893.3 0.0 copy-start.2
  893.3 4.0 fusion.35
  897.3 0.0 all-reduce.14.cloned.1.call-update
  897.3 0.0 copy-done.2
  897.3 0.1 slice_reduce_fusion
  897.4 78.0 %psum.63 = f32[96]{0:T(128)S(1)} all-reduce(f32[96]{0:T(128)S(1)} %slice_reduce_fusion), channel_id=1, replica_groups=mesh['chan'=64,'row'=4] {'chan','row'}, use_global_device_ids=true, to_apply=%region_15.16 | all-reduce | flops 96 | bytes 768 | tf_op jit(solution)/shard_map/psum | solution.py:63
  975.5 174.8 %all-reduce.14.cloned.1.call-done = f32[96,2048]{1,0:T(8,128)} async-done(((f32[96,2048]{1,0:T(8,128)}), f32[96,2048]{1,0:T(8,128)}) %all-reduce.14.cloned.1.call-update) | async-done | bytes 786448 | tf_op jit(solution)/shard_map/psum | solution.py:63
  1150.2 2.1 multiply_divide_fusion
  (4 shorter events, 0.1 us)
Async XLA Ops:
  9.9 5.9 collective-permute-start
  11.2 5.9 collective-permute-start.1
  20.2 5.6 collective-permute-start.2
  21.5 5.6 collective-permute-start.3
  30.3 5.8 collective-permute-start.4
  31.6 26.4 %copy-start.1 = (s32[32,2048]{1,0:T(8,128)S(1)}, s32[32,2048]{1,0:T(8,128)}, u32[]{:S(2)}) copy-start(s32[32,2048]{1,0:T(8,128)} %param.5) | copy-start | bytes 786436
  31.6 26.4 %copy-start = (f32[96,2048]{1,0:T(8,128)S(1)}, f32[96,2048]{1,0:T(8,128)}, u32[]{:S(2)}) copy-start(f32[96,2048]{1,0:T(8,128)} %param.7) | copy-start | bytes 2359300
  31.6 5.8 collective-permute-start.5
  41.6 65.9 %copy-start.3 = (f32[1,1,128,512]{3,2,1,0:T(8,128)S(1)}, f32[1,1,128,512]{3,2,1,0:T(8,128)}, u32[]{:S(2)}) copy-start(f32[1,1,128,512]{3,2,1,0:T(8,128)} %param.6) | copy-start | bytes 786436
  41.6 65.9 %all-to-all-start = ((bf16[1,64,32,512]{3,2,0,1:T(8,128)(2,1)}), bf16[1,64,32,512]{3,2,0,1:T(8,128)(2,1)}, u32[]{:S(2)}, u32[]{:S(2)}) async-start(bf16[1,64,32,512]{3,2,0,1:T(8,128)(2,1)} %fusion.12), calls=%async_computation | async-start | bytes 4194304 | tf_op jit(solution)/shard_map/all_to_all | solution.py:36
  57.9 308.9 %all-reduce.8.cloned.1.call-start = ((), (), s32[]{:S(2)}) async-start(), calls=%async_computation.1 | async-start | bytes 1572864 | tf_op jit(solution)/shard_map/psum | solution.py:63
  114.0 514.0 %all-reduce.10.cloned.1.call-start = ((), (), s32[]{:S(2)}) async-start(), calls=%async_computation.2 | async-start | bytes 1572864 | tf_op jit(solution)/shard_map/psum | solution.py:63
  374.8 514.4 %all-reduce.12.cloned.1.call-start = ((), (), s32[]{:S(2)}) async-start(), calls=%async_computation.3 | async-start | bytes 1572864 | tf_op jit(solution)/shard_map/psum | solution.py:63
  636.1 514.2 %all-reduce.14.cloned.1.call-start = ((), (), s32[]{:S(2)}) async-start(), calls=%async_computation.4 | async-start | bytes 1572864 | tf_op jit(solution)/shard_map/psum | solution.py:63
  893.3 4.0 copy-start.2
Sparse Core Ops, SparseCore 0:
  114.2 252.5 all-reduce.7
  374.9 253.0 all-reduce.9
  636.2 252.9 all-reduce.11
  897.4 252.7 all-reduce.13
where the time goes:
time: 1160 us
  waiting for transfers between devices  751 us (65%)
  blocking collectives  313 us (27%)
  starting transfers between devices  33.7 us (3%)
  matrix products  26.3 us (2%)
  other arithmetic  20 us (2%)
  between operations  14 us (1%)
    psum x4, waiting for transfers between devices, shards(): spec_num, spec_den = lax.psum((spec_num, spec_den), ('chan', 'row'))  698 us
    psum x4, blocking collectives, shards(): spec_num, spec_den = lax.psum((spec_num, spec_den), ('chan', 'row'))  313 us
    all_to_all x1, waiting for transfers between devices, shards(): lax.all_to_all(smoothed, 'chan', split_axis=1, concat_axis=2, tiled=True)[0]  49.4 us
  transfers between devices with their start and end apart: 11, of which 8 were waited for; matrix products, arithmetic and copies ran while one was open for 0% of the time, Pallas kernels for 0%

commit v1 on v0

v1 whole, which is shorter than its diff:
```python
import jax
import jax.numpy as jnp
import numpy as np
from jax import lax
from jax.sharding import PartitionSpec as P

FIXED = 32
FREE = 96
PASSES = 3
ITERS = 4
CHAN = ("z", "y", "core")
PLANE = ("y", "row")
CORES = 2
HALF = FREE // CORES
LANES = 128


def with_rims(counts):
    size = lax.axis_size("row")
    up = [(i, i + 1) for i in range(size - 1)]
    down = [(j, i) for i, j in up]
    first = counts[:, :PASSES].astype(jnp.bfloat16)
    last = counts[:, -PASSES:].astype(jnp.bfloat16)
    before = lax.ppermute(last, "row", up)
    after = lax.ppermute(first, "row", down)
    parts = [before.astype(jnp.float32), counts.astype(jnp.float32), after.astype(jnp.float32)]
    return jnp.concatenate(parts, axis=1)


def smoothed(counts):
    field = with_rims(counts)
    lines = counts.shape[1]
    row, last = lax.axis_index("row"), lax.axis_size("row") - 1
    for step in range(PASSES):
        center = field[:, 1:-1]
        side = jnp.pad(center, ((0, 0), (0, 0), (0, 0), (1, 1)))
        beside = field[:, 2:] + field[:, :-2] + side[..., 2:] + side[..., :-2]
        field = 0.4 * center + 0.15 * beside
        rim = PASSES - 1 - step
        if rim:
            at = jnp.arange(lines + 2 * rim)
            inside = ((at >= rim) | (row > 0)) & ((at < lines + rim) | (row < last))
            field = jnp.where(inside[None, :, None, None], field, 0.0)
    return field.astype(jnp.bfloat16)


def to_all(x, axes):
    count = 1
    for axis in axes:
        count *= lax.axis_size(axis)
    return lax.all_to_all(jnp.broadcast_to(x[None], (count,) + x.shape), axes, 0, 0, tiled=True)


def summed_block(num, den):
    shards = num.shape[1] // LANES
    mine = lax.axis_index("core")
    blocks = num.reshape(CORES, HALF, shards, LANES).transpose(0, 2, 1, 3)
    rows = jnp.pad(den.reshape(CORES, 1, 1, HALF), ((0, 0), (0, 0), (0, 7), (0, LANES - HALF)))
    rows = jnp.broadcast_to(rows, (CORES, shards, 8, LANES))
    blocks = jnp.concatenate([blocks, rows], axis=2)
    kept = lax.dynamic_index_in_dim(blocks, mine, 0, keepdims=False)
    sent = lax.dynamic_index_in_dim(blocks, 1 - mine, 0, keepdims=False)
    chip = kept + lax.ppermute(sent, "core", [(0, 1), (1, 0)])
    plane = jnp.sum(lax.all_to_all(chip, PLANE, 0, 0, tiled=True), axis=0)
    total = jnp.sum(to_all(plane, ("z",)), axis=0)
    return total[:HALF], total[HALF, :HALF]


def gathered(block):
    halves = lax.all_gather(to_all(block, PLANE), "core")
    return halves.transpose(0, 2, 1, 3).reshape(FREE, -1)


def shards(counts, template_mask, weights_init, spectra_init):
    pixel_data = lax.all_to_all(smoothed(counts), CHAN, split_axis=1, concat_axis=2, tiled=True)[0]
    pixel_wide = pixel_data.astype(jnp.float32)
    weights = weights_init[0]
    template = template_mask.astype(jnp.float32)
    free_spectra = spectra_init
    shard = lax.axis_index("y") * lax.axis_size("row") + lax.axis_index("row")
    block = lax.dynamic_slice(
        spectra_init, (lax.axis_index("core") * HALF, shard * LANES), (HALF, LANES)
    )
    for iteration in range(ITERS):
        spectra = jnp.concatenate([template, free_spectra], axis=0)
        spectra_low = spectra.astype(jnp.bfloat16)
        weight_den = jnp.sum(spectra, axis=1)
        weight_low = weights.astype(jnp.bfloat16)
        intensity = jnp.einsum(
            "kc,lkp->lcp", spectra_low, weight_low, preferred_element_type=jnp.float32
        )
        ratios = (pixel_wide / intensity).astype(jnp.bfloat16)
        numerator = jnp.einsum(
            "kc,lcp->lkp", spectra_low, ratios, preferred_element_type=jnp.float32
        )
        weights = weights * numerator / weight_den[None, :, None]
        new_low = weights.astype(jnp.bfloat16)
        new_intensity = jnp.einsum(
            "kc,lkp->lcp", spectra_low, new_low, preferred_element_type=jnp.float32
        )
        new_ratios = (pixel_wide / new_intensity).astype(jnp.bfloat16)
        spec_num = jnp.einsum(
            "lkp,lcp->kc", new_low[:, FIXED:], new_ratios, preferred_element_type=jnp.float32
        )
        spec_den = jnp.sum(weights[:, FIXED:], axis=(0, 2))
        block_num, block_den = summed_block(spec_num, spec_den)
        block = block * block_num / block_den[:, None]
        free_spectra = gathered(block)
    return (weights[None], free_spectra)


def solution(mesh):
    devices = np.asarray(mesh.devices)
    fine = jax.sharding.Mesh(devices.reshape(8, 4, 2, 4), ("z", "y", "core", "row"))
    placed = (P("row", None, CHAN, None), P(), P("row", CHAN, None, None), P())
    return jax.shard_map(
        shards,
        mesh=fine,
        in_specs=placed,
        out_specs=(P("row", CHAN, None, None), P()),
        check_vma=False,
    )
```

time: 1160 us -> 317 us (0.27)
  waiting for transfers between devices: 751 us -> 68.4 us
  blocking collectives: 313 us -> 160 us
  between operations: 14 us -> 1.13 us
    psum x4 -> x0, waiting for transfers between devices: 698 us -> none  [shards(): spec_num, spec_den = lax.psum((spec_num, spec_den), ('chan', 'row'))]
    psum x4 -> x0, blocking collectives: 313 us -> none  [shards(): spec_num, spec_den = lax.psum((spec_num, spec_den), ('chan', 'row'))]
    all_to_all x0 -> x11, blocking collectives: none -> 136 us  [the longest x7 82.2 us: to_all(): lax.all_to_all(jnp.broadcast_to(x[None], (count,) + x.shape), axes, 0, 0,...]
    all_gather x0 -> x4, blocking collectives: none -> 24.4 us  [gathered(): halves = lax.all_gather(to_all(block, PLANE), 'core')]
    dot_general x0 -> x4, matrix products: none -> 11.7 us  [shards(): jnp.einsum('kc,lkp->lcp', spectra_low, new_low, preferred_element_type=jn...]
    all_to_all x1 -> x2, waiting for transfers between devices: 49.4 us -> 58.3 us  [the longest x1 49.5 us: shards(): lax.all_to_all(smoothed(counts), CHAN, split_axis=1, concat_axis=2, tiled...]
  transfers between devices with their start and end apart: 11 -> 8, of which waited for: 8 -> 8; matrix products, arithmetic and copies ran while one was open for 0% -> 0% of each run, Pallas kernels for 0% -> 0%
where the time goes in v1:
time: 317 us; the launch traced here: 316 us
  blocking collectives  160 us (50%)
  waiting for transfers between devices  68.4 us (22%)
  matrix products  30.3 us (10%)
  starting transfers between devices  26 us (8%)
  other arithmetic  23.5 us (7%)
  local copies, waits for them, and re-layouts  6.66 us (2%)
    all_to_all x7, blocking collectives, to_all(): lax.all_to_all(jnp.broadcast_to(x[None], (count,) + x.shape), axes, 0, 0,...  82.2 us
    all_to_all x4, blocking collectives, summed_block(): plane = jnp.sum(lax.all_to_all(chip, PLANE, 0, 0, tiled=True), axis=0)  53.6 us
    all_to_all x1, waiting for transfers between devices, shards(): lax.all_to_all(smoothed(counts), CHAN, split_axis=1, concat_axis=2, tiled...  49.5 us
    all_gather x4, blocking collectives, gathered(): halves = lax.all_gather(to_all(block, PLANE), 'core')  24.4 us
    all_to_all x1, starting transfers between devices, shards(): lax.all_to_all(smoothed(counts), CHAN, split_axis=1, concat_axis=2, tiled...  13.9 us
    dot_general x4, matrix products, shards(): jnp.einsum('kc,lkp->lcp', spectra_low, new_low, preferred_element_type=jn...  11.7 us
    dot_general x4, matrix products, shards(): jnp.einsum('lkp,lcp->kc', new_low[:, FIXED:], new_ratios, preferred_eleme...  9.38 us
    dot_general x4, matrix products, shards(): jnp.einsum('kc,lcp->lkp', spectra_low, ratios, preferred_element_type=jnp...  9.2 us
  transfers between devices with their start and end apart: 8, of which 8 were waited for; matrix products, arithmetic and copies ran while one was open for 0% of the time, Pallas kernels for 0%

profile of v1, /device:TPU:1, one launch (start us, length us, event | category | flops | bytes accessed | tf_op | source)
XLA Modules:
  0.0 316.2 jit_solution(1793145094733820677)
XLA Ops:
  0.6 5.1 %bitcast_convert_fusion = (f32[1,64,32,512]{3,2,0,1:T(8,128)}, bf16[1,64,32,512]{3,2,0,1:T(8,128)(2,1)S(1)}) fusion(s32[1,64,32,512]{3,2,1,0:T(8,128)} %param.4), kind=kLoop, calls=%fused_computation.41 | loop fusion | flops 2097152 | bytes 10485760 | tf_op jit(solution)/shard_map/convert_element_type | solution.py:26
  5.7 4.0 %collective-permute-start = (bf16[1,3,32,512]{3,2,0,1:T(8,128)(2,1)S(1)}, bf16[1,3,32,512]{3,2,0,1:T(8,128)(2,1)S(1)}, u32[]{:S(2)}, u32[]{:S(2)}) collective-permute-start(bf16[1,3,32,512]{3,2,0,1:T(8,128)(2,1)S(1)} %get-tuple-element.4), channel_id=1, source_target_pairs={{0,1},{1,2},{2,3},{4,5},{5,6},{6,7},{8,9},{9,10},{10,11},{12,13},{... | collective-permute-start | bytes 294920 | tf_op jit(solution)/shard_map/ppermute | solution.py:24
  9.7 1.3 collective-permute-start.1
  11.0 0.3 collective-permute-done
  11.3 3.7 %collective-permute-done.1 = bf16[1,3,32,512]{3,2,0,1:T(8,128)(2,1)S(1)} collective-permute-done((bf16[1,3,32,512]{3,2,0,1:T(8,128)(2,1)S(1)}, bf16[1,3,32,512]{3,2,0,1:T(8,128)(2,1)S(1)}, u32[]{:S(2)}, u32[]{:S(2)}) %collective-permute-start.1) | collective-permute-done | bytes 98336 | tf_op jit(solution)/shard_map/ppermute | solution.py:25
  15.0 3.1 pad_maximum_fusion
  18.1 0.8 slice.136
  19.0 3.4 %fusion.4 = f32[1,68,32,512]{3,2,0,1:T(8,128)S(1)} fusion(f32[1,68,32,512]{3,2,0,1:T(8,128)S(1)} %slice.136, f32[1,70,32,512]{3,2,0,1:T(8,128)S(1)} %pad_maximum_fusion, pred[68]{0:T(512)(128)(4,1)S(1)} %or_and_fusion), kind=kLoop, calls=%fused_computation.19 | loop fusion | flops 7798784 | bytes 17825860 | tf_op jit(solution)/shard_map/jit(_where)/select_n | solution.py:43
  22.3 0.8 slice.139
  23.2 3.3 %fusion.9 = f32[1,66,32,512]{3,2,0,1:T(8,128)S(1)} fusion(f32[1,66,32,512]{3,2,0,1:T(8,128)S(1)} %slice.139, f32[1,68,32,512]{3,2,0,1:T(8,128)S(1)} %fusion.4, pred[66]{0:T(512)(128)(4,1)S(1)} %or_and_fusion.1), kind=kLoop, calls=%fused_computation.25 | loop fusion | flops 7569408 | bytes 17301570 | tf_op jit(solution)/shard_map/jit(_where)/select_n | solution.py:43
  26.5 0.8 slice.142
  27.3 4.2 %fusion.14 = bf16[1,64,32,512]{3,2,0,1:T(8,128)(2,1)} fusion(f32[1,64,32,512]{3,2,0,1:T(8,128)S(1)} %slice.142, f32[1,66,32,512]{3,2,0,1:T(8,128)S(1)} %fusion.9), kind=kLoop, calls=%fused_computation.31 | loop fusion | flops 7340032 | bytes 14680064 | tf_op jit(solution)/shard_map/convert_element_type | solution.py:44
  31.5 13.9 %all-to-all-start = ((bf16[1,64,32,512]{3,2,0,1:T(8,128)(2,1)}), bf16[1,64,32,512]{3,2,0,1:T(8,128)(2,1)S(1)}, u32[]{:S(2)}, u32[]{:S(2)}) async-start(bf16[1,64,32,512]{3,2,0,1:T(8,128)(2,1)} %fusion.14), calls=%async_computation | async-start | bytes 4194304 | tf_op jit(solution)/shard_map/all_to_all | solution.py:75
  45.6 49.5 %all-to-all-done = bf16[1,64,32,512]{3,2,0,1:T(8,128)(2,1)S(1)} async-done(((bf16[1,64,32,512]{3,2,0,1:T(8,128)(2,1)}), bf16[1,64,32,512]{3,2,0,1:T(8,128)(2,1)S(1)}, u32[]{:S(2)}, u32[]{:S(2)}) %all-to-all-start) | async-done | bytes 2097184 | tf_op jit(solution)/shard_map/all_to_all | solution.py:75
  95.1 2.7 fusion.123
  97.8 2.2 fusion.16
  100.2 2.3 convolution_bitcast_fusion.3
  102.6 0.8 fusion.67
  103.4 2.1 collective-permute-start.2
  105.5 1.8 collective-permute-done.2
  107.3 1.1 fusion.70
  108.4 16.0 %all_to_all.69 = f32[16,56,128]{2,1,0:T(8,128)S(1)} all-to-all(f32[16,56,128]{2,1,0:T(8,128)S(1)} %fusion.70), channel_id=1, replica_groups=mesh['z'=8,'y'=4,'core'=2,'row'=4] {'y','row'}, dimensions={0} | all-to-all | bytes 917504 | tf_op jit(solution)/shard_map/all_to_all | solution.py:64
  124.4 0.7 broadcast_in_dim.64
  125.1 3.4 %all-to-all-start.2 = ((f32[8,56,128]{2,1,0:T(8,128)}), f32[8,56,128]{2,1,0:T(8,128)S(1)}, u32[]{:S(2)}, u32[]{:S(2)}) async-start(f32[8,56,128]{2,1,0:T(8,128)} %broadcast_in_dim.64), calls=%async_computation.2 | async-start | bytes 458752 | tf_op jit(solution)/shard_map/all_to_all | solution.py:51
  128.5 8.8 %all-to-all-done.2 = f32[8,56,128]{2,1,0:T(8,128)S(1)} async-done(((f32[8,56,128]{2,1,0:T(8,128)}), f32[8,56,128]{2,1,0:T(8,128)S(1)}, u32[]{:S(2)}, u32[]{:S(2)}) %all-to-all-start.2) | async-done | bytes 229408 | tf_op jit(solution)/shard_map/all_to_all | solution.py:51
  137.3 0.8 fusion.100
  138.2 12.1 %all_to_all.70 = f32[16,48,128]{2,1,0:T(8,128)S(1)} all-to-all(f32[16,48,128]{2,1,0:T(8,128)S(1)} %broadcast_in_dim.65), channel_id=1, replica_groups=mesh['z'=8,'y'=4,'core'=2,'row'=4] {'y','row'}, dimensions={0} | all-to-all | bytes 786432 | tf_op jit(solution)/shard_map/all_to_all | solution.py:51
  150.3 6.1 %all-gather = f32[32,48,128]{2,1,0:T(8,128)S(1)} all-gather(f32[16,48,128]{2,1,0:T(8,128)S(1)} %all_to_all.70), channel_id=2, replica_groups=mesh['z'=8,'y'=4,'core'=2,'row'=4] {'core'}, dimensions={0}, use_global_device_ids=true | all-gather | bytes 1179648 | tf_op jit(solution)/shard_map/all_gather | solution.py:70
  156.4 0.2 copy.64
  156.6 0.2 copy.99
  157.0 1.8 fusion.128
  158.8 3.2 %fusion.18 = bf16[1,2048,512]{2,1,0:T(8,128)(2,1)} fusion(bf16[1,2048,512]{2,1,0:T(8,128)(2,1)S(1)} %bitcast.344, f32[96,2048]{1,0:T(8,128)S(1)} %bitcast.337, f32[32,2048]{1,0:T(8,128)S(1)} %convert_element_type.108, f32[1,128,512]{2,1,0:T(8,128)} %get-tuple-element.9), kind=kOutput, calls=%fused_computation.35 | convolution fusion | flops 272695296 | bytes 5505024 | tf_op jit(solution)/shard_map/kc,lkp->lcp/dot_general | solution.py:98
  162.2 2.3 convolution_bitcast_fusion.2
  164.7 0.5 collective-permute-start.3
  165.1 1.4 collective-permute-done.3
  166.6 12.6 %all_to_all.71 = f32[16,56,128]{2,1,0:T(8,128)S(1)} all-to-all(f32[16,56,128]{2,1,0:T(8,128)S(1)} %fusion.65), channel_id=1, replica_groups=mesh['z'=8,'y'=4,'core'=2,'row'=4] {'y','row'}, dimensions={0} | all-to-all | bytes 917504 | tf_op jit(solution)/shard_map/all_to_all | solution.py:64
  179.2 11.3 %all_to_all.72 = f32[8,56,128]{2,1,0:T(8,128)S(1)} all-to-all(f32[8,56,128]{2,1,0:T(8,128)S(1)} %broadcast_in_dim.119), channel_id=1, replica_groups=mesh['z'=8,'y'=4,'core'=2,'row'=4] {'z'}, dimensions={0} | all-to-all | bytes 458752 | tf_op jit(solution)/shard_map/all_to_all | solution.py:51
  190.7 12.1 %all_to_all.73 = f32[16,48,128]{2,1,0:T(8,128)S(1)} all-to-all(f32[16,48,128]{2,1,0:T(8,128)S(1)} %broadcast_in_dim.120), channel_id=1, replica_groups=mesh['z'=8,'y'=4,'core'=2,'row'=4] {'y','row'}, dimensions={0} | all-to-all | bytes 786432 | tf_op jit(solution)/shard_map/all_to_all | solution.py:51
  202.8 6.1 %all-gather.1 = f32[32,48,128]{2,1,0:T(8,128)S(1)} all-gather(f32[16,48,128]{2,1,0:T(8,128)S(1)} %all_to_all.73), channel_id=3, replica_groups=mesh['z'=8,'y'=4,'core'=2,'row'=4] {'core'}, dimensions={0}, use_global_device_ids=true | all-gather | bytes 1179648 | tf_op jit(solution)/shard_map/all_gather | solution.py:70
  208.9 0.2 copy.68
  209.1 0.2 copy.98
  209.5 1.8 fusion.133
  211.3 3.2 %fusion.20 = bf16[1,2048,512]{2,1,0:T(8,128)(2,1)} fusion(bf16[1,2048,512]{2,1,0:T(8,128)(2,1)S(1)} %bitcast.346, f32[96,2048]{1,0:T(8,128)S(1)} %bitcast.340, f32[32,2048]{1,0:T(8,128)S(1)} %convert_element_type.108, f32[1,128,512]{2,1,0:T(8,128)} %get-tuple-element.11), kind=kOutput, calls=%fused_computation.37 | convolution fusion | flops 272695296 | bytes 5505024 | tf_op jit(solution)/shard_map/kc,lkp->lcp/dot_general | solution.py:98
  214.7 2.3 convolution_bitcast_fusion.1
  217.2 0.5 collective-permute-start.4
  217.6 1.4 collective-permute-done.4
  219.1 12.6 %all_to_all.74 = f32[16,56,128]{2,1,0:T(8,128)S(1)} all-to-all(f32[16,56,128]{2,1,0:T(8,128)S(1)} %fusion.60), channel_id=1, replica_groups=mesh['z'=8,'y'=4,'core'=2,'row'=4] {'y','row'}, dimensions={0} | all-to-all | bytes 917504 | tf_op jit(solution)/shard_map/all_to_all | solution.py:64
  231.7 11.3 %all_to_all.75 = f32[8,56,128]{2,1,0:T(8,128)S(1)} all-to-all(f32[8,56,128]{2,1,0:T(8,128)S(1)} %broadcast_in_dim.123), channel_id=1, replica_groups=mesh['z'=8,'y'=4,'core'=2,'row'=4] {'z'}, dimensions={0} | all-to-all | bytes 458752 | tf_op jit(solution)/shard_map/all_to_all | solution.py:51
  243.2 12.1 %all_to_all.76 = f32[16,48,128]{2,1,0:T(8,128)S(1)} all-to-all(f32[16,48,128]{2,1,0:T(8,128)S(1)} %broadcast_in_dim.124), channel_id=1, replica_groups=mesh['z'=8,'y'=4,'core'=2,'row'=4] {'y','row'}, dimensions={0} | all-to-all | bytes 786432 | tf_op jit(solution)/shard_map/all_to_all | solution.py:51
  255.3 6.1 %all-gather.2 = f32[32,48,128]{2,1,0:T(8,128)S(1)} all-gather(f32[16,48,128]{2,1,0:T(8,128)S(1)} %all_to_all.76), channel_id=4, replica_groups=mesh['z'=8,'y'=4,'core'=2,'row'=4] {'core'}, dimensions={0}, use_global_device_ids=true | all-gather | bytes 1179648 | tf_op jit(solution)/shard_map/all_gather | solution.py:70
  261.4 0.2 copy.72
  261.6 0.2 copy.97
  261.9 0.1 fusion.49
  262.0 2.8 fusion.138
  264.8 3.2 %fusion.22 = bf16[1,2048,512]{2,1,0:T(8,128)(2,1)} fusion(bf16[1,2048,512]{2,1,0:T(8,128)(2,1)S(1)} %bitcast.348, bf16[1,128,512]{2,1,0:T(8,128)(2,1)} %get-tuple-element.12, f32[96,2048]{1,0:T(8,128)S(1)} %bitcast.334, f32[32,2048]{1,0:T(8,128)S(1)} %convert_element_type.108), kind=kOutput, calls=%fused_computation.39 | convolution fusion | flops 272629760 | bytes 5373952 | tf_op jit(solution)/shard_map/kc,lkp->lcp/dot_general | solution.py:98
  268.2 2.4 convolution_bitcast_fusion
  270.6 0.4 collective-permute-start.5
  271.1 1.5 collective-permute-done.5
  272.6 12.5 %all_to_all.77 = f32[16,56,128]{2,1,0:T(8,128)S(1)} all-to-all(f32[16,56,128]{2,1,0:T(8,128)S(1)} %fusion.55), channel_id=1, replica_groups=mesh['z'=8,'y'=4,'core'=2,'row'=4] {'y','row'}, dimensions={0} | all-to-all | bytes 917504 | tf_op jit(solution)/shard_map/all_to_all | solution.py:64
  285.2 11.3 %all_to_all.78 = f32[8,56,128]{2,1,0:T(8,128)S(1)} all-to-all(f32[8,56,128]{2,1,0:T(8,128)S(1)} %broadcast_in_dim.128), channel_id=1, replica_groups=mesh['z'=8,'y'=4,'core'=2,'row'=4] {'z'}, dimensions={0} | all-to-all | bytes 458752 | tf_op jit(solution)/shard_map/all_to_all | solution.py:51
  296.6 12.1 %all_to_all.79 = f32[16,48,128]{2,1,0:T(8,128)S(1)} all-to-all(f32[16,48,128]{2,1,0:T(8,128)S(1)} %broadcast_in_dim.129), channel_id=1, replica_groups=mesh['z'=8,'y'=4,'core'=2,'row'=4] {'y','row'}, dimensions={0} | all-to-all | bytes 786432 | tf_op jit(solution)/shard_map/all_to_all | solution.py:51
  308.7 6.1 %all-gather.3 = f32[32,48,128]{2,1,0:T(8,128)S(1)} all-gather(f32[16,48,128]{2,1,0:T(8,128)S(1)} %all_to_all.79), channel_id=5, replica_groups=mesh['z'=8,'y'=4,'core'=2,'row'=4] {'core'}, dimensions={0}, use_global_device_ids=true | all-gather | bytes 1179648 | tf_op jit(solution)/shard_map/all_gather | solution.py:70
  314.8 0.2 copy.76
  315.1 1.1 copy.96
  (79 shorter events, 2.3 us)
Async XLA Ops:
  5.7 5.6 %collective-permute-start = (bf16[1,3,32,512]{3,2,0,1:T(8,128)(2,1)S(1)}, bf16[1,3,32,512]{3,2,0,1:T(8,128)(2,1)S(1)}, u32[]{:S(2)}, u32[]{:S(2)}) collective-permute-start(bf16[1,3,32,512]{3,2,0,1:T(8,128)(2,1)S(1)} %get-tuple-element.4), channel_id=1, source_target_pairs={{0,1},{1,2},{2,3},{4,5},{5,6},{6,7},{8,9},{9,10},{10,11},{12,13},{... | collective-permute-start | bytes 294920 | tf_op jit(solution)/shard_map/ppermute | solution.py:24
  9.7 5.4 %collective-permute-start.1 = (bf16[1,3,32,512]{3,2,0,1:T(8,128)(2,1)S(1)}, bf16[1,3,32,512]{3,2,0,1:T(8,128)(2,1)S(1)}, u32[]{:S(2)}, u32[]{:S(2)}) collective-permute-start(bf16[1,3,32,512]{3,2,0,1:T(8,128)(2,1)S(1)} %get-tuple-element.5), channel_id=1, source_target_pairs={{1,0},{2,1},{3,2},{5,4},{6,5},{7,6},{9,8},{10,9},{11,10},{13,12},{... | collective-permute-start | bytes 294920 | tf_op jit(solution)/shard_map/ppermute | solution.py:25
  31.5 13.9 %copy-start.1 = (s32[32,2048]{1,0:T(8,128)S(1)}, s32[32,2048]{1,0:T(8,128)}, u32[]{:S(2)}) copy-start(s32[32,2048]{1,0:T(8,128)} %param.5) | copy-start | bytes 786436
  31.5 13.9 %copy-start = (f32[96,2048]{1,0:T(8,128)S(1)}, f32[96,2048]{1,0:T(8,128)}, u32[]{:S(2)}) copy-start(f32[96,2048]{1,0:T(8,128)} %param.7) | copy-start | bytes 2359300
  31.5 63.6 %all-to-all-start = ((bf16[1,64,32,512]{3,2,0,1:T(8,128)(2,1)}), bf16[1,64,32,512]{3,2,0,1:T(8,128)(2,1)S(1)}, u32[]{:S(2)}, u32[]{:S(2)}) async-start(bf16[1,64,32,512]{3,2,0,1:T(8,128)(2,1)} %fusion.14), calls=%async_computation | async-start | bytes 4194304 | tf_op jit(solution)/shard_map/all_to_all | solution.py:75
  97.8 2.3 copy-start.8
  103.4 3.9 %collective-permute-start.2 = (f32[16,56,128]{2,1,0:T(8,128)}, f32[16,56,128]{2,1,0:T(8,128)}, u32[]{:S(2)}, u32[]{:S(2)}) collective-permute-start(f32[16,56,128]{2,1,0:T(8,128)} %fusion.67), channel_id=1, source_target_pairs={{0,4},{4,0},{1,5},{5,1},{2,6},{6,2},{3,7},{7,3},{8,12},{12,8},{9,1... | collective-permute-start | bytes 1376264 | tf_op jit(solution)/shard_map/ppermute | solution.py:63
  125.1 12.2 %all-to-all-start.2 = ((f32[8,56,128]{2,1,0:T(8,128)}), f32[8,56,128]{2,1,0:T(8,128)S(1)}, u32[]{:S(2)}, u32[]{:S(2)}) async-start(f32[8,56,128]{2,1,0:T(8,128)} %broadcast_in_dim.64), calls=%async_computation.2 | async-start | bytes 458752 | tf_op jit(solution)/shard_map/all_to_all | solution.py:51
  158.8 3.2 %copy-start.3 = (f32[1,128,512]{2,1,0:T(8,128)S(1)}, f32[1,128,512]{2,1,0:T(8,128)}, u32[]{:S(2)}) copy-start(f32[1,128,512]{2,1,0:T(8,128)} %get-tuple-element.9) | copy-start | bytes 786436
  158.8 3.3 %copy-start.6 = (bf16[1,128,512]{2,1,0:T(8,128)(2,1)S(1)}, bf16[1,128,512]{2,1,0:T(8,128)(2,1)}, u32[]{:S(2)}) copy-start(bf16[1,128,512]{2,1,0:T(8,128)(2,1)} %get-tuple-element.8) | copy-start | bytes 393220
  164.7 1.9 collective-permute-start.3
  211.3 3.2 %copy-start.4 = (f32[1,128,512]{2,1,0:T(8,128)S(1)}, f32[1,128,512]{2,1,0:T(8,128)}, u32[]{:S(2)}) copy-start(f32[1,128,512]{2,1,0:T(8,128)} %get-tuple-element.11) | copy-start | bytes 786436
  211.3 3.3 %copy-start.7 = (bf16[1,128,512]{2,1,0:T(8,128)(2,1)S(1)}, bf16[1,128,512]{2,1,0:T(8,128)(2,1)}, u32[]{:S(2)}) copy-start(bf16[1,128,512]{2,1,0:T(8,128)(2,1)} %get-tuple-element.10) | copy-start | bytes 393220
  217.2 1.9 collective-permute-start.4
  264.8 3.2 %copy-start.2 = (f32[1,128,512]{2,1,0:T(8,128)}, f32[1,128,512]{2,1,0:T(8,128)S(1)}, u32[]{:S(2)}) copy-start(f32[1,128,512]{2,1,0:T(8,128)S(1)} %get-tuple-element.13) | copy-start | bytes 786436
  264.8 3.2 %copy-start.5 = (bf16[1,128,512]{2,1,0:T(8,128)(2,1)S(1)}, bf16[1,128,512]{2,1,0:T(8,128)(2,1)}, u32[]{:S(2)}) copy-start(bf16[1,128,512]{2,1,0:T(8,128)(2,1)} %get-tuple-element.12) | copy-start | bytes 393220
  270.6 1.9 collective-permute-start.5

commit v2 on v1

v2 whole, which is shorter than its diff:
```python
import jax
import jax.numpy as jnp
import numpy as np
from jax import lax
from jax.experimental import pallas as pl
from jax.experimental.pallas import tpu as pltpu
from jax.sharding import PartitionSpec as P

FIXED = 32
FREE = 96
PASSES = 3
ITERS = 4
CHAN = ("z", "y", "core")
PLANE = ("y", "row")
CORES = 2
HALF = FREE // CORES
LANES = 128
DEN_ROWS = 8
CHUNK = 256
VMEM = pl.BlockSpec(memory_space=pltpu.VMEM)
SMEM = pl.BlockSpec(memory_space=pltpu.SMEM)


def with_rims(counts):
    size = lax.axis_size("row")
    up = [(i, i + 1) for i in range(size - 1)]
    down = [(j, i) for i, j in up]
    first = counts[:, :PASSES].astype(jnp.bfloat16)
    last = counts[:, -PASSES:].astype(jnp.bfloat16)
    before = lax.ppermute(last, "row", up)
    after = lax.ppermute(first, "row", down)
    parts = [before.astype(jnp.float32), counts.astype(jnp.float32), after.astype(jnp.float32)]
    return jnp.concatenate(parts, axis=1)


def smoothed(counts):
    field = with_rims(counts)
    lines = counts.shape[1]
    row, last = lax.axis_index("row"), lax.axis_size("row") - 1
    for step in range(PASSES):
        center = field[:, 1:-1]
        side = jnp.pad(center, ((0, 0), (0, 0), (0, 0), (1, 1)))
        beside = field[:, 2:] + field[:, :-2] + side[..., 2:] + side[..., :-2]
        field = 0.4 * center + 0.15 * beside
        rim = PASSES - 1 - step
        if rim:
            at = jnp.arange(lines + 2 * rim)
            inside = ((at >= rim) | (row > 0)) & ((at < lines + rim) | (row < last))
            field = jnp.where(inside[None, :, None, None], field, 0.0)
    return field.astype(jnp.bfloat16)


def to_all(x, axes):
    count = 1
    for axis in axes:
        count *= lax.axis_size(axis)
    return lax.all_to_all(jnp.broadcast_to(x[None], (count,) + x.shape), axes, 0, 0, tiled=True)


def summed_block(kept, sent):
    chip = kept + lax.ppermute(sent, "core", [(0, 1), (1, 0)])
    plane = jnp.sum(lax.all_to_all(chip, PLANE, 0, 0, tiled=True), axis=0)
    total = jnp.sum(to_all(plane, ("z",)), axis=0)
    return total[:HALF], total[HALF, :HALF]


def update_kernel(core, data, template, halves, weights, new_weights, kept, sent, low, low_t):
    channels, pixels = data.shape
    shards = channels // LANES
    den = [jnp.sum(template[...].astype(jnp.float32), axis=1, keepdims=True)]
    low[:FIXED] = template[...]
    for half in range(CORES):
        rows = pl.ds(FIXED + half * HALF, HALF)
        total = jnp.zeros((HALF, LANES), jnp.float32)
        for shard in range(shards):
            part = halves[half, shard]
            total = total + part
            low[rows, pl.ds(shard * LANES, LANES)] = part.astype(jnp.bfloat16)
        den.append(jnp.sum(total, axis=1, keepdims=True))
    weight_den = jnp.concatenate(den, axis=0)
    for shard in range(shards):
        low_t[pl.ds(shard * LANES, LANES), :] = low[:, pl.ds(shard * LANES, LANES)].T

    old = weights[...]
    old_low = old.astype(jnp.bfloat16)

    def ratios_of(chunk, held):
        part = pl.ds(chunk * CHUNK, CHUNK)
        intensity = jnp.dot(low_t[part, :], held, preferred_element_type=jnp.float32)
        return (data[part, :].astype(jnp.float32) / intensity).astype(jnp.bfloat16)

    numerator = jnp.zeros(old.shape, jnp.float32)
    for chunk in range(channels // CHUNK):
        ratios = ratios_of(chunk, old_low)
        numerator += jnp.dot(
            low[:, pl.ds(chunk * CHUNK, CHUNK)], ratios, preferred_element_type=jnp.float32
        )
    new = old * numerator / weight_den
    new_weights[...] = new
    new_low = new.astype(jnp.bfloat16)
    mine = core[0]
    sums = jnp.sum(new[FIXED:], axis=1, keepdims=True)
    at = lax.broadcasted_iota(jnp.int32, (HALF, LANES), 0)
    lane = lax.broadcasted_iota(jnp.int32, (HALF, LANES), 1)
    den_rows = []
    for half in range(CORES):
        column = jnp.broadcast_to(sums[half * HALF : (half + 1) * HALF], (HALF, LANES))
        row = jnp.sum(jnp.where(at == lane, column, 0.0), axis=0, keepdims=True)
        den_rows.append(jnp.broadcast_to(row, (DEN_ROWS, LANES)))
    first = mine == 0
    kept_row = jnp.where(first, den_rows[0], den_rows[1])
    sent_row = jnp.where(first, den_rows[1], den_rows[0])
    for chunk in range(channels // CHUNK):
        ratios = ratios_of(chunk, new_low)
        terms = lax.dot_general(
            new_low[FIXED:], ratios, (((1,), (1,)), ((), ())), preferred_element_type=jnp.float32
        )
        for part in range(CHUNK // LANES):
            shard = chunk * (CHUNK // LANES) + part
            upper = terms[:HALF, part * LANES : (part + 1) * LANES]
            lower = terms[HALF:, part * LANES : (part + 1) * LANES]
            kept[shard, :HALF] = jnp.where(first, upper, lower)
            sent[shard, :HALF] = jnp.where(first, lower, upper)
            kept[shard, HALF:] = kept_row
            sent[shard, HALF:] = sent_row


def update(core, data, template, halves, weights):
    channels = data.shape[0]
    message = jax.ShapeDtypeStruct((channels // LANES, HALF + DEN_ROWS, LANES), jnp.float32)
    components = template.shape[0] + FREE
    return pl.pallas_call(
        update_kernel,
        out_shape=(jax.ShapeDtypeStruct(weights.shape, jnp.float32), message, message),
        in_specs=[SMEM, VMEM, VMEM, VMEM, VMEM],
        out_specs=(VMEM, VMEM, VMEM),
        scratch_shapes=[
            pltpu.VMEM((components, channels), jnp.bfloat16),
            pltpu.VMEM((channels, components), jnp.bfloat16),
        ],
        compiler_params=pltpu.CompilerParams(vmem_limit_bytes=32 * 1024 * 1024),
        name="update",
    )(core, data, template, halves, weights)


def shards(counts, template_mask, weights_init, spectra_init):
    pixel_data = lax.all_to_all(smoothed(counts), CHAN, split_axis=1, concat_axis=2, tiled=True)
    data = pixel_data.reshape(-1, pixel_data.shape[-1])
    core = lax.axis_index("core")
    template = template_mask.astype(jnp.bfloat16)
    weights = weights_init[0, 0]
    shard = lax.axis_index("y") * lax.axis_size("row") + lax.axis_index("row")
    halves = spectra_init.reshape(CORES, HALF, -1, LANES).transpose(0, 2, 1, 3)
    block = halves[core, shard]
    for iteration in range(ITERS):
        weights, kept, sent = update(core[None], data, template, halves, weights)
        num, den = summed_block(kept, sent)
        block = block * num / den[:, None]
        halves = lax.all_gather(to_all(block, PLANE), "core")
    free_spectra = halves.transpose(0, 2, 1, 3).reshape(FREE, -1)
    return (weights[None, None], free_spectra)


def solution(mesh):
    devices = np.asarray(mesh.devices)
    fine = jax.sharding.Mesh(devices.reshape(8, 4, 2, 4), ("z", "y", "core", "row"))
    placed = (P("row", None, CHAN, None), P(), P("row", CHAN, None, None), P())
    return jax.shard_map(
        shards,
        mesh=fine,
        in_specs=placed,
        out_specs=(P("row", CHAN, None, None), P()),
        check_vma=False,
    )
```

time: 317 us -> 295 us (0.931)
  matrix products: 30.3 us -> 0 us
  Pallas kernels: 0 us -> 14.4 us
  other arithmetic: 23.5 us -> 19.8 us
    dot_general x12 -> x0, matrix products: 30.3 us -> none  [the longest x4 11.7 us: shards(): jnp.einsum('kc,lkp->lcp', spectra_low, new_low, preferred_element_type=jn...]
    pallas_call x0 -> x4, Pallas kernels: none -> 14.4 us  [update(): pl.pallas_call(update_kernel, out_shape=(jax.ShapeDtypeStruct(weights.sha...]
where the time goes in v2:
time: 295 us; the launch traced here: 294 us
  blocking collectives  160 us (54%)
  waiting for transfers between devices  66 us (22%)
  starting transfers between devices  26.1 us (9%)
  other arithmetic  19.8 us (7%)
  Pallas kernels  14.4 us (5%)
  local copies, waits for them, and re-layouts  6.93 us (2%)
    all_to_all x7, blocking collectives, to_all(): lax.all_to_all(jnp.broadcast_to(x[None], (count,) + x.shape), axes, 0, 0,...  82.2 us
    all_to_all x4, blocking collectives, summed_block(): plane = jnp.sum(lax.all_to_all(chip, PLANE, 0, 0, tiled=True), axis=0)  53.6 us
    all_to_all x1, waiting for transfers between devices, shards(): lax.all_to_all(smoothed(counts), CHAN, split_axis=1, concat_axis=2, tiled...  48.4 us
    all_gather x4, blocking collectives, shards(): halves = lax.all_gather(to_all(block, PLANE), 'core')  24.4 us
    pallas_call x4, Pallas kernels, update(): pl.pallas_call(update_kernel, out_shape=(jax.ShapeDtypeStruct(weights.sha...  14.4 us
    all_to_all x1, starting transfers between devices, shards(): lax.all_to_all(smoothed(counts), CHAN, split_axis=1, concat_axis=2, tiled...  13.9 us
    all_to_all x1, waiting for transfers between devices, to_all(): lax.all_to_all(jnp.broadcast_to(x[None], (count,) + x.shape), axes, 0, 0,...  7.83 us
    select_n x2, other arithmetic, smoothed(): field = jnp.where(inside[None, :, None, None], field, 0.0)  6.67 us
  transfers between devices with their start and end apart: 8, of which 8 were waited for; matrix products, arithmetic and copies ran while one was open for 0% of the time, Pallas kernels for 0%

profile of v2, /device:TPU:1, one launch (start us, length us, event | category | flops | bytes accessed | tf_op | source)
XLA Modules:
  0.0 294.4 jit_solution(17775787727379252946)
XLA Ops:
  0.6 5.1 %bitcast_convert_fusion = (f32[1,64,32,512]{3,2,0,1:T(8,128)}, bf16[1,64,32,512]{3,2,0,1:T(8,128)(2,1)S(1)}) fusion(s32[1,64,32,512]{3,2,1,0:T(8,128)} %param.4), kind=kLoop, calls=%fused_computation.25 | loop fusion | flops 2097152 | bytes 10485760 | tf_op jit(solution)/shard_map/convert_element_type | solution.py:32
  5.7 4.0 %collective-permute-start = (bf16[1,3,32,512]{3,2,0,1:T(8,128)(2,1)S(1)}, bf16[1,3,32,512]{3,2,0,1:T(8,128)(2,1)S(1)}, u32[]{:S(2)}, u32[]{:S(2)}) collective-permute-start(bf16[1,3,32,512]{3,2,0,1:T(8,128)(2,1)S(1)} %get-tuple-element.28), channel_id=1, source_target_pairs={{0,1},{1,2},{2,3},{4,5},{5,6},{6,7},{8,9},{9,10},{10,11},{12,13},{... | collective-permute-start | bytes 294920 | tf_op jit(solution)/shard_map/ppermute | solution.py:30
  9.7 1.3 collective-permute-start.1
  11.0 0.3 collective-permute-done
  11.3 3.7 %collective-permute-done.1 = bf16[1,3,32,512]{3,2,0,1:T(8,128)(2,1)S(1)} collective-permute-done((bf16[1,3,32,512]{3,2,0,1:T(8,128)(2,1)S(1)}, bf16[1,3,32,512]{3,2,0,1:T(8,128)(2,1)S(1)}, u32[]{:S(2)}, u32[]{:S(2)}) %collective-permute-start.1) | collective-permute-done | bytes 98336 | tf_op jit(solution)/shard_map/ppermute | solution.py:31
  15.0 3.1 %pad_maximum_fusion = f32[1,70,32,512]{3,2,0,1:T(8,128)S(1)} fusion(f32[1,3,32,512]{3,2,0,1:T(8,128)S(1)} %convert_element_type.25, f32[1,64,32,512]{3,2,0,1:T(8,128)} %get-tuple-element.26, f32[1,3,32,512]{3,2,0,1:T(8,128)S(1)} %convert_element_type.23), kind=kLoop, calls=%fused_computation.6 | loop fusion | flops 2293760 | bytes 9175040 | tf_op jit(solution)/shard_map/concatenate | solution.py:33
  18.1 0.8 slice.104
  19.0 3.4 %fusion.4 = f32[1,68,32,512]{3,2,0,1:T(8,128)S(1)} fusion(f32[1,68,32,512]{3,2,0,1:T(8,128)S(1)} %slice.104, f32[1,70,32,512]{3,2,0,1:T(8,128)S(1)} %pad_maximum_fusion, pred[68]{0:T(512)(128)(4,1)S(1)} %or_and_fusion), kind=kLoop, calls=%fused_computation.11 | loop fusion | flops 7798784 | bytes 17825860 | tf_op jit(solution)/shard_map/jit(_where)/select_n | solution.py:49
  22.3 0.8 slice.107
  23.2 3.3 %fusion.9 = f32[1,66,32,512]{3,2,0,1:T(8,128)S(1)} fusion(f32[1,66,32,512]{3,2,0,1:T(8,128)S(1)} %slice.107, f32[1,68,32,512]{3,2,0,1:T(8,128)S(1)} %fusion.4, pred[66]{0:T(512)(128)(4,1)S(1)} %or_and_fusion.1), kind=kLoop, calls=%fused_computation.17 | loop fusion | flops 7569408 | bytes 17301570 | tf_op jit(solution)/shard_map/jit(_where)/select_n | solution.py:49
  26.5 0.8 slice.110
  27.3 4.2 %fusion.14 = bf16[1,64,32,512]{3,2,0,1:T(8,128)(2,1)} fusion(f32[1,64,32,512]{3,2,0,1:T(8,128)S(1)} %slice.110, f32[1,66,32,512]{3,2,0,1:T(8,128)S(1)} %fusion.9), kind=kLoop, calls=%fused_computation.23 | loop fusion | flops 7340032 | bytes 14680064 | tf_op jit(solution)/shard_map/convert_element_type | solution.py:50
  31.5 0.0 copy-start.3
  31.5 0.0 copy-start.2
  31.5 0.0 copy-start
  31.5 13.9 %all-to-all-start = ((bf16[1,64,32,512]{3,2,0,1:T(8,128)(2,1)}), bf16[1,64,32,512]{3,2,0,1:T(8,128)(2,1)S(1)}, u32[]{:S(2)}, u32[]{:S(2)}) async-start(bf16[1,64,32,512]{3,2,0,1:T(8,128)(2,1)} %fusion.14), calls=%async_computation | async-start | bytes 4194304 | tf_op jit(solution)/shard_map/all_to_all | solution.py:147
  45.4 0.0 copy-done.3
  45.5 0.0 copy-done.2
  45.5 0.1 copy.17
  45.6 0.0 copy-start.1
  45.6 0.9 copy-done.1
  46.5 0.2 copy.22
  46.7 48.4 %all-to-all-done = bf16[1,64,32,512]{3,2,0,1:T(8,128)(2,1)S(1)} async-done(((bf16[1,64,32,512]{3,2,0,1:T(8,128)(2,1)}), bf16[1,64,32,512]{3,2,0,1:T(8,128)(2,1)S(1)}, u32[]{:S(2)}, u32[]{:S(2)}) %all-to-all-start) | async-done | bytes 2097184 | tf_op jit(solution)/shard_map/all_to_all | solution.py:147
  95.1 0.0 copy-done
  95.1 3.6 %update.4 = (f32[128,512]{1,0:T(8,128)S(1)}, f32[16,56,128]{2,1,0:T(8,128)S(1)}, f32[16,56,128]{2,1,0:T(8,128)S(1)}) custom-call(s32[1]{0:T(128)} %bitcast.core, bf16[2048,512]{1,0:T(8,128)(2,1)S(1)} %bitcast.33, bf16[32,2048]{1,0:T(8,128)(2,1)S(1)} %convert_element_type.27.template, f32[2,16,48,128]{3,2,1,0:T(8,128)S(1)} %bitcast.38, f32[128,512]{1,0:T(8,128)S(1)} %bitcast.41), custom_call_target="tpu_custom_call" | custom-call | tf_op jit(solution)/shard_map/update/pallas_call | solution.py:132
  98.7 2.2 collective-permute-start.2
  100.9 1.4 collective-permute-done.2
  102.4 0.1 add.78
  102.4 16.0 %all_to_all.69 = f32[16,56,128]{2,1,0:T(8,128)S(1)} all-to-all(f32[16,56,128]{2,1,0:T(8,128)S(1)} %add.78), channel_id=1, replica_groups=mesh['z'=8,'y'=4,'core'=2,'row'=4] {'y','row'}, dimensions={0} | all-to-all | bytes 917504 | tf_op jit(solution)/shard_map/all_to_all | solution.py:62
  118.4 0.7 broadcast_in_dim.49
  119.1 3.4 %all-to-all-start.2 = ((f32[8,56,128]{2,1,0:T(8,128)}), f32[8,56,128]{2,1,0:T(8,128)S(1)}, u32[]{:S(2)}, u32[]{:S(2)}) async-start(f32[8,56,128]{2,1,0:T(8,128)} %broadcast_in_dim.49), calls=%async_computation.2 | async-start | bytes 458752 | tf_op jit(solution)/shard_map/all_to_all | solution.py:57
  122.5 1.0 constant_dynamic-slice_fusion
  123.5 7.8 %all-to-all-done.2 = f32[8,56,128]{2,1,0:T(8,128)S(1)} async-done(((f32[8,56,128]{2,1,0:T(8,128)}), f32[8,56,128]{2,1,0:T(8,128)S(1)}, u32[]{:S(2)}, u32[]{:S(2)}) %all-to-all-start.2) | async-done | bytes 229408 | tf_op jit(solution)/shard_map/all_to_all | solution.py:57
  131.4 0.1 fusion.18
  131.5 12.1 %all_to_all.70 = f32[16,48,128]{2,1,0:T(8,128)S(1)} all-to-all(f32[16,48,128]{2,1,0:T(8,128)S(1)} %broadcast_in_dim.50), channel_id=1, replica_groups=mesh['z'=8,'y'=4,'core'=2,'row'=4] {'y','row'}, dimensions={0} | all-to-all | bytes 786432 | tf_op jit(solution)/shard_map/all_to_all | solution.py:57
  143.6 6.1 %all-gather = f32[32,48,128]{2,1,0:T(8,128)S(1)} all-gather(f32[16,48,128]{2,1,0:T(8,128)S(1)} %all_to_all.70), channel_id=2, replica_groups=mesh['z'=8,'y'=4,'core'=2,'row'=4] {'core'}, dimensions={0}, use_global_device_ids=true | all-gather | bytes 1179648 | tf_op jit(solution)/shard_map/all_gather | solution.py:159
  149.7 3.6 %update.5 = (f32[128,512]{1,0:T(8,128)S(1)}, f32[16,56,128]{2,1,0:T(8,128)S(1)}, f32[16,56,128]{2,1,0:T(8,128)S(1)}) custom-call(s32[1]{0:T(128)} %bitcast.core, bf16[2048,512]{1,0:T(8,128)(2,1)S(1)} %bitcast.34, bf16[32,2048]{1,0:T(8,128)(2,1)S(1)} %convert_element_type.27.template, f32[2,16,48,128]{3,2,1,0:T(8,128)S(1)} %bitcast.39, ...), custom_call_target="tpu_custom_call" | custom-call | tf_op jit(solution)/shard_map/update/pallas_call | solution.py:132
  153.3 0.5 collective-permute-start.3
  153.7 1.4 collective-permute-done.3
  155.2 12.5 %all_to_all.71 = f32[16,56,128]{2,1,0:T(8,128)S(1)} all-to-all(f32[16,56,128]{2,1,0:T(8,128)S(1)} %add.79), channel_id=1, replica_groups=mesh['z'=8,'y'=4,'core'=2,'row'=4] {'y','row'}, dimensions={0} | all-to-all | bytes 917504 | tf_op jit(solution)/shard_map/all_to_all | solution.py:62
  167.8 11.3 %all_to_all.72 = f32[8,56,128]{2,1,0:T(8,128)S(1)} all-to-all(f32[8,56,128]{2,1,0:T(8,128)S(1)} %broadcast_in_dim.51), channel_id=1, replica_groups=mesh['z'=8,'y'=4,'core'=2,'row'=4] {'z'}, dimensions={0} | all-to-all | bytes 458752 | tf_op jit(solution)/shard_map/all_to_all | solution.py:57
  179.2 0.1 fusion.17
  179.3 12.1 %all_to_all.73 = f32[16,48,128]{2,1,0:T(8,128)S(1)} all-to-all(f32[16,48,128]{2,1,0:T(8,128)S(1)} %broadcast_in_dim.52), channel_id=1, replica_groups=mesh['z'=8,'y'=4,'core'=2,'row'=4] {'y','row'}, dimensions={0} | all-to-all | bytes 786432 | tf_op jit(solution)/shard_map/all_to_all | solution.py:57
  191.4 6.1 %all-gather.1 = f32[32,48,128]{2,1,0:T(8,128)S(1)} all-gather(f32[16,48,128]{2,1,0:T(8,128)S(1)} %all_to_all.73), channel_id=3, replica_groups=mesh['z'=8,'y'=4,'core'=2,'row'=4] {'core'}, dimensions={0}, use_global_device_ids=true | all-gather | bytes 1179648 | tf_op jit(solution)/shard_map/all_gather | solution.py:159
  197.5 3.6 %update.6 = (f32[128,512]{1,0:T(8,128)S(1)}, f32[16,56,128]{2,1,0:T(8,128)S(1)}, f32[16,56,128]{2,1,0:T(8,128)S(1)}) custom-call(s32[1]{0:T(128)} %bitcast.core, bf16[2048,512]{1,0:T(8,128)(2,1)S(1)} %bitcast.35, bf16[32,2048]{1,0:T(8,128)(2,1)S(1)} %convert_element_type.27.template, f32[2,16,48,128]{3,2,1,0:T(8,128)S(1)} %bitcast.40, ...), custom_call_target="tpu_custom_call" | custom-call | tf_op jit(solution)/shard_map/update/pallas_call | solution.py:132
  201.1 0.5 collective-permute-start.4
  201.5 1.4 collective-permute-done.4
  203.0 12.6 %all_to_all.74 = f32[16,56,128]{2,1,0:T(8,128)S(1)} all-to-all(f32[16,56,128]{2,1,0:T(8,128)S(1)} %add.80), channel_id=1, replica_groups=mesh['z'=8,'y'=4,'core'=2,'row'=4] {'y','row'}, dimensions={0} | all-to-all | bytes 917504 | tf_op jit(solution)/shard_map/all_to_all | solution.py:62
  215.6 11.3 %all_to_all.75 = f32[8,56,128]{2,1,0:T(8,128)S(1)} all-to-all(f32[8,56,128]{2,1,0:T(8,128)S(1)} %broadcast_in_dim.53), channel_id=1, replica_groups=mesh['z'=8,'y'=4,'core'=2,'row'=4] {'z'}, dimensions={0} | all-to-all | bytes 458752 | tf_op jit(solution)/shard_map/all_to_all | solution.py:57
  226.9 0.1 fusion.16
  227.1 12.1 %all_to_all.76 = f32[16,48,128]{2,1,0:T(8,128)S(1)} all-to-all(f32[16,48,128]{2,1,0:T(8,128)S(1)} %broadcast_in_dim.54), channel_id=1, replica_groups=mesh['z'=8,'y'=4,'core'=2,'row'=4] {'y','row'}, dimensions={0} | all-to-all | bytes 786432 | tf_op jit(solution)/shard_map/all_to_all | solution.py:57
  239.1 6.1 %all-gather.2 = f32[32,48,128]{2,1,0:T(8,128)S(1)} all-gather(f32[16,48,128]{2,1,0:T(8,128)S(1)} %all_to_all.76), channel_id=4, replica_groups=mesh['z'=8,'y'=4,'core'=2,'row'=4] {'core'}, dimensions={0}, use_global_device_ids=true | all-gather | bytes 1179648 | tf_op jit(solution)/shard_map/all_gather | solution.py:159
  245.2 3.6 %update.7 = (f32[128,512]{1,0:T(8,128)}, f32[16,56,128]{2,1,0:T(8,128)S(1)}, f32[16,56,128]{2,1,0:T(8,128)S(1)}) custom-call(s32[1]{0:T(128)} %bitcast.core, bf16[2048,512]{1,0:T(8,128)(2,1)S(1)} %bitcast.36, bf16[32,2048]{1,0:T(8,128)(2,1)S(1)} %convert_element_type.27.template, f32[2,16,48,128]{3,2,1,0:T(8,128)S(1)} %bitcast.37, ...), custom_call_target="tpu_custom_call" | custom-call | tf_op jit(solution)/shard_map/update/pallas_call | solution.py:132
  248.8 0.5 collective-permute-start.5
  249.3 1.4 collective-permute-done.5
  250.8 12.6 %all_to_all.77 = f32[16,56,128]{2,1,0:T(8,128)S(1)} all-to-all(f32[16,56,128]{2,1,0:T(8,128)S(1)} %add.81), channel_id=1, replica_groups=mesh['z'=8,'y'=4,'core'=2,'row'=4] {'y','row'}, dimensions={0} | all-to-all | bytes 917504 | tf_op jit(solution)/shard_map/all_to_all | solution.py:62
  263.4 11.3 %all_to_all.78 = f32[8,56,128]{2,1,0:T(8,128)S(1)} all-to-all(f32[8,56,128]{2,1,0:T(8,128)S(1)} %broadcast_in_dim.95), channel_id=1, replica_groups=mesh['z'=8,'y'=4,'core'=2,'row'=4] {'z'}, dimensions={0} | all-to-all | bytes 458752 | tf_op jit(solution)/shard_map/all_to_all | solution.py:57
  274.7 0.1 fusion.15
  274.9 12.1 %all_to_all.79 = f32[16,48,128]{2,1,0:T(8,128)S(1)} all-to-all(f32[16,48,128]{2,1,0:T(8,128)S(1)} %broadcast_in_dim.96), channel_id=1, replica_groups=mesh['z'=8,'y'=4,'core'=2,'row'=4] {'y','row'}, dimensions={0} | all-to-all | bytes 786432 | tf_op jit(solution)/shard_map/all_to_all | solution.py:57
  286.9 6.1 %all-gather.3 = f32[32,48,128]{2,1,0:T(8,128)S(1)} all-gather(f32[16,48,128]{2,1,0:T(8,128)S(1)} %all_to_all.79), channel_id=5, replica_groups=mesh['z'=8,'y'=4,'core'=2,'row'=4] {'core'}, dimensions={0}, use_global_device_ids=true | all-gather | bytes 1179648 | tf_op jit(solution)/shard_map/all_gather | solution.py:159
  293.0 0.2 copy.16
  293.3 1.1 copy.21
  (28 shorter events, 0.6 us)
Async XLA Ops:
  5.7 5.6 %collective-permute-start = (bf16[1,3,32,512]{3,2,0,1:T(8,128)(2,1)S(1)}, bf16[1,3,32,512]{3,2,0,1:T(8,128)(2,1)S(1)}, u32[]{:S(2)}, u32[]{:S(2)}) collective-permute-start(bf16[1,3,32,512]{3,2,0,1:T(8,128)(2,1)S(1)} %get-tuple-element.28), channel_id=1, source_target_pairs={{0,1},{1,2},{2,3},{4,5},{5,6},{6,7},{8,9},{9,10},{10,11},{12,13},{... | collective-permute-start | bytes 294920 | tf_op jit(solution)/shard_map/ppermute | solution.py:30
  9.7 5.4 %collective-permute-start.1 = (bf16[1,3,32,512]{3,2,0,1:T(8,128)(2,1)S(1)}, bf16[1,3,32,512]{3,2,0,1:T(8,128)(2,1)S(1)}, u32[]{:S(2)}, u32[]{:S(2)}) collective-permute-start(bf16[1,3,32,512]{3,2,0,1:T(8,128)(2,1)S(1)} %get-tuple-element.29), channel_id=1, source_target_pairs={{1,0},{2,1},{3,2},{5,4},{6,5},{7,6},{9,8},{10,9},{11,10},{13,12},{... | collective-permute-start | bytes 294920 | tf_op jit(solution)/shard_map/ppermute | solution.py:31
  31.5 13.9 %copy-start.3 = (s32[32,2048]{1,0:T(8,128)S(1)}, s32[32,2048]{1,0:T(8,128)}, u32[]{:S(2)}) copy-start(s32[32,2048]{1,0:T(8,128)} %param.5) | copy-start | bytes 786436
  31.5 13.9 %copy-start.2 = (f32[96,2048]{1,0:T(8,128)S(1)}, f32[96,2048]{1,0:T(8,128)}, u32[]{:S(2)}) copy-start(f32[96,2048]{1,0:T(8,128)} %param.7) | copy-start | bytes 2359300
  31.5 63.6 %copy-start = (f32[1,1,128,512]{3,2,1,0:T(8,128)S(1)}, f32[1,1,128,512]{3,2,1,0:T(8,128)}, u32[]{:S(2)}) copy-start(f32[1,1,128,512]{3,2,1,0:T(8,128)} %param.6) | copy-start | bytes 786436
  31.5 63.6 %all-to-all-start = ((bf16[1,64,32,512]{3,2,0,1:T(8,128)(2,1)}), bf16[1,64,32,512]{3,2,0,1:T(8,128)(2,1)S(1)}, u32[]{:S(2)}, u32[]{:S(2)}) async-start(bf16[1,64,32,512]{3,2,0,1:T(8,128)(2,1)} %fusion.14), calls=%async_computation | async-start | bytes 4194304 | tf_op jit(solution)/shard_map/all_to_all | solution.py:147
  45.6 0.9 copy-start.1
  98.7 3.7 %collective-permute-start.2 = (f32[16,56,128]{2,1,0:T(8,128)S(1)}, f32[16,56,128]{2,1,0:T(8,128)S(1)}, u32[]{:S(2)}, u32[]{:S(2)}) collective-permute-start(f32[16,56,128]{2,1,0:T(8,128)S(1)} %get-tuple-element.15), channel_id=1, source_target_pairs={{0,4},{4,0},{1,5},{5,1},{2,6},{6,2},{3,7},{7,3},{8,12},{12,8},{9,1... | collective-permute-start | bytes 1376264 | tf_op jit(solution)/shard_map/ppermute | solution.py:61
  119.1 12.2 %all-to-all-start.2 = ((f32[8,56,128]{2,1,0:T(8,128)}), f32[8,56,128]{2,1,0:T(8,128)S(1)}, u32[]{:S(2)}, u32[]{:S(2)}) async-start(f32[8,56,128]{2,1,0:T(8,128)} %broadcast_in_dim.49), calls=%async_computation.2 | async-start | bytes 458752 | tf_op jit(solution)/shard_map/all_to_all | solution.py:57
  153.3 1.9 collective-permute-start.3
  201.1 1.9 collective-permute-start.4
  248.8 1.9 collective-permute-start.5

commit v3 on v2

v3 whole, which is shorter than its diff:
```python
import jax
import jax.numpy as jnp
import numpy as np
from jax import lax
from jax.experimental import pallas as pl
from jax.experimental.pallas import tpu as pltpu
from jax.sharding import PartitionSpec as P

FIXED = 32
FREE = 96
PASSES = 3
ITERS = 4
CHAN = ("z", "y", "core")
PLANE = ("y", "row")
CORES = 2
HALF = FREE // CORES
LANES = 128
DEN_ROWS = 8
CHUNK = 256
ROWS = 8
TAU = 8.0 / 3.0
SCALE = 0.15**3
VMEM = pl.BlockSpec(memory_space=pltpu.VMEM)
SMEM = pl.BlockSpec(memory_space=pltpu.SMEM)
ANY = pl.BlockSpec(memory_space=pl.ANY)


def column_sums(width):
    beside = np.eye(width, k=1) + np.eye(width, k=-1)
    powers = [3 * beside, 3 * beside @ beside, beside @ beside @ beside]
    return jnp.asarray(np.concatenate(powers, axis=1), jnp.bfloat16)


def beside_of(rows, sums):
    width = rows.shape[-1]
    flat = rows.reshape(-1, width).astype(jnp.bfloat16)
    out = jnp.dot(flat, sums, preferred_element_type=jnp.float32)
    return [out[:, at * width : (at + 1) * width].reshape(rows.shape) for at in range(PASSES)]


def inner_kernel(counts, sums, out, held, plain, beside, once, twice, done, in_sem, out_sem):
    lines = counts.shape[0]
    turns = lines // ROWS

    def fetch(turn):
        rows = pl.ds(turn * ROWS, ROWS)
        return pltpu.make_async_copy(counts.at[rows], held.at[rows], in_sem.at[turn])

    def ship(turn):
        start = turn * ROWS - PASSES
        return pltpu.make_async_copy(
            done.at[pl.ds(start + ROWS, ROWS)], out.at[pl.ds(start, ROWS)], out_sem.at[turn]
        )

    for turn in range(turns):
        fetch(turn).start()

    for turn in range(turns):
        fetch(turn).wait()
        base = turn * ROWS
        x = held[pl.ds(base, ROWS)].astype(jnp.float32)
        plain[pl.ds(base + ROWS, ROWS)] = x
        for at, value in enumerate(beside_of(x, sums[...])):
            beside[at, pl.ds(base + ROWS, ROWS)] = value
        for step, (source, target) in enumerate(((plain, once), (once, twice), (twice, done))):
            for row in range(ROWS):
                at = base + ROWS + row - step - 1
                value = TAU * source[at] + (source[at - 1] + source[at + 1]) + beside[step, at]
                if step == PASSES - 1:
                    value = (SCALE * value).astype(jnp.bfloat16)
                target[at] = value

        if turn:
            ship(turn).start()

    short = pltpu.make_async_copy(
        done.at[pl.ds(ROWS + PASSES, ROWS - 2 * PASSES)], out.at[pl.ds(PASSES, ROWS - 2 * PASSES)], out_sem.at[0]
    )
    short.start()
    short.wait()
    for turn in range(1, turns):
        ship(turn).wait()


def edge_kernel(flags, sums, counts_first, counts_last, before, after, inner, out, ends, sem):
    del inner
    lines = out.shape[0]
    copies = []
    for top in (True, False):
        near, rim = (counts_first, before) if top else (counts_last, after)
        pair = (rim[...], near[...]) if top else (near[...], rim[...])
        field = jnp.concatenate(pair, axis=0).astype(jnp.float32)
        beside = beside_of(field, sums[...])
        rows = [field[row] for row in range(3 * PASSES)]
        flag = flags[0] if top else flags[1]
        for step in range(PASSES):
            rows = [
                TAU * rows[row + 1] + (rows[row] + rows[row + 2]) + beside[step][row + 1 + step]
                for row in range(len(rows) - 2)
            ]
            beyond = PASSES - 1 - step
            for row in range(beyond):
                spot = row if top else len(rows) - 1 - row
                rows[spot] = rows[spot] * flag
        side = 0 if top else 1
        for row in range(PASSES):
            ends[side, row] = (SCALE * rows[row]).astype(jnp.bfloat16)
        target = out.at[pl.ds(0 if top else lines - PASSES, PASSES)]
        copies.append(pltpu.make_async_copy(ends.at[side], target, sem.at[side]))
        copies[-1].start()
    for copy in copies:
        copy.wait()


def smoothed(counts):
    lines, channels, width = counts.shape
    size, row = lax.axis_size("row"), lax.axis_index("row")
    up = [(i, i + 1) for i in range(size - 1)]
    down = [(j, i) for i, j in up]
    first, last = lax.optimization_barrier((counts[: 2 * PASSES], counts[-2 * PASSES :]))
    first, last = first.astype(jnp.bfloat16), last.astype(jnp.bfloat16)
    before = lax.ppermute(last[PASSES:], "row", up)
    after = lax.ppermute(first[:PASSES], "row", down)
    flags = jnp.stack([row > 0, row < size - 1]).astype(jnp.float32)
    shape = jax.ShapeDtypeStruct(counts.shape, jnp.bfloat16)
    sums = column_sums(width)
    padded = (lines + 2 * ROWS, channels, width)
    inner = pl.pallas_call(
        inner_kernel,
        out_shape=shape,
        in_specs=[ANY, VMEM],
        out_specs=ANY,
        scratch_shapes=[
            pltpu.VMEM(counts.shape, jnp.int32),
            pltpu.VMEM(padded, jnp.float32),
            pltpu.VMEM((PASSES,) + padded, jnp.float32),
            pltpu.VMEM(padded, jnp.float32),
            pltpu.VMEM(padded, jnp.float32),
            pltpu.VMEM(padded, jnp.bfloat16),
            pltpu.SemaphoreType.DMA((lines // ROWS,)),
            pltpu.SemaphoreType.DMA((lines // ROWS,)),
        ],
        compiler_params=pltpu.CompilerParams(vmem_limit_bytes=44 * 1024 * 1024),
        cost_estimate=pl.CostEstimate(
            flops=2 * lines * channels * width * width, bytes_accessed=6 * lines * channels * width, transcendentals=0
        ),
        name="smooth_inner",
    )(counts, sums)
    return pl.pallas_call(
        edge_kernel,
        out_shape=shape,
        in_specs=[SMEM, VMEM, VMEM, VMEM, VMEM, VMEM, ANY],
        out_specs=ANY,
        scratch_shapes=[
            pltpu.VMEM((2, PASSES, channels, width), jnp.bfloat16),
            pltpu.SemaphoreType.DMA((2,)),
        ],
        input_output_aliases={6: 0},
        compiler_params=pltpu.CompilerParams(vmem_limit_bytes=12 * 1024 * 1024),
        name="smooth_edges",
    )(flags, sums, first, last, before, after, inner)


def to_all(x, axes):
    count = 1
    for axis in axes:
        count *= lax.axis_size(axis)
    return lax.all_to_all(jnp.broadcast_to(x[None], (count,) + x.shape), axes, 0, 0, tiled=True)


def summed_block(kept, sent):
    chip = kept + lax.ppermute(sent, "core", [(0, 1), (1, 0)])
    plane = jnp.sum(lax.all_to_all(chip, PLANE, 0, 0, tiled=True), axis=0)
    total = jnp.sum(to_all(plane, ("z",)), axis=0)
    return total[:HALF], total[HALF, :HALF]


def update_kernel(core, data, template, own, other, weights, new_weights, kept, sent, low, low_t):
    channels, pixels = data.shape
    shards = channels // LANES
    mine = core[0]
    first = mine == 0
    den = []
    low[:FIXED] = template[...]
    for half, blocks in ((mine, own), (1 - mine, other)):
        rows = pl.ds(pl.multiple_of(FIXED + half * HALF, 16), HALF)
        total = jnp.zeros((HALF, LANES), jnp.float32)
        for shard in range(shards):
            part = blocks[shard]
            total = total + part
            low[rows, pl.ds(shard * LANES, LANES)] = part.astype(jnp.bfloat16)
        den.append(jnp.sum(total, axis=1, keepdims=True))
    upper, lower = jnp.where(first, den[0], den[1]), jnp.where(first, den[1], den[0])
    fixed = jnp.sum(template[...].astype(jnp.float32), axis=1, keepdims=True)
    weight_den = jnp.concatenate([fixed, upper, lower], axis=0)
    for shard in range(shards):
        low_t[pl.ds(shard * LANES, LANES), :] = low[:, pl.ds(shard * LANES, LANES)].T

    old = weights[...]
    old_low = old.astype(jnp.bfloat16)

    def ratios_of(chunk, held):
        part = pl.ds(chunk * CHUNK, CHUNK)
        intensity = jnp.dot(low_t[part, :], held, preferred_element_type=jnp.float32)
        return (data[part, :].astype(jnp.float32) / intensity).astype(jnp.bfloat16)

    numerator = jnp.zeros(old.shape, jnp.float32)
    for chunk in range(channels // CHUNK):
        ratios = ratios_of(chunk, old_low)
        numerator += jnp.dot(
            low[:, pl.ds(chunk * CHUNK, CHUNK)], ratios, preferred_element_type=jnp.float32
        )
    new = old * numerator / weight_den
    new_weights[...] = new
    new_low = new.astype(jnp.bfloat16)
    sums = jnp.sum(new[FIXED:], axis=1, keepdims=True)
    at = lax.broadcasted_iota(jnp.int32, (HALF, LANES), 0)
    lane = lax.broadcasted_iota(jnp.int32, (HALF, LANES), 1)
    den_rows = []
    for half in range(CORES):
        column = jnp.broadcast_to(sums[half * HALF : (half + 1) * HALF], (HALF, LANES))
        row = jnp.sum(jnp.where(at == lane, column, 0.0), axis=0, keepdims=True)
        den_rows.append(jnp.broadcast_to(row, (DEN_ROWS, LANES)))
    kept_row = jnp.where(first, den_rows[0], den_rows[1])
    sent_row = jnp.where(first, den_rows[1], den_rows[0])
    for chunk in range(channels // CHUNK):
        ratios = ratios_of(chunk, new_low)
        terms = lax.dot_general(
            new_low[FIXED:], ratios, (((1,), (1,)), ((), ())), preferred_element_type=jnp.float32
        )
        for part in range(CHUNK // LANES):
            shard = chunk * (CHUNK // LANES) + part
            upper = terms[:HALF, part * LANES : (part + 1) * LANES]
            lower = terms[HALF:, part * LANES : (part + 1) * LANES]
            kept[shard, :HALF] = jnp.where(first, upper, lower)
            sent[shard, :HALF] = jnp.where(first, lower, upper)
            kept[shard, HALF:] = kept_row
            sent[shard, HALF:] = sent_row


def update(core, data, template, own, other, weights):
    channels = data.shape[0]
    message = jax.ShapeDtypeStruct((channels // LANES, HALF + DEN_ROWS, LANES), jnp.float32)
    components = template.shape[0] + FREE
    return pl.pallas_call(
        update_kernel,
        out_shape=(jax.ShapeDtypeStruct(weights.shape, jnp.float32), message, message),
        in_specs=[SMEM, VMEM, VMEM, VMEM, VMEM, VMEM],
        out_specs=(VMEM, VMEM, VMEM),
        scratch_shapes=[
            pltpu.VMEM((components, channels), jnp.bfloat16),
            pltpu.VMEM((channels, components), jnp.bfloat16),
        ],
        compiler_params=pltpu.CompilerParams(vmem_limit_bytes=16 * 1024 * 1024),
        name="update",
    )(core, data, template, own, other, weights)


def whole_kernel(core, own, other, out):
    for half, blocks in ((core[0], own), (1 - core[0], other)):
        rows = pl.ds(pl.multiple_of(half * HALF, 8), HALF)
        for shard in range(blocks.shape[0]):
            out[rows, pl.ds(shard * LANES, LANES)] = blocks[shard]


def whole(core, own, other):
    return pl.pallas_call(
        whole_kernel,
        out_shape=jax.ShapeDtypeStruct((FREE, own.shape[0] * LANES), jnp.float32),
        in_specs=[SMEM, VMEM, VMEM],
        out_specs=VMEM,
        name="whole",
    )(core, own, other)


def shards(counts, template_mask, weights_init, spectra_init):
    pixel_data = lax.all_to_all(smoothed(counts[0]), CHAN, split_axis=0, concat_axis=0, tiled=True)
    data = pixel_data.reshape(-1, pixel_data.shape[-1])
    core = lax.axis_index("core")
    template = template_mask.astype(jnp.bfloat16)
    weights = weights_init[0, 0]
    shard = lax.axis_index("y") * lax.axis_size("row") + lax.axis_index("row")
    halves = spectra_init.reshape(CORES, HALF, -1, LANES).transpose(0, 2, 1, 3)
    own, other = halves[core], halves[1 - core]
    block = own[shard]
    for iteration in range(ITERS):
        weights, kept, sent = update(core[None], data, template, own, other, weights)
        num, den = summed_block(kept, sent)
        block = block * num / den[:, None]
        own = to_all(block, PLANE)
        other = lax.ppermute(own, "core", [(0, 1), (1, 0)])
    return (weights[None, None], whole(core[None], own, other))


def solution(mesh):
    devices = np.asarray(mesh.devices)
    fine = jax.sharding.Mesh(devices.reshape(8, 4, 2, 4), ("z", "y", "core", "row"))
    placed = (P("row", None, CHAN, None), P(), P("row", CHAN, None, None), P())
    return jax.shard_map(
        shards,
        mesh=fine,
        in_specs=placed,
        out_specs=(P("row", CHAN, None, None), P()),
        check_vma=False,
    )
```

time: 295 us -> 283 us (0.959)
  blocking collectives: 160 us -> 137 us
  other arithmetic: 19.8 us -> 0.87 us
  starting transfers between devices: 26.1 us -> 41.5 us
  Pallas kernels: 14.4 us -> 24.6 us
  local copies, waits for them, and re-layouts: 6.93 us -> 11.1 us
    all_gather x4 -> x0, blocking collectives: 24.4 us -> none  [shards(): halves = lax.all_gather(to_all(block, PLANE), 'core')]
    ppermute x2 -> x6, starting transfers between devices: 5.24 us -> 21.7 us  [the longest x4 16.5 us: shards(): other = lax.ppermute(own, 'core', [(0, 1), (1, 0)])]
    pallas_call x0 -> x3, Pallas kernels: none -> 10.3 us  [the longest x1 6.1 us: smoothed(): pl.pallas_call(inner_kernel, out_shape=shape, in_specs=[ANY, VMEM], out_s...]
    convert_element_type x4 -> x3, other arithmetic: 9.33 us -> 0.14 us  [the longest x1 0.08 us: smoothed(): flags = jnp.stack([row > 0, row < size - 1]).astype(jnp.float32)]
    select_n x2 -> x0, other arithmetic: 6.67 us -> none  [smoothed(): field = jnp.where(inside[None, :, None, None], field, 0.0)]
    unnamed x10 -> x17, local copies, waits for them, and re-layouts: 2.15 us -> 7.82 us
    concatenate x1 -> x0, other arithmetic: 3.05 us -> none  [with_rims(): return jnp.concatenate(parts, axis=1)]
  transfers between devices with their start and end apart: 8 -> 12, of which waited for: 8 -> 10; matrix products, arithmetic and copies ran while one was open for 0% -> 1% of each run, Pallas kernels for 0% -> 2%
where the time goes in v3:
time: 283 us
  blocking collectives  137 us (48%)
  waiting for transfers between devices  66.2 us (23%)
  starting transfers between devices  41.5 us (15%)
  Pallas kernels  24.6 us (9%)
  local copies, waits for them, and re-layouts  11.1 us (4%)
    all_to_all x7, blocking collectives, to_all(): lax.all_to_all(jnp.broadcast_to(x[None], (count,) + x.shape), axes, 0, 0,...  82.2 us
    all_to_all x4, blocking collectives, summed_block(): plane = jnp.sum(lax.all_to_all(chip, PLANE, 0, 0, tiled=True), axis=0)  55.1 us
    all_to_all x1, waiting for transfers between devices, shards(): lax.all_to_all(smoothed(counts[0]), CHAN, split_axis=0, concat_axis=0, ti...  47.2 us
    ppermute x4, starting transfers between devices, shards(): other = lax.ppermute(own, 'core', [(0, 1), (1, 0)])  16.5 us
    pallas_call x4, Pallas kernels, update(): pl.pallas_call(update_kernel, out_shape=(jax.ShapeDtypeStruct(weights.sha...  14.3 us
    all_to_all x1, starting transfers between devices, shards(): lax.all_to_all(smoothed(counts[0]), CHAN, split_axis=0, concat_axis=0, ti...  12.7 us
    all_to_all x1, waiting for transfers between devices, to_all(): lax.all_to_all(jnp.broadcast_to(x[None], (count,) + x.shape), axes, 0, 0,...  7.82 us
    unnamed x17, local copies, waits for them, and re-layouts  7.82 us
  transfers between devices with their start and end apart: 12, of which 10 were waited for; matrix products, arithmetic and copies ran while one was open for 1% of the time, Pallas kernels for 2%

profile of v3, /device:TPU:1, one launch (start us, length us, event | category | flops | bytes accessed | tf_op | source)
XLA Modules:
  0.0 282.6 jit_solution(9932111926953078701)
XLA Ops:
  0.6 1.2 slice_bitcast_fusion
  1.9 4.0 %collective-permute-start = (bf16[3,32,512]{2,1,0:T(8,128)(2,1)S(1)}, bf16[3,32,512]{2,1,0:T(8,128)(2,1)S(1)}, u32[]{:S(2)}, u32[]{:S(2)}) collective-permute-start(bf16[3,32,512]{2,1,0:T(8,128)(2,1)S(1)} %slice.56), channel_id=1, source_target_pairs={{0,1},{1,2},{2,3},{4,5},{5,6},{6,7},{8,9},{9,10},{10,11},{12,13},{... | collective-permute-start | bytes 294920 | tf_op jit(solution)/shard_map/ppermute | solution.py:122
  5.9 1.3 collective-permute-start.1
  7.2 0.1 add_convert_fusion.flags
  7.3 1.4 copy-done.1
  8.7 2.2 copy-done.2
  10.8 6.1 %smooth_inner.1.inner = bf16[64,32,512]{2,1,0:T(8,128)(2,1)S(1)} custom-call(s32[64,32,512]{2,1,0:T(8,128)S(1)} %bitcast.35, bf16[512,1536]{1,0:T(8,128)(2,1)S(1)} %copy-done.1), custom_call_target="tpu_custom_call" | custom-call | flops 1073741824 | bytes 6291456 | tf_op jit(solution)/shard_map/smooth_inner/pallas_call | solution.py:128
  17.0 0.0 collective-permute-done.before
  17.0 0.0 collective-permute-done.1.after
  17.0 2.1 smooth_edges.1
  19.1 0.0 copy-start
  19.1 1.3 copy-done
  20.5 12.7 %all-to-all-start = ((bf16[64,32,512]{2,1,0:T(8,128)(2,1)}), bf16[64,32,512]{2,1,0:T(8,128)(2,1)S(1)}, u32[]{:S(2)}, u32[]{:S(2)}) async-start(bf16[64,32,512]{2,1,0:T(8,128)(2,1)} %copy-done), calls=%async_computation | async-start | bytes 4194304 | tf_op jit(solution)/shard_map/all_to_all | solution.py:277
  33.3 0.0 copy-start.3
  33.3 1.3 copy.14
  34.6 0.0 copy-start.4
  34.6 0.1 constant_dynamic-slice_fusion
  34.7 0.8 copy-done.4
  35.5 0.2 copy_bitcast_fusion
  35.7 47.2 %all-to-all-done = bf16[64,32,512]{2,1,0:T(8,128)(2,1)S(1)} async-done(((bf16[64,32,512]{2,1,0:T(8,128)(2,1)}), bf16[64,32,512]{2,1,0:T(8,128)(2,1)S(1)}, u32[]{:S(2)}, u32[]{:S(2)}) %all-to-all-start) | async-done | bytes 2097184 | tf_op jit(solution)/shard_map/all_to_all | solution.py:277
  82.9 3.6 %update.4 = (f32[128,512]{1,0:T(8,128)S(1)}, f32[16,56,128]{2,1,0:T(8,128)S(1)}, f32[16,56,128]{2,1,0:T(8,128)S(1)}) custom-call(s32[1]{0:T(128)} %bitcast.core, bf16[2048,512]{1,0:T(8,128)(2,1)S(1)} %bitcast.31, bf16[32,2048]{1,0:T(8,128)(2,1)S(1)} %convert_element_type.15.template, f32[16,48,128]{2,1,0:T(8,128)S(1)} %get-tuple-element.35.own, ...), custom_call_target="tpu_custom_call" | custom-call | tf_op jit(solution)/shard_map/update/pallas_call | solution.py:245
  86.5 2.2 collective-permute-start.2
  88.7 1.4 collective-permute-done.2
  90.2 0.1 add.33
  90.2 17.4 %all_to_all.65 = f32[16,56,128]{2,1,0:T(8,128)S(1)} all-to-all(f32[16,56,128]{2,1,0:T(8,128)S(1)} %add.33), channel_id=1, replica_groups=mesh['z'=8,'y'=4,'core'=2,'row'=4] {'y','row'}, dimensions={0} | all-to-all | bytes 917504 | tf_op jit(solution)/shard_map/all_to_all | solution.py:173
  107.7 0.7 broadcast_in_dim.21
  108.4 3.4 %all-to-all-start.2 = ((f32[8,56,128]{2,1,0:T(8,128)}), f32[8,56,128]{2,1,0:T(8,128)S(1)}, u32[]{:S(2)}, u32[]{:S(2)}) async-start(f32[8,56,128]{2,1,0:T(8,128)} %broadcast_in_dim.21), calls=%async_computation.2 | async-start | bytes 458752 | tf_op jit(solution)/shard_map/all_to_all | solution.py:168
  111.8 1.0 constant_dynamic-slice_fusion.2
  112.8 7.8 %all-to-all-done.2 = f32[8,56,128]{2,1,0:T(8,128)S(1)} async-done(((f32[8,56,128]{2,1,0:T(8,128)}), f32[8,56,128]{2,1,0:T(8,128)S(1)}, u32[]{:S(2)}, u32[]{:S(2)}) %all-to-all-start.2) | async-done | bytes 229408 | tf_op jit(solution)/shard_map/all_to_all | solution.py:168
  120.6 0.1 fusion.3
  120.7 12.1 %all_to_all.66.own = f32[16,48,128]{2,1,0:T(8,128)S(1)} all-to-all(f32[16,48,128]{2,1,0:T(8,128)S(1)} %broadcast_in_dim.22), channel_id=1, replica_groups=mesh['z'=8,'y'=4,'core'=2,'row'=4] {'y','row'}, dimensions={0} | all-to-all | bytes 786432 | tf_op jit(solution)/shard_map/all_to_all | solution.py:168
  132.8 4.1 %collective-permute-start.3 = (f32[16,48,128]{2,1,0:T(8,128)S(1)}, f32[16,48,128]{2,1,0:T(8,128)S(1)}, u32[]{:S(2)}, u32[]{:S(2)}) collective-permute-start(f32[16,48,128]{2,1,0:T(8,128)S(1)} %all_to_all.66.own), channel_id=1, source_target_pairs={{0,4},{4,0},{1,5},{5,1},{2,6},{6,2},{3,7},{7,3},{8,12},{12,8},{9,1... | collective-permute-start | bytes 1179656 | tf_op jit(solution)/shard_map/ppermute | solution.py:291
  136.9 1.3 collective-permute-done.3.other
  138.3 3.6 %update.5 = (f32[128,512]{1,0:T(8,128)S(1)}, f32[16,56,128]{2,1,0:T(8,128)S(1)}, f32[16,56,128]{2,1,0:T(8,128)S(1)}) custom-call(s32[1]{0:T(128)} %bitcast.core, bf16[2048,512]{1,0:T(8,128)(2,1)S(1)} %bitcast.32, bf16[32,2048]{1,0:T(8,128)(2,1)S(1)} %convert_element_type.15.template, f32[16,48,128]{2,1,0:T(8,128)S(1)} %all_to_all.66.own, ...), custom_call_target="tpu_custom_call" | custom-call | tf_op jit(solution)/shard_map/update/pallas_call | solution.py:245
  141.9 0.5 collective-permute-start.4
  142.4 1.4 collective-permute-done.4
  143.8 0.1 add.34
  143.9 12.5 %all_to_all.67 = f32[16,56,128]{2,1,0:T(8,128)S(1)} all-to-all(f32[16,56,128]{2,1,0:T(8,128)S(1)} %add.34), channel_id=1, replica_groups=mesh['z'=8,'y'=4,'core'=2,'row'=4] {'y','row'}, dimensions={0} | all-to-all | bytes 917504 | tf_op jit(solution)/shard_map/all_to_all | solution.py:173
  156.5 11.3 %all_to_all.68 = f32[8,56,128]{2,1,0:T(8,128)S(1)} all-to-all(f32[8,56,128]{2,1,0:T(8,128)S(1)} %broadcast_in_dim.23), channel_id=1, replica_groups=mesh['z'=8,'y'=4,'core'=2,'row'=4] {'z'}, dimensions={0} | all-to-all | bytes 458752 | tf_op jit(solution)/shard_map/all_to_all | solution.py:168
  167.8 0.1 fusion.2
  167.9 12.1 %all_to_all.69.own = f32[16,48,128]{2,1,0:T(8,128)S(1)} all-to-all(f32[16,48,128]{2,1,0:T(8,128)S(1)} %broadcast_in_dim.24), channel_id=1, replica_groups=mesh['z'=8,'y'=4,'core'=2,'row'=4] {'y','row'}, dimensions={0} | all-to-all | bytes 786432 | tf_op jit(solution)/shard_map/all_to_all | solution.py:168
  180.0 4.1 %collective-permute-start.5 = (f32[16,48,128]{2,1,0:T(8,128)S(1)}, f32[16,48,128]{2,1,0:T(8,128)S(1)}, u32[]{:S(2)}, u32[]{:S(2)}) collective-permute-start(f32[16,48,128]{2,1,0:T(8,128)S(1)} %all_to_all.69.own), channel_id=1, source_target_pairs={{0,4},{4,0},{1,5},{5,1},{2,6},{6,2},{3,7},{7,3},{8,12},{12,8},{9,1... | collective-permute-start | bytes 1179656 | tf_op jit(solution)/shard_map/ppermute | solution.py:291
  184.1 1.3 collective-permute-done.5.other
  185.4 3.6 %update.6 = (f32[128,512]{1,0:T(8,128)S(1)}, f32[16,56,128]{2,1,0:T(8,128)S(1)}, f32[16,56,128]{2,1,0:T(8,128)S(1)}) custom-call(s32[1]{0:T(128)} %bitcast.core, bf16[2048,512]{1,0:T(8,128)(2,1)S(1)} %bitcast.33, bf16[32,2048]{1,0:T(8,128)(2,1)S(1)} %convert_element_type.15.template, f32[16,48,128]{2,1,0:T(8,128)S(1)} %all_to_all.69.own, ...), custom_call_target="tpu_custom_call" | custom-call | tf_op jit(solution)/shard_map/update/pallas_call | solution.py:245
  189.0 0.5 collective-permute-start.6
  189.5 1.4 collective-permute-done.6
  191.0 0.1 add.35
  191.0 12.5 %all_to_all.70 = f32[16,56,128]{2,1,0:T(8,128)S(1)} all-to-all(f32[16,56,128]{2,1,0:T(8,128)S(1)} %add.35), channel_id=1, replica_groups=mesh['z'=8,'y'=4,'core'=2,'row'=4] {'y','row'}, dimensions={0} | all-to-all | bytes 917504 | tf_op jit(solution)/shard_map/all_to_all | solution.py:173
  203.6 11.3 %all_to_all.71 = f32[8,56,128]{2,1,0:T(8,128)S(1)} all-to-all(f32[8,56,128]{2,1,0:T(8,128)S(1)} %broadcast_in_dim.25), channel_id=1, replica_groups=mesh['z'=8,'y'=4,'core'=2,'row'=4] {'z'}, dimensions={0} | all-to-all | bytes 458752 | tf_op jit(solution)/shard_map/all_to_all | solution.py:168
  214.9 0.1 fusion.1
  215.1 12.1 %all_to_all.72.own = f32[16,48,128]{2,1,0:T(8,128)S(1)} all-to-all(f32[16,48,128]{2,1,0:T(8,128)S(1)} %broadcast_in_dim.26), channel_id=1, replica_groups=mesh['z'=8,'y'=4,'core'=2,'row'=4] {'y','row'}, dimensions={0} | all-to-all | bytes 786432 | tf_op jit(solution)/shard_map/all_to_all | solution.py:168
  227.1 4.1 %collective-permute-start.7 = (f32[16,48,128]{2,1,0:T(8,128)S(1)}, f32[16,48,128]{2,1,0:T(8,128)S(1)}, u32[]{:S(2)}, u32[]{:S(2)}) collective-permute-start(f32[16,48,128]{2,1,0:T(8,128)S(1)} %all_to_all.72.own), channel_id=1, source_target_pairs={{0,4},{4,0},{1,5},{5,1},{2,6},{6,2},{3,7},{7,3},{8,12},{12,8},{9,1... | collective-permute-start | bytes 1179656 | tf_op jit(solution)/shard_map/ppermute | solution.py:291
  231.2 1.3 collective-permute-done.7.other
  232.6 3.6 %update.7 = (f32[128,512]{1,0:T(8,128)}, f32[16,56,128]{2,1,0:T(8,128)S(1)}, f32[16,56,128]{2,1,0:T(8,128)S(1)}) custom-call(s32[1]{0:T(128)} %bitcast.core, bf16[2048,512]{1,0:T(8,128)(2,1)S(1)} %bitcast.34, bf16[32,2048]{1,0:T(8,128)(2,1)S(1)} %convert_element_type.15.template, f32[16,48,128]{2,1,0:T(8,128)S(1)} %all_to_all.72.own, ...), custom_call_target="tpu_custom_call" | custom-call | tf_op jit(solution)/shard_map/update/pallas_call | solution.py:245
  236.2 0.5 collective-permute-start.8
  236.7 1.4 collective-permute-done.8
  238.2 12.5 %all_to_all.73 = f32[16,56,128]{2,1,0:T(8,128)S(1)} all-to-all(f32[16,56,128]{2,1,0:T(8,128)S(1)} %add.36), channel_id=1, replica_groups=mesh['z'=8,'y'=4,'core'=2,'row'=4] {'y','row'}, dimensions={0} | all-to-all | bytes 917504 | tf_op jit(solution)/shard_map/all_to_all | solution.py:173
  250.8 11.3 %all_to_all.74 = f32[8,56,128]{2,1,0:T(8,128)S(1)} all-to-all(f32[8,56,128]{2,1,0:T(8,128)S(1)} %broadcast_in_dim.28), channel_id=1, replica_groups=mesh['z'=8,'y'=4,'core'=2,'row'=4] {'z'}, dimensions={0} | all-to-all | bytes 458752 | tf_op jit(solution)/shard_map/all_to_all | solution.py:168
  262.1 0.1 fusion
  262.2 12.1 %all_to_all.75.own = f32[16,48,128]{2,1,0:T(8,128)S(1)} all-to-all(f32[16,48,128]{2,1,0:T(8,128)S(1)} %broadcast_in_dim.29), channel_id=1, replica_groups=mesh['z'=8,'y'=4,'core'=2,'row'=4] {'y','row'}, dimensions={0} | all-to-all | bytes 786432 | tf_op jit(solution)/shard_map/all_to_all | solution.py:168
  274.3 4.1 %collective-permute-start.9 = (f32[16,48,128]{2,1,0:T(8,128)S(1)}, f32[16,48,128]{2,1,0:T(8,128)S(1)}, u32[]{:S(2)}, u32[]{:S(2)}) collective-permute-start(f32[16,48,128]{2,1,0:T(8,128)S(1)} %all_to_all.75.own), channel_id=1, source_target_pairs={{0,4},{4,0},{1,5},{5,1},{2,6},{6,2},{3,7},{7,3},{8,12},{12,8},{9,1... | collective-permute-start | bytes 1179656 | tf_op jit(solution)/shard_map/ppermute | solution.py:291
  278.4 1.3 collective-permute-done.9.other
  279.8 0.8 copy-done.6
  280.5 2.0 whole.1
  (33 shorter events, 0.5 us)
Async XLA Ops:
  1.9 15.1 %collective-permute-start = (bf16[3,32,512]{2,1,0:T(8,128)(2,1)S(1)}, bf16[3,32,512]{2,1,0:T(8,128)(2,1)S(1)}, u32[]{:S(2)}, u32[]{:S(2)}) collective-permute-start(bf16[3,32,512]{2,1,0:T(8,128)(2,1)S(1)} %slice.56), channel_id=1, source_target_pairs={{0,1},{1,2},{2,3},{4,5},{5,6},{6,7},{8,9},{9,10},{10,11},{12,13},{... | collective-permute-start | bytes 294920 | tf_op jit(solution)/shard_map/ppermute | solution.py:122
  5.9 11.1 %collective-permute-start.1 = (bf16[3,32,512]{2,1,0:T(8,128)(2,1)S(1)}, bf16[3,32,512]{2,1,0:T(8,128)(2,1)S(1)}, u32[]{:S(2)}, u32[]{:S(2)}) collective-permute-start(bf16[3,32,512]{2,1,0:T(8,128)(2,1)S(1)} %slice.57), channel_id=1, source_target_pairs={{1,0},{2,1},{3,2},{5,4},{6,5},{7,6},{9,8},{10,9},{11,10},{13,12},{... | collective-permute-start | bytes 294920 | tf_op jit(solution)/shard_map/ppermute | solution.py:123
  7.3 1.4 copy-start.1
  8.7 2.2 copy-start.2
  19.1 1.3 copy-start
  20.5 12.8 %copy-start.7 = (s32[32,2048]{1,0:T(8,128)S(1)}, s32[32,2048]{1,0:T(8,128)}, u32[]{:S(2)}) copy-start(s32[32,2048]{1,0:T(8,128)} %param.6) | copy-start | bytes 786436
  20.5 62.4 %all-to-all-start = ((bf16[64,32,512]{2,1,0:T(8,128)(2,1)}), bf16[64,32,512]{2,1,0:T(8,128)(2,1)S(1)}, u32[]{:S(2)}, u32[]{:S(2)}) async-start(bf16[64,32,512]{2,1,0:T(8,128)(2,1)} %copy-done), calls=%async_computation | async-start | bytes 4194304 | tf_op jit(solution)/shard_map/all_to_all | solution.py:277
  33.3 49.6 %copy-start.3 = (f32[1,1,128,512]{3,2,1,0:T(8,128)S(1)}, f32[1,1,128,512]{3,2,1,0:T(8,128)}, u32[]{:S(2)}) copy-start(f32[1,1,128,512]{3,2,1,0:T(8,128)} %param.7) | copy-start | bytes 786436
  34.6 0.9 copy-start.4
  86.5 3.7 %collective-permute-start.2 = (f32[16,56,128]{2,1,0:T(8,128)S(1)}, f32[16,56,128]{2,1,0:T(8,128)S(1)}, u32[]{:S(2)}, u32[]{:S(2)}) collective-permute-start(f32[16,56,128]{2,1,0:T(8,128)S(1)} %get-tuple-element.19), channel_id=1, source_target_pairs={{0,4},{4,0},{1,5},{5,1},{2,6},{6,2},{3,7},{7,3},{8,12},{12,8},{9,1... | collective-permute-start | bytes 1376264 | tf_op jit(solution)/shard_map/ppermute | solution.py:172
  108.4 12.2 %all-to-all-start.2 = ((f32[8,56,128]{2,1,0:T(8,128)}), f32[8,56,128]{2,1,0:T(8,128)S(1)}, u32[]{:S(2)}, u32[]{:S(2)}) async-start(f32[8,56,128]{2,1,0:T(8,128)} %broadcast_in_dim.21), calls=%async_computation.2 | async-start | bytes 458752 | tf_op jit(solution)/shard_map/all_to_all | solution.py:168
  132.8 5.5 %collective-permute-start.3 = (f32[16,48,128]{2,1,0:T(8,128)S(1)}, f32[16,48,128]{2,1,0:T(8,128)S(1)}, u32[]{:S(2)}, u32[]{:S(2)}) collective-permute-start(f32[16,48,128]{2,1,0:T(8,128)S(1)} %all_to_all.66.own), channel_id=1, source_target_pairs={{0,4},{4,0},{1,5},{5,1},{2,6},{6,2},{3,7},{7,3},{8,12},{12,8},{9,1... | collective-permute-start | bytes 1179656 | tf_op jit(solution)/shard_map/ppermute | solution.py:291
  141.9 1.9 collective-permute-start.4
  180.0 5.5 %collective-permute-start.5 = (f32[16,48,128]{2,1,0:T(8,128)S(1)}, f32[16,48,128]{2,1,0:T(8,128)S(1)}, u32[]{:S(2)}, u32[]{:S(2)}) collective-permute-start(f32[16,48,128]{2,1,0:T(8,128)S(1)} %all_to_all.69.own), channel_id=1, source_target_pairs={{0,4},{4,0},{1,5},{5,1},{2,6},{6,2},{3,7},{7,3},{8,12},{12,8},{9,1... | collective-permute-start | bytes 1179656 | tf_op jit(solution)/shard_map/ppermute | solution.py:291
  189.0 1.9 collective-permute-start.6
  227.1 5.5 %collective-permute-start.7 = (f32[16,48,128]{2,1,0:T(8,128)S(1)}, f32[16,48,128]{2,1,0:T(8,128)S(1)}, u32[]{:S(2)}, u32[]{:S(2)}) collective-permute-start(f32[16,48,128]{2,1,0:T(8,128)S(1)} %all_to_all.72.own), channel_id=1, source_target_pairs={{0,4},{4,0},{1,5},{5,1},{2,6},{6,2},{3,7},{7,3},{8,12},{12,8},{9,1... | collective-permute-start | bytes 1179656 | tf_op jit(solution)/shard_map/ppermute | solution.py:291
  236.2 1.9 collective-permute-start.8
  274.3 5.5 %copy-start.5 = (f32[16,48,128]{2,1,0:T(8,128)}, f32[16,48,128]{2,1,0:T(8,128)S(1)}, u32[]{:S(2)}) copy-start(f32[16,48,128]{2,1,0:T(8,128)S(1)} %all_to_all.75.own) | copy-start | bytes 1179652
  274.3 5.5 %collective-permute-start.9 = (f32[16,48,128]{2,1,0:T(8,128)S(1)}, f32[16,48,128]{2,1,0:T(8,128)S(1)}, u32[]{:S(2)}, u32[]{:S(2)}) collective-permute-start(f32[16,48,128]{2,1,0:T(8,128)S(1)} %all_to_all.75.own), channel_id=1, source_target_pairs={{0,4},{4,0},{1,5},{5,1},{2,6},{6,2},{3,7},{7,3},{8,12},{12,8},{9,1... | collective-permute-start | bytes 1179656 | tf_op jit(solution)/shard_map/ppermute | solution.py:291
  279.8 0.8 copy-start.6

commit v4 on v3

--- a/solution.py
+++ b/solution.py
@@ -18,17 +18,31 @@
 DEN_ROWS = 8
 CHUNK = 256
 ROWS = 8
+INNER_MIB = 60
+EDGE_MIB = 53
 TAU = 8.0 / 3.0
 SCALE = 0.15**3
 VMEM = pl.BlockSpec(memory_space=pltpu.VMEM)
 SMEM = pl.BlockSpec(memory_space=pltpu.SMEM)
-ANY = pl.BlockSpec(memory_space=pl.ANY)
+HBM = pl.BlockSpec(memory_space=pltpu.HBM)
 
 
 def column_sums(width):
-    beside = np.eye(width, k=1) + np.eye(width, k=-1)
-    powers = [3 * beside, 3 * beside @ beside, beside @ beside @ beside]
-    return jnp.asarray(np.concatenate(powers, axis=1), jnp.bfloat16)
+    row = lax.broadcasted_iota(jnp.int32, (width, width), 0)
+    column = lax.broadcasted_iota(jnp.int32, (width, width), 1)
+    apart, total = jnp.abs(row - column), row + column
+    corner = (total == 0) | (total == 2 * width - 2)
+    beside_corner = (total == 1) | (total == 2 * width - 3)
+    first = jnp.where(apart == 1, 3.0, 0.0)
+    second = jnp.where(apart == 2, 3.0, jnp.where(apart == 0, jnp.where(corner, 3.0, 6.0), 0.0))
+    third = jnp.where(apart == 3, 1.0, jnp.where(apart == 1, jnp.where(beside_corner, 2.0, 3.0), 0.0))
+    return [power.astype(jnp.bfloat16) for power in (first, second, third)]
+
+
+def fill_sums(sums):
+    width = sums.shape[0]
+    for at, power in enumerate(column_sums(width)):
+        sums[:, pl.ds(at * width, width)] = power
 
 
 def beside_of(rows, sums):
@@ -38,7 +52,7 @@
     return [out[:, at * width : (at + 1) * width].reshape(rows.shape) for at in range(PASSES)]
 
 
-def inner_kernel(counts, sums, out, held, plain, beside, once, twice, done, in_sem, out_sem):
+def inner_kernel(counts, out, sums, held, plain, beside, once, twice, done, in_sem, out_sem):
     lines = counts.shape[0]
     turns = lines // ROWS
 
@@ -54,6 +68,7 @@
 
     for turn in range(turns):
         fetch(turn).start()
+    fill_sums(sums)
 
     for turn in range(turns):
         fetch(turn).wait()
@@ -82,14 +97,27 @@
         ship(turn).wait()
 
 
-def edge_kernel(flags, sums, counts_first, counts_last, before, after, inner, out, ends, sem):
+def edge_kernel(flags, counts, before, after, inner, out, sums, near, rim, ends, in_sem, sem):
     del inner
     lines = out.shape[0]
+    rows = 2 * PASSES
+    fetches = [
+        pltpu.make_async_copy(counts.at[pl.ds(0, rows)], near.at[0], in_sem.at[0]),
+        pltpu.make_async_copy(counts.at[pl.ds(lines - rows, rows)], near.at[1], in_sem.at[1]),
+        pltpu.make_async_copy(before, rim.at[0], in_sem.at[2]),
+        pltpu.make_async_copy(after, rim.at[1], in_sem.at[3]),
+    ]
+    for fetch in fetches:
+        fetch.start()
+    fill_sums(sums)
+    for fetch in fetches:
+        fetch.wait()
     copies = []
     for top in (True, False):
-        near, rim = (counts_first, before) if top else (counts_last, after)
-        pair = (rim[...], near[...]) if top else (near[...], rim[...])
-        field = jnp.concatenate(pair, axis=0).astype(jnp.float32)
+        side = 0 if top else 1
+        own, beyond = near[side].astype(jnp.float32), rim[side].astype(jnp.float32)
+        pair = (beyond, own) if top else (own, beyond)
+        field = jnp.concatenate(pair, axis=0)
         beside = beside_of(field, sums[...])
         rows = [field[row] for row in range(3 * PASSES)]
         flag = flags[0] if top else flags[1]
@@ -102,7 +130,6 @@
             for row in range(beyond):
                 spot = row if top else len(rows) - 1 - row
                 rows[spot] = rows[spot] * flag
-        side = 0 if top else 1
         for row in range(PASSES):
             ends[side, row] = (SCALE * rows[row]).astype(jnp.bfloat16)
         target = out.at[pl.ds(0 if top else lines - PASSES, PASSES)]
@@ -117,20 +144,20 @@
     size, row = lax.axis_size("row"), lax.axis_index("row")
     up = [(i, i + 1) for i in range(size - 1)]
     down = [(j, i) for i, j in up]
-    first, last = lax.optimization_barrier((counts[: 2 * PASSES], counts[-2 * PASSES :]))
-    first, last = first.astype(jnp.bfloat16), last.astype(jnp.bfloat16)
-    before = lax.ppermute(last[PASSES:], "row", up)
-    after = lax.ppermute(first[:PASSES], "row", down)
+    first, last = lax.optimization_barrier((counts[:PASSES], counts[-PASSES:]))
+    before = lax.ppermute(last.astype(jnp.bfloat16), "row", up)
+    after = lax.ppermute(first.astype(jnp.bfloat16), "row", down)
     flags = jnp.stack([row > 0, row < size - 1]).astype(jnp.float32)
     shape = jax.ShapeDtypeStruct(counts.shape, jnp.bfloat16)
-    sums = column_sums(width)
     padded = (lines + 2 * ROWS, channels, width)
+    sums = pltpu.VMEM((width, PASSES * width), jnp.bfloat16)
     inner = pl.pallas_call(
         inner_kernel,
         out_shape=shape,
-        in_specs=[ANY, VMEM],
-        out_specs=ANY,
+        in_specs=[HBM],
+        out_specs=HBM,
         scratch_shapes=[
+            sums,
             pltpu.VMEM(counts.shape, jnp.int32),
             pltpu.VMEM(padded, jnp.float32),
             pltpu.VMEM((PASSES,) + padded, jnp.float32),
@@ -140,25 +167,29 @@
             pltpu.SemaphoreType.DMA((lines // ROWS,)),
             pltpu.SemaphoreType.DMA((lines // ROWS,)),
         ],
-        compiler_params=pltpu.CompilerParams(vmem_limit_bytes=44 * 1024 * 1024),
+        compiler_params=pltpu.CompilerParams(vmem_limit_bytes=INNER_MIB * 1024 * 1024),
         cost_estimate=pl.CostEstimate(
             flops=2 * lines * channels * width * width, bytes_accessed=6 * lines * channels * width, transcendentals=0
         ),
         name="smooth_inner",
-    )(counts, sums)
+    )(counts)
     return pl.pallas_call(
         edge_kernel,
         out_shape=shape,
-        in_specs=[SMEM, VMEM, VMEM, VMEM, VMEM, VMEM, ANY],
-        out_specs=ANY,
+        in_specs=[SMEM, HBM, HBM, HBM, HBM],
+        out_specs=HBM,
         scratch_shapes=[
+            sums,
+            pltpu.VMEM((2, 2 * PASSES, channels, width), jnp.int32),
             pltpu.VMEM((2, PASSES, channels, width), jnp.bfloat16),
+            pltpu.VMEM((2, PASSES, channels, width), jnp.bfloat16),
+            pltpu.SemaphoreType.DMA((4,)),
             pltpu.SemaphoreType.DMA((2,)),
         ],
-        input_output_aliases={6: 0},
-        compiler_params=pltpu.CompilerParams(vmem_limit_bytes=12 * 1024 * 1024),
+        input_output_aliases={4: 0},
+        compiler_params=pltpu.CompilerParams(vmem_limit_bytes=EDGE_MIB * 1024 * 1024),
         name="smooth_edges",
-    )(flags, sums, first, last, before, after, inner)
+    )(flags, counts, before, after, inner)
 
 
 def to_all(x, axes):
@@ -282,7 +313,7 @@
     shard = lax.axis_index("y") * lax.axis_size("row") + lax.axis_index("row")
     halves = spectra_init.reshape(CORES, HALF, -1, LANES).transpose(0, 2, 1, 3)
     own, other = halves[core], halves[1 - core]
-    block = own[shard]
+    own, other, block = lax.optimization_barrier((own, other, own[shard]))
     for iteration in range(ITERS):
         weights, kept, sent = update(core[None], data, template, own, other, weights)
         num, den = summed_block(kept, sent)

time: 283 us -> 279 us (0.986)
  blocking collectives: 137 us -> 149 us
  waiting for transfers between devices: 66.2 us -> 58.5 us
  local copies, waits for them, and re-layouts: 11.1 us -> 4.25 us
  starting transfers between devices: 41.5 us -> 38.1 us
    all_to_all x7 -> x8, blocking collectives: 82.2 us -> 93.4 us  [to_all(): lax.all_to_all(jnp.broadcast_to(x[None], (count,) + x.shape), axes, 0, 0,...]
    all_to_all x1 -> x0, waiting for transfers between devices: 7.82 us -> none  [to_all(): lax.all_to_all(jnp.broadcast_to(x[None], (count,) + x.shape), axes, 0, 0,...]
    unnamed x17 -> x11, local copies, waits for them, and re-layouts: 7.82 us -> 2.09 us
    all_to_all x1 -> x0, starting transfers between devices: 3.4 us -> none  [to_all(): lax.all_to_all(jnp.broadcast_to(x[None], (count,) + x.shape), axes, 0, 0,...]
  transfers between devices with their start and end apart: 12 -> 11, of which waited for: 10 -> 9; matrix products, arithmetic and copies ran while one was open for 1% -> 1% of each run, Pallas kernels for 2% -> 2%
where the time goes in v4:
time: 279 us; the launch traced here: 278 us
  blocking collectives  149 us (53%)
  waiting for transfers between devices  58.5 us (21%)
  starting transfers between devices  38.1 us (14%)
  Pallas kernels  26.6 us (10%)
  local copies, waits for them, and re-layouts  4.25 us (2%)
    all_to_all x8, blocking collectives, to_all(): lax.all_to_all(jnp.broadcast_to(x[None], (count,) + x.shape), axes, 0, 0,...  93.4 us
    all_to_all x4, blocking collectives, summed_block(): plane = jnp.sum(lax.all_to_all(chip, PLANE, 0, 0, tiled=True), axis=0)  55.1 us
    all_to_all x1, waiting for transfers between devices, shards(): lax.all_to_all(smoothed(counts[0]), CHAN, split_axis=0, concat_axis=0, ti...  47.4 us
    ppermute x4, starting transfers between devices, shards(): other = lax.ppermute(own, 'core', [(0, 1), (1, 0)])  16.5 us
    pallas_call x4, Pallas kernels, update(): pl.pallas_call(update_kernel, out_shape=(jax.ShapeDtypeStruct(weights.sha...  14.3 us
    all_to_all x1, starting transfers between devices, shards(): lax.all_to_all(smoothed(counts[0]), CHAN, split_axis=0, concat_axis=0, ti...  12.7 us
    pallas_call x1, Pallas kernels, smoothed(): pl.pallas_call(inner_kernel, out_shape=shape, in_specs=[HBM], out_specs=H...  6.8 us
    ppermute x4, waiting for transfers between devices, summed_block(): chip = kept + lax.ppermute(sent, 'core', [(0, 1), (1, 0)])  5.78 us
  transfers between devices with their start and end apart: 11, of which 9 were waited for; matrix products, arithmetic and copies ran while one was open for 1% of the time, Pallas kernels for 2%

profile of v4, /device:TPU:1, one launch (start us, length us, event | category | flops | bytes accessed | tf_op | source)
XLA Modules:
  0.0 277.9 jit_solution(10300528971802598787)
XLA Ops:
  0.6 1.1 slice_bitcast_fusion
  1.7 4.0 %collective-permute-start = (bf16[3,32,512]{2,1,0:T(8,128)(2,1)S(1)}, bf16[3,32,512]{2,1,0:T(8,128)(2,1)S(1)}, u32[]{:S(2)}, u32[]{:S(2)}) collective-permute-start(bf16[3,32,512]{2,1,0:T(8,128)(2,1)S(1)} %convert_element_type.13), channel_id=1, source_target_pairs={{0,1},{1,2},{2,3},{4,5},{5,6},{6,7},{8,9},{9,10},{10,11},{12,13},{... | collective-permute-start | bytes 294920 | tf_op jit(solution)/shard_map/ppermute | solution.py:148
  5.7 1.3 collective-permute-start.1
  7.0 0.1 add_convert_fusion.flags
  7.1 6.8 %smooth_inner.1.inner = bf16[64,32,512]{2,1,0:T(8,128)(2,1)} custom-call(s32[64,32,512]{2,1,0:T(8,128)} %bitcast.36), custom_call_target="tpu_custom_call" | custom-call | flops 1073741824 | bytes 6291456 | tf_op jit(solution)/shard_map/smooth_inner/pallas_call | solution.py:154
  13.9 0.0 collective-permute-done.before
  13.9 0.0 collective-permute-done.1.after
  13.9 3.4 %smooth_edges.1 = bf16[64,32,512]{2,1,0:T(8,128)(2,1)} custom-call(f32[2]{0:T(128)S(1)} %add_convert_fusion.flags, s32[64,32,512]{2,1,0:T(8,128)} %bitcast.37, bf16[3,32,512]{2,1,0:T(8,128)(2,1)S(1)} %collective-permute-done.before, bf16[3,32,512]{2,1,0:T(8,128)(2,1)S(1)} %collective-permute-done.1.after, ...), custom_call_target="tpu_custom_call", output_to_operand_aliasing={{}: (4, {})} | custom-call | tf_op jit(solution)/shard_map/smooth_edges/pallas_call | solution.py:176
  17.4 0.0 copy-start.3
  17.4 12.7 %all-to-all-start = ((bf16[64,32,512]{2,1,0:T(8,128)(2,1)}), bf16[64,32,512]{2,1,0:T(8,128)(2,1)S(1)}, u32[]{:S(2)}, u32[]{:S(2)}) async-start(bf16[64,32,512]{2,1,0:T(8,128)(2,1)} %smooth_edges.1), calls=%async_computation | async-start | bytes 4194304 | tf_op jit(solution)/shard_map/all_to_all | solution.py:308
  30.1 0.0 copy-done.3
  30.2 0.0 copy-start
  30.2 1.3 copy.13
  31.5 0.6 constant_dynamic-slice_fusion
  32.1 0.1 constant_dynamic-slice_fusion.1
  32.2 0.2 copy_bitcast_fusion
  32.4 47.4 %all-to-all-done = bf16[64,32,512]{2,1,0:T(8,128)(2,1)S(1)} async-done(((bf16[64,32,512]{2,1,0:T(8,128)(2,1)}), bf16[64,32,512]{2,1,0:T(8,128)(2,1)S(1)}, u32[]{:S(2)}, u32[]{:S(2)}) %all-to-all-start) | async-done | bytes 2097184 | tf_op jit(solution)/shard_map/all_to_all | solution.py:308
  79.8 0.0 copy-done
  79.8 3.6 %update.4 = (f32[128,512]{1,0:T(8,128)S(1)}, f32[16,56,128]{2,1,0:T(8,128)S(1)}, f32[16,56,128]{2,1,0:T(8,128)S(1)}) custom-call(s32[1]{0:T(128)} %bitcast.core, bf16[2048,512]{1,0:T(8,128)(2,1)S(1)} %bitcast.31, bf16[32,2048]{1,0:T(8,128)(2,1)S(1)} %convert_element_type.15.template, f32[16,48,128]{2,1,0:T(8,128)S(1)} %get-tuple-element.22.own, ...), custom_call_target="tpu_custom_call" | custom-call | tf_op jit(solution)/shard_map/update/pallas_call | solution.py:276
  83.4 0.0 copy-start.4
  83.4 2.2 collective-permute-start.2
  85.6 1.4 collective-permute-done.2
  87.1 0.1 add.33
  87.1 17.4 %all_to_all.65 = f32[16,56,128]{2,1,0:T(8,128)S(1)} all-to-all(f32[16,56,128]{2,1,0:T(8,128)S(1)} %add.33), channel_id=1, replica_groups=mesh['z'=8,'y'=4,'core'=2,'row'=4] {'y','row'}, dimensions={0} | all-to-all | bytes 917504 | tf_op jit(solution)/shard_map/all_to_all | solution.py:204
  104.6 11.3 %all_to_all.66 = f32[8,56,128]{2,1,0:T(8,128)S(1)} all-to-all(f32[8,56,128]{2,1,0:T(8,128)S(1)} %broadcast_in_dim.21), channel_id=1, replica_groups=mesh['z'=8,'y'=4,'core'=2,'row'=4] {'z'}, dimensions={0} | all-to-all | bytes 458752 | tf_op jit(solution)/shard_map/all_to_all | solution.py:199
  116.0 0.0 copy-done.4
  116.0 0.1 fusion.3
  116.1 12.1 %all_to_all.67.own = f32[16,48,128]{2,1,0:T(8,128)S(1)} all-to-all(f32[16,48,128]{2,1,0:T(8,128)S(1)} %broadcast_in_dim.22), channel_id=1, replica_groups=mesh['z'=8,'y'=4,'core'=2,'row'=4] {'y','row'}, dimensions={0} | all-to-all | bytes 786432 | tf_op jit(solution)/shard_map/all_to_all | solution.py:199
  128.2 4.1 %collective-permute-start.3 = (f32[16,48,128]{2,1,0:T(8,128)S(1)}, f32[16,48,128]{2,1,0:T(8,128)S(1)}, u32[]{:S(2)}, u32[]{:S(2)}) collective-permute-start(f32[16,48,128]{2,1,0:T(8,128)S(1)} %all_to_all.67.own), channel_id=1, source_target_pairs={{0,4},{4,0},{1,5},{5,1},{2,6},{6,2},{3,7},{7,3},{8,12},{12,8},{9,1... | collective-permute-start | bytes 1179656 | tf_op jit(solution)/shard_map/ppermute | solution.py:322
  132.3 1.3 collective-permute-done.3.other
  133.6 3.6 %update.5 = (f32[128,512]{1,0:T(8,128)S(1)}, f32[16,56,128]{2,1,0:T(8,128)S(1)}, f32[16,56,128]{2,1,0:T(8,128)S(1)}) custom-call(s32[1]{0:T(128)} %bitcast.core, bf16[2048,512]{1,0:T(8,128)(2,1)S(1)} %bitcast.32, bf16[32,2048]{1,0:T(8,128)(2,1)S(1)} %convert_element_type.15.template, f32[16,48,128]{2,1,0:T(8,128)S(1)} %all_to_all.67.own, ...), custom_call_target="tpu_custom_call" | custom-call | tf_op jit(solution)/shard_map/update/pallas_call | solution.py:276
  137.2 0.5 collective-permute-start.4
  137.7 1.4 collective-permute-done.4
  139.2 12.5 %all_to_all.68 = f32[16,56,128]{2,1,0:T(8,128)S(1)} all-to-all(f32[16,56,128]{2,1,0:T(8,128)S(1)} %add.34), channel_id=1, replica_groups=mesh['z'=8,'y'=4,'core'=2,'row'=4] {'y','row'}, dimensions={0} | all-to-all | bytes 917504 | tf_op jit(solution)/shard_map/all_to_all | solution.py:204
  151.8 11.3 %all_to_all.69 = f32[8,56,128]{2,1,0:T(8,128)S(1)} all-to-all(f32[8,56,128]{2,1,0:T(8,128)S(1)} %broadcast_in_dim.23), channel_id=1, replica_groups=mesh['z'=8,'y'=4,'core'=2,'row'=4] {'z'}, dimensions={0} | all-to-all | bytes 458752 | tf_op jit(solution)/shard_map/all_to_all | solution.py:199
  163.1 0.1 fusion.2
  163.2 12.1 %all_to_all.70.own = f32[16,48,128]{2,1,0:T(8,128)S(1)} all-to-all(f32[16,48,128]{2,1,0:T(8,128)S(1)} %broadcast_in_dim.24), channel_id=1, replica_groups=mesh['z'=8,'y'=4,'core'=2,'row'=4] {'y','row'}, dimensions={0} | all-to-all | bytes 786432 | tf_op jit(solution)/shard_map/all_to_all | solution.py:199
  175.3 4.1 %collective-permute-start.5 = (f32[16,48,128]{2,1,0:T(8,128)S(1)}, f32[16,48,128]{2,1,0:T(8,128)S(1)}, u32[]{:S(2)}, u32[]{:S(2)}) collective-permute-start(f32[16,48,128]{2,1,0:T(8,128)S(1)} %all_to_all.70.own), channel_id=1, source_target_pairs={{0,4},{4,0},{1,5},{5,1},{2,6},{6,2},{3,7},{7,3},{8,12},{12,8},{9,1... | collective-permute-start | bytes 1179656 | tf_op jit(solution)/shard_map/ppermute | solution.py:322
  179.4 1.3 collective-permute-done.5.other
  180.8 3.6 %update.6 = (f32[128,512]{1,0:T(8,128)S(1)}, f32[16,56,128]{2,1,0:T(8,128)S(1)}, f32[16,56,128]{2,1,0:T(8,128)S(1)}) custom-call(s32[1]{0:T(128)} %bitcast.core, bf16[2048,512]{1,0:T(8,128)(2,1)S(1)} %bitcast.33, bf16[32,2048]{1,0:T(8,128)(2,1)S(1)} %convert_element_type.15.template, f32[16,48,128]{2,1,0:T(8,128)S(1)} %all_to_all.70.own, ...), custom_call_target="tpu_custom_call" | custom-call | tf_op jit(solution)/shard_map/update/pallas_call | solution.py:276
  184.4 0.5 collective-permute-start.6
  184.8 1.4 collective-permute-done.6
  186.3 12.6 %all_to_all.71 = f32[16,56,128]{2,1,0:T(8,128)S(1)} all-to-all(f32[16,56,128]{2,1,0:T(8,128)S(1)} %add.35), channel_id=1, replica_groups=mesh['z'=8,'y'=4,'core'=2,'row'=4] {'y','row'}, dimensions={0} | all-to-all | bytes 917504 | tf_op jit(solution)/shard_map/all_to_all | solution.py:204
  199.0 11.3 %all_to_all.72 = f32[8,56,128]{2,1,0:T(8,128)S(1)} all-to-all(f32[8,56,128]{2,1,0:T(8,128)S(1)} %broadcast_in_dim.25), channel_id=1, replica_groups=mesh['z'=8,'y'=4,'core'=2,'row'=4] {'z'}, dimensions={0} | all-to-all | bytes 458752 | tf_op jit(solution)/shard_map/all_to_all | solution.py:199
  210.3 0.1 fusion.1
  210.4 12.1 %all_to_all.73.own = f32[16,48,128]{2,1,0:T(8,128)S(1)} all-to-all(f32[16,48,128]{2,1,0:T(8,128)S(1)} %broadcast_in_dim.26), channel_id=1, replica_groups=mesh['z'=8,'y'=4,'core'=2,'row'=4] {'y','row'}, dimensions={0} | all-to-all | bytes 786432 | tf_op jit(solution)/shard_map/all_to_all | solution.py:199
  222.5 4.1 %collective-permute-start.7 = (f32[16,48,128]{2,1,0:T(8,128)S(1)}, f32[16,48,128]{2,1,0:T(8,128)S(1)}, u32[]{:S(2)}, u32[]{:S(2)}) collective-permute-start(f32[16,48,128]{2,1,0:T(8,128)S(1)} %all_to_all.73.own), channel_id=1, source_target_pairs={{0,4},{4,0},{1,5},{5,1},{2,6},{6,2},{3,7},{7,3},{8,12},{12,8},{9,1... | collective-permute-start | bytes 1179656 | tf_op jit(solution)/shard_map/ppermute | solution.py:322
  226.6 1.3 collective-permute-done.7.other
  228.0 3.6 %update.7 = (f32[128,512]{1,0:T(8,128)}, f32[16,56,128]{2,1,0:T(8,128)S(1)}, f32[16,56,128]{2,1,0:T(8,128)S(1)}) custom-call(s32[1]{0:T(128)} %bitcast.core, bf16[2048,512]{1,0:T(8,128)(2,1)S(1)} %bitcast.34, bf16[32,2048]{1,0:T(8,128)(2,1)S(1)} %convert_element_type.15.template, f32[16,48,128]{2,1,0:T(8,128)S(1)} %all_to_all.73.own, ...), custom_call_target="tpu_custom_call" | custom-call | tf_op jit(solution)/shard_map/update/pallas_call | solution.py:276
  231.5 0.5 collective-permute-start.8
  232.0 1.4 collective-permute-done.8
  233.5 12.5 %all_to_all.74 = f32[16,56,128]{2,1,0:T(8,128)S(1)} all-to-all(f32[16,56,128]{2,1,0:T(8,128)S(1)} %add.36), channel_id=1, replica_groups=mesh['z'=8,'y'=4,'core'=2,'row'=4] {'y','row'}, dimensions={0} | all-to-all | bytes 917504 | tf_op jit(solution)/shard_map/all_to_all | solution.py:204
  246.1 11.3 %all_to_all.75 = f32[8,56,128]{2,1,0:T(8,128)S(1)} all-to-all(f32[8,56,128]{2,1,0:T(8,128)S(1)} %broadcast_in_dim.28), channel_id=1, replica_groups=mesh['z'=8,'y'=4,'core'=2,'row'=4] {'z'}, dimensions={0} | all-to-all | bytes 458752 | tf_op jit(solution)/shard_map/all_to_all | solution.py:199
  257.4 0.1 fusion
  257.6 12.1 %all_to_all.76.own = f32[16,48,128]{2,1,0:T(8,128)S(1)} all-to-all(f32[16,48,128]{2,1,0:T(8,128)S(1)} %broadcast_in_dim.29), channel_id=1, replica_groups=mesh['z'=8,'y'=4,'core'=2,'row'=4] {'y','row'}, dimensions={0} | all-to-all | bytes 786432 | tf_op jit(solution)/shard_map/all_to_all | solution.py:199
  269.6 0.0 copy-start.1
  269.6 4.1 %collective-permute-start.9 = (f32[16,48,128]{2,1,0:T(8,128)S(1)}, f32[16,48,128]{2,1,0:T(8,128)S(1)}, u32[]{:S(2)}, u32[]{:S(2)}) collective-permute-start(f32[16,48,128]{2,1,0:T(8,128)S(1)} %all_to_all.76.own), channel_id=1, source_target_pairs={{0,4},{4,0},{1,5},{5,1},{2,6},{6,2},{3,7},{7,3},{8,12},{12,8},{9,1... | collective-permute-start | bytes 1179656 | tf_op jit(solution)/shard_map/ppermute | solution.py:322
  273.8 1.3 collective-permute-done.9.other
  275.1 0.0 copy-done.1
  275.1 0.0 copy-start.2
  275.1 0.7 copy-done.2
  275.9 2.0 whole.1
  (26 shorter events, 0.6 us)
Async XLA Ops:
  1.7 12.2 %collective-permute-start = (bf16[3,32,512]{2,1,0:T(8,128)(2,1)S(1)}, bf16[3,32,512]{2,1,0:T(8,128)(2,1)S(1)}, u32[]{:S(2)}, u32[]{:S(2)}) collective-permute-start(bf16[3,32,512]{2,1,0:T(8,128)(2,1)S(1)} %convert_element_type.13), channel_id=1, source_target_pairs={{0,1},{1,2},{2,3},{4,5},{5,6},{6,7},{8,9},{9,10},{10,11},{12,13},{... | collective-permute-start | bytes 294920 | tf_op jit(solution)/shard_map/ppermute | solution.py:148
  5.7 8.2 %collective-permute-start.1 = (bf16[3,32,512]{2,1,0:T(8,128)(2,1)S(1)}, bf16[3,32,512]{2,1,0:T(8,128)(2,1)S(1)}, u32[]{:S(2)}, u32[]{:S(2)}) collective-permute-start(bf16[3,32,512]{2,1,0:T(8,128)(2,1)S(1)} %convert_element_type.14), channel_id=1, source_target_pairs={{1,0},{2,1},{3,2},{5,4},{6,5},{7,6},{9,8},{10,9},{11,10},{13,12},{... | collective-permute-start | bytes 294920 | tf_op jit(solution)/shard_map/ppermute | solution.py:149
  17.4 12.8 %copy-start.3 = (s32[32,2048]{1,0:T(8,128)S(1)}, s32[32,2048]{1,0:T(8,128)}, u32[]{:S(2)}) copy-start(s32[32,2048]{1,0:T(8,128)} %param.5) | copy-start | bytes 786436
  17.4 62.4 %all-to-all-start = ((bf16[64,32,512]{2,1,0:T(8,128)(2,1)}), bf16[64,32,512]{2,1,0:T(8,128)(2,1)S(1)}, u32[]{:S(2)}, u32[]{:S(2)}) async-start(bf16[64,32,512]{2,1,0:T(8,128)(2,1)} %smooth_edges.1), calls=%async_computation | async-start | bytes 4194304 | tf_op jit(solution)/shard_map/all_to_all | solution.py:308
  30.2 49.6 %copy-start = (f32[1,1,128,512]{3,2,1,0:T(8,128)S(1)}, f32[1,1,128,512]{3,2,1,0:T(8,128)}, u32[]{:S(2)}) copy-start(f32[1,1,128,512]{3,2,1,0:T(8,128)} %param.6) | copy-start | bytes 786436
  83.4 32.5 %copy-start.4 = (f32[1,48,1,128]{3,2,1,0:T(1,128)S(1)}, f32[1,48,1,128]{3,2,1,0:T(1,128)}, u32[]{:S(2)}) copy-start(f32[1,48,1,128]{3,2,1,0:T(1,128)} %constant_dynamic-slice_fusion) | copy-start | bytes 73732
  83.4 3.7 %collective-permute-start.2 = (f32[16,56,128]{2,1,0:T(8,128)S(1)}, f32[16,56,128]{2,1,0:T(8,128)S(1)}, u32[]{:S(2)}, u32[]{:S(2)}) collective-permute-start(f32[16,56,128]{2,1,0:T(8,128)S(1)} %get-tuple-element.25), channel_id=1, source_target_pairs={{0,4},{4,0},{1,5},{5,1},{2,6},{6,2},{3,7},{7,3},{8,12},{12,8},{9,1... | collective-permute-start | bytes 1376264 | tf_op jit(solution)/shard_map/ppermute | solution.py:203
  128.2 5.5 %collective-permute-start.3 = (f32[16,48,128]{2,1,0:T(8,128)S(1)}, f32[16,48,128]{2,1,0:T(8,128)S(1)}, u32[]{:S(2)}, u32[]{:S(2)}) collective-permute-start(f32[16,48,128]{2,1,0:T(8,128)S(1)} %all_to_all.67.own), channel_id=1, source_target_pairs={{0,4},{4,0},{1,5},{5,1},{2,6},{6,2},{3,7},{7,3},{8,12},{12,8},{9,1... | collective-permute-start | bytes 1179656 | tf_op jit(solution)/shard_map/ppermute | solution.py:322
  137.2 1.9 collective-permute-start.4
  175.3 5.5 %collective-permute-start.5 = (f32[16,48,128]{2,1,0:T(8,128)S(1)}, f32[16,48,128]{2,1,0:T(8,128)S(1)}, u32[]{:S(2)}, u32[]{:S(2)}) collective-permute-start(f32[16,48,128]{2,1,0:T(8,128)S(1)} %all_to_all.70.own), channel_id=1, source_target_pairs={{0,4},{4,0},{1,5},{5,1},{2,6},{6,2},{3,7},{7,3},{8,12},{12,8},{9,1... | collective-permute-start | bytes 1179656 | tf_op jit(solution)/shard_map/ppermute | solution.py:322
  184.4 1.9 collective-permute-start.6
  222.5 5.5 %collective-permute-start.7 = (f32[16,48,128]{2,1,0:T(8,128)S(1)}, f32[16,48,128]{2,1,0:T(8,128)S(1)}, u32[]{:S(2)}, u32[]{:S(2)}) collective-permute-start(f32[16,48,128]{2,1,0:T(8,128)S(1)} %all_to_all.73.own), channel_id=1, source_target_pairs={{0,4},{4,0},{1,5},{5,1},{2,6},{6,2},{3,7},{7,3},{8,12},{12,8},{9,1... | collective-permute-start | bytes 1179656 | tf_op jit(solution)/shard_map/ppermute | solution.py:322
  231.5 1.9 collective-permute-start.8
  269.6 5.5 %copy-start.1 = (f32[16,48,128]{2,1,0:T(8,128)}, f32[16,48,128]{2,1,0:T(8,128)S(1)}, u32[]{:S(2)}) copy-start(f32[16,48,128]{2,1,0:T(8,128)S(1)} %all_to_all.76.own) | copy-start | bytes 1179652
  269.6 5.5 %collective-permute-start.9 = (f32[16,48,128]{2,1,0:T(8,128)S(1)}, f32[16,48,128]{2,1,0:T(8,128)S(1)}, u32[]{:S(2)}, u32[]{:S(2)}) collective-permute-start(f32[16,48,128]{2,1,0:T(8,128)S(1)} %all_to_all.76.own), channel_id=1, source_target_pairs={{0,4},{4,0},{1,5},{5,1},{2,6},{6,2},{3,7},{7,3},{8,12},{12,8},{9,1... | collective-permute-start | bytes 1179656 | tf_op jit(solution)/shard_map/ppermute | solution.py:322
  275.1 0.8 copy-start.2

commit v5 on v4

--- a/solution.py
+++ b/solution.py
@@ -300,6 +300,7 @@
         out_shape=jax.ShapeDtypeStruct((FREE, own.shape[0] * LANES), jnp.float32),
         in_specs=[SMEM, VMEM, VMEM],
         out_specs=VMEM,
+        compiler_params=pltpu.CompilerParams(vmem_limit_bytes=4 * 1024 * 1024),
         name="whole",
     )(core, own, other)
 

time: 279 us -> 277 us (level)
  no operation moved by 1% of the time
where the time goes in v5:
time: 277 us; the launch traced here: 276 us
  blocking collectives  149 us (54%)
  waiting for transfers between devices  58.5 us (21%)
  starting transfers between devices  38.1 us (14%)
  Pallas kernels  25.5 us (9%)
  local copies, waits for them, and re-layouts  3.5 us (1%)
    all_to_all x8, blocking collectives, to_all(): lax.all_to_all(jnp.broadcast_to(x[None], (count,) + x.shape), axes, 0, 0,...  93.4 us
    all_to_all x4, blocking collectives, summed_block(): plane = jnp.sum(lax.all_to_all(chip, PLANE, 0, 0, tiled=True), axis=0)  55.1 us
    all_to_all x1, waiting for transfers between devices, shards(): lax.all_to_all(smoothed(counts[0]), CHAN, split_axis=0, concat_axis=0, ti...  47.4 us
    ppermute x4, starting transfers between devices, shards(): other = lax.ppermute(own, 'core', [(0, 1), (1, 0)])  16.5 us
    pallas_call x4, Pallas kernels, update(): pl.pallas_call(update_kernel, out_shape=(jax.ShapeDtypeStruct(weights.sha...  14.3 us
    all_to_all x1, starting transfers between devices, shards(): lax.all_to_all(smoothed(counts[0]), CHAN, split_axis=0, concat_axis=0, ti...  12.7 us
    pallas_call x1, Pallas kernels, smoothed(): pl.pallas_call(inner_kernel, out_shape=shape, in_specs=[HBM], out_specs=H...  6.79 us
    ppermute x4, waiting for transfers between devices, summed_block(): chip = kept + lax.ppermute(sent, 'core', [(0, 1), (1, 0)])  5.78 us
  transfers between devices with their start and end apart: 11, of which 9 were waited for; matrix products, arithmetic and copies ran while one was open for 1% of the time, Pallas kernels for 2%

profile of v5, /device:TPU:1, one launch (start us, length us, event | category | flops | bytes accessed | tf_op | source)
XLA Modules:
  0.0 276.0 jit_solution(4671182532409842506)
XLA Ops:
  0.6 1.1 slice_bitcast_fusion
  1.7 4.0 %collective-permute-start = (bf16[3,32,512]{2,1,0:T(8,128)(2,1)S(1)}, bf16[3,32,512]{2,1,0:T(8,128)(2,1)S(1)}, u32[]{:S(2)}, u32[]{:S(2)}) collective-permute-start(bf16[3,32,512]{2,1,0:T(8,128)(2,1)S(1)} %convert_element_type.13), channel_id=1, source_target_pairs={{0,1},{1,2},{2,3},{4,5},{5,6},{6,7},{8,9},{9,10},{10,11},{12,13},{... | collective-permute-start | bytes 294920 | tf_op jit(solution)/shard_map/ppermute | solution.py:148
  5.7 1.3 collective-permute-start.1
  7.0 0.1 add_convert_fusion.flags
  7.1 6.8 %smooth_inner.1.inner = bf16[64,32,512]{2,1,0:T(8,128)(2,1)} custom-call(s32[64,32,512]{2,1,0:T(8,128)} %bitcast.36), custom_call_target="tpu_custom_call" | custom-call | flops 1073741824 | bytes 6291456 | tf_op jit(solution)/shard_map/smooth_inner/pallas_call | solution.py:154
  13.9 0.0 collective-permute-done.before
  13.9 0.0 collective-permute-done.1.after
  13.9 3.4 %smooth_edges.1 = bf16[64,32,512]{2,1,0:T(8,128)(2,1)} custom-call(f32[2]{0:T(128)S(1)} %add_convert_fusion.flags, s32[64,32,512]{2,1,0:T(8,128)} %bitcast.37, bf16[3,32,512]{2,1,0:T(8,128)(2,1)S(1)} %collective-permute-done.before, bf16[3,32,512]{2,1,0:T(8,128)(2,1)S(1)} %collective-permute-done.1.after, ...), custom_call_target="tpu_custom_call", output_to_operand_aliasing={{}: (4, {})} | custom-call | tf_op jit(solution)/shard_map/smooth_edges/pallas_call | solution.py:176
  17.3 0.0 copy-start.1
  17.4 12.7 %all-to-all-start = ((bf16[64,32,512]{2,1,0:T(8,128)(2,1)}), bf16[64,32,512]{2,1,0:T(8,128)(2,1)S(1)}, u32[]{:S(2)}, u32[]{:S(2)}) async-start(bf16[64,32,512]{2,1,0:T(8,128)(2,1)} %smooth_edges.1), calls=%async_computation | async-start | bytes 4194304 | tf_op jit(solution)/shard_map/all_to_all | solution.py:309
  30.1 0.0 copy-done.1
  30.2 0.0 copy-start
  30.2 1.3 copy.13
  31.5 0.6 constant_dynamic-slice_fusion
  32.1 0.1 constant_dynamic-slice_fusion.1
  32.2 0.2 copy_bitcast_fusion
  32.4 47.4 %all-to-all-done = bf16[64,32,512]{2,1,0:T(8,128)(2,1)S(1)} async-done(((bf16[64,32,512]{2,1,0:T(8,128)(2,1)}), bf16[64,32,512]{2,1,0:T(8,128)(2,1)S(1)}, u32[]{:S(2)}, u32[]{:S(2)}) %all-to-all-start) | async-done | bytes 2097184 | tf_op jit(solution)/shard_map/all_to_all | solution.py:309
  79.8 0.0 copy-done
  79.8 3.6 %update.4 = (f32[128,512]{1,0:T(8,128)S(1)}, f32[16,56,128]{2,1,0:T(8,128)S(1)}, f32[16,56,128]{2,1,0:T(8,128)S(1)}) custom-call(s32[1]{0:T(128)} %bitcast.core, bf16[2048,512]{1,0:T(8,128)(2,1)S(1)} %bitcast.31, bf16[32,2048]{1,0:T(8,128)(2,1)S(1)} %convert_element_type.15.template, f32[16,48,128]{2,1,0:T(8,128)S(1)} %get-tuple-element.22.own, ...), custom_call_target="tpu_custom_call" | custom-call | tf_op jit(solution)/shard_map/update/pallas_call | solution.py:276
  83.4 0.0 copy-start.2
  83.4 2.2 collective-permute-start.2
  85.6 1.4 collective-permute-done.2
  87.1 0.1 add.33
  87.1 17.4 %all_to_all.65 = f32[16,56,128]{2,1,0:T(8,128)S(1)} all-to-all(f32[16,56,128]{2,1,0:T(8,128)S(1)} %add.33), channel_id=1, replica_groups=mesh['z'=8,'y'=4,'core'=2,'row'=4] {'y','row'}, dimensions={0} | all-to-all | bytes 917504 | tf_op jit(solution)/shard_map/all_to_all | solution.py:204
  104.6 11.3 %all_to_all.66 = f32[8,56,128]{2,1,0:T(8,128)S(1)} all-to-all(f32[8,56,128]{2,1,0:T(8,128)S(1)} %broadcast_in_dim.21), channel_id=1, replica_groups=mesh['z'=8,'y'=4,'core'=2,'row'=4] {'z'}, dimensions={0} | all-to-all | bytes 458752 | tf_op jit(solution)/shard_map/all_to_all | solution.py:199
  115.9 0.0 copy-done.2
  116.0 0.1 fusion.3
  116.1 12.1 %all_to_all.67.own = f32[16,48,128]{2,1,0:T(8,128)S(1)} all-to-all(f32[16,48,128]{2,1,0:T(8,128)S(1)} %broadcast_in_dim.22), channel_id=1, replica_groups=mesh['z'=8,'y'=4,'core'=2,'row'=4] {'y','row'}, dimensions={0} | all-to-all | bytes 786432 | tf_op jit(solution)/shard_map/all_to_all | solution.py:199
  128.2 4.1 %collective-permute-start.3 = (f32[16,48,128]{2,1,0:T(8,128)S(1)}, f32[16,48,128]{2,1,0:T(8,128)S(1)}, u32[]{:S(2)}, u32[]{:S(2)}) collective-permute-start(f32[16,48,128]{2,1,0:T(8,128)S(1)} %all_to_all.67.own), channel_id=1, source_target_pairs={{0,4},{4,0},{1,5},{5,1},{2,6},{6,2},{3,7},{7,3},{8,12},{12,8},{9,1... | collective-permute-start | bytes 1179656 | tf_op jit(solution)/shard_map/ppermute | solution.py:323
  132.3 1.3 collective-permute-done.3.other
  133.6 3.6 %update.5 = (f32[128,512]{1,0:T(8,128)S(1)}, f32[16,56,128]{2,1,0:T(8,128)S(1)}, f32[16,56,128]{2,1,0:T(8,128)S(1)}) custom-call(s32[1]{0:T(128)} %bitcast.core, bf16[2048,512]{1,0:T(8,128)(2,1)S(1)} %bitcast.32, bf16[32,2048]{1,0:T(8,128)(2,1)S(1)} %convert_element_type.15.template, f32[16,48,128]{2,1,0:T(8,128)S(1)} %all_to_all.67.own, ...), custom_call_target="tpu_custom_call" | custom-call | tf_op jit(solution)/shard_map/update/pallas_call | solution.py:276
  137.2 0.5 collective-permute-start.4
  137.7 1.4 collective-permute-done.4
  139.2 12.5 %all_to_all.68 = f32[16,56,128]{2,1,0:T(8,128)S(1)} all-to-all(f32[16,56,128]{2,1,0:T(8,128)S(1)} %add.34), channel_id=1, replica_groups=mesh['z'=8,'y'=4,'core'=2,'row'=4] {'y','row'}, dimensions={0} | all-to-all | bytes 917504 | tf_op jit(solution)/shard_map/all_to_all | solution.py:204
  151.8 11.3 %all_to_all.69 = f32[8,56,128]{2,1,0:T(8,128)S(1)} all-to-all(f32[8,56,128]{2,1,0:T(8,128)S(1)} %broadcast_in_dim.23), channel_id=1, replica_groups=mesh['z'=8,'y'=4,'core'=2,'row'=4] {'z'}, dimensions={0} | all-to-all | bytes 458752 | tf_op jit(solution)/shard_map/all_to_all | solution.py:199
  163.1 0.1 fusion.2
  163.2 12.1 %all_to_all.70.own = f32[16,48,128]{2,1,0:T(8,128)S(1)} all-to-all(f32[16,48,128]{2,1,0:T(8,128)S(1)} %broadcast_in_dim.24), channel_id=1, replica_groups=mesh['z'=8,'y'=4,'core'=2,'row'=4] {'y','row'}, dimensions={0} | all-to-all | bytes 786432 | tf_op jit(solution)/shard_map/all_to_all | solution.py:199
  175.3 4.1 %collective-permute-start.5 = (f32[16,48,128]{2,1,0:T(8,128)S(1)}, f32[16,48,128]{2,1,0:T(8,128)S(1)}, u32[]{:S(2)}, u32[]{:S(2)}) collective-permute-start(f32[16,48,128]{2,1,0:T(8,128)S(1)} %all_to_all.70.own), channel_id=1, source_target_pairs={{0,4},{4,0},{1,5},{5,1},{2,6},{6,2},{3,7},{7,3},{8,12},{12,8},{9,1... | collective-permute-start | bytes 1179656 | tf_op jit(solution)/shard_map/ppermute | solution.py:323
  179.4 1.3 collective-permute-done.5.other
  180.8 3.6 %update.6 = (f32[128,512]{1,0:T(8,128)S(1)}, f32[16,56,128]{2,1,0:T(8,128)S(1)}, f32[16,56,128]{2,1,0:T(8,128)S(1)}) custom-call(s32[1]{0:T(128)} %bitcast.core, bf16[2048,512]{1,0:T(8,128)(2,1)S(1)} %bitcast.33, bf16[32,2048]{1,0:T(8,128)(2,1)S(1)} %convert_element_type.15.template, f32[16,48,128]{2,1,0:T(8,128)S(1)} %all_to_all.70.own, ...), custom_call_target="tpu_custom_call" | custom-call | tf_op jit(solution)/shard_map/update/pallas_call | solution.py:276
  184.4 0.5 collective-permute-start.6
  184.8 1.4 collective-permute-done.6
  186.3 12.6 %all_to_all.71 = f32[16,56,128]{2,1,0:T(8,128)S(1)} all-to-all(f32[16,56,128]{2,1,0:T(8,128)S(1)} %add.35), channel_id=1, replica_groups=mesh['z'=8,'y'=4,'core'=2,'row'=4] {'y','row'}, dimensions={0} | all-to-all | bytes 917504 | tf_op jit(solution)/shard_map/all_to_all | solution.py:204
  199.0 11.3 %all_to_all.72 = f32[8,56,128]{2,1,0:T(8,128)S(1)} all-to-all(f32[8,56,128]{2,1,0:T(8,128)S(1)} %broadcast_in_dim.25), channel_id=1, replica_groups=mesh['z'=8,'y'=4,'core'=2,'row'=4] {'z'}, dimensions={0} | all-to-all | bytes 458752 | tf_op jit(solution)/shard_map/all_to_all | solution.py:199
  210.3 0.1 fusion.1
  210.4 12.1 %all_to_all.73.own = f32[16,48,128]{2,1,0:T(8,128)S(1)} all-to-all(f32[16,48,128]{2,1,0:T(8,128)S(1)} %broadcast_in_dim.26), channel_id=1, replica_groups=mesh['z'=8,'y'=4,'core'=2,'row'=4] {'y','row'}, dimensions={0} | all-to-all | bytes 786432 | tf_op jit(solution)/shard_map/all_to_all | solution.py:199
  222.5 4.1 %collective-permute-start.7 = (f32[16,48,128]{2,1,0:T(8,128)S(1)}, f32[16,48,128]{2,1,0:T(8,128)S(1)}, u32[]{:S(2)}, u32[]{:S(2)}) collective-permute-start(f32[16,48,128]{2,1,0:T(8,128)S(1)} %all_to_all.73.own), channel_id=1, source_target_pairs={{0,4},{4,0},{1,5},{5,1},{2,6},{6,2},{3,7},{7,3},{8,12},{12,8},{9,1... | collective-permute-start | bytes 1179656 | tf_op jit(solution)/shard_map/ppermute | solution.py:323
  226.6 1.3 collective-permute-done.7.other
  227.9 3.6 %update.7 = (f32[128,512]{1,0:T(8,128)}, f32[16,56,128]{2,1,0:T(8,128)S(1)}, f32[16,56,128]{2,1,0:T(8,128)S(1)}) custom-call(s32[1]{0:T(128)} %bitcast.core, bf16[2048,512]{1,0:T(8,128)(2,1)S(1)} %bitcast.34, bf16[32,2048]{1,0:T(8,128)(2,1)S(1)} %convert_element_type.15.template, f32[16,48,128]{2,1,0:T(8,128)S(1)} %all_to_all.73.own, ...), custom_call_target="tpu_custom_call" | custom-call | tf_op jit(solution)/shard_map/update/pallas_call | solution.py:276
  231.5 0.5 collective-permute-start.8
  232.0 1.4 collective-permute-done.8
  233.5 12.5 %all_to_all.74 = f32[16,56,128]{2,1,0:T(8,128)S(1)} all-to-all(f32[16,56,128]{2,1,0:T(8,128)S(1)} %add.36), channel_id=1, replica_groups=mesh['z'=8,'y'=4,'core'=2,'row'=4] {'y','row'}, dimensions={0} | all-to-all | bytes 917504 | tf_op jit(solution)/shard_map/all_to_all | solution.py:204
  246.1 11.3 %all_to_all.75 = f32[8,56,128]{2,1,0:T(8,128)S(1)} all-to-all(f32[8,56,128]{2,1,0:T(8,128)S(1)} %broadcast_in_dim.28), channel_id=1, replica_groups=mesh['z'=8,'y'=4,'core'=2,'row'=4] {'z'}, dimensions={0} | all-to-all | bytes 458752 | tf_op jit(solution)/shard_map/all_to_all | solution.py:199
  257.4 0.1 fusion
  257.6 12.1 %all_to_all.76.own = f32[16,48,128]{2,1,0:T(8,128)S(1)} all-to-all(f32[16,48,128]{2,1,0:T(8,128)S(1)} %broadcast_in_dim.29), channel_id=1, replica_groups=mesh['z'=8,'y'=4,'core'=2,'row'=4] {'y','row'}, dimensions={0} | all-to-all | bytes 786432 | tf_op jit(solution)/shard_map/all_to_all | solution.py:199
  269.6 4.1 %collective-permute-start.9 = (f32[16,48,128]{2,1,0:T(8,128)S(1)}, f32[16,48,128]{2,1,0:T(8,128)S(1)}, u32[]{:S(2)}, u32[]{:S(2)}) collective-permute-start(f32[16,48,128]{2,1,0:T(8,128)S(1)} %all_to_all.76.own), channel_id=1, source_target_pairs={{0,4},{4,0},{1,5},{5,1},{2,6},{6,2},{3,7},{7,3},{8,12},{12,8},{9,1... | collective-permute-start | bytes 1179656 | tf_op jit(solution)/shard_map/ppermute | solution.py:323
  273.7 1.3 collective-permute-done.9.other
  275.1 0.9 whole.1
  (26 shorter events, 0.6 us)
Async XLA Ops:
  1.7 12.2 %collective-permute-start = (bf16[3,32,512]{2,1,0:T(8,128)(2,1)S(1)}, bf16[3,32,512]{2,1,0:T(8,128)(2,1)S(1)}, u32[]{:S(2)}, u32[]{:S(2)}) collective-permute-start(bf16[3,32,512]{2,1,0:T(8,128)(2,1)S(1)} %convert_element_type.13), channel_id=1, source_target_pairs={{0,1},{1,2},{2,3},{4,5},{5,6},{6,7},{8,9},{9,10},{10,11},{12,13},{... | collective-permute-start | bytes 294920 | tf_op jit(solution)/shard_map/ppermute | solution.py:148
  5.7 8.2 %collective-permute-start.1 = (bf16[3,32,512]{2,1,0:T(8,128)(2,1)S(1)}, bf16[3,32,512]{2,1,0:T(8,128)(2,1)S(1)}, u32[]{:S(2)}, u32[]{:S(2)}) collective-permute-start(bf16[3,32,512]{2,1,0:T(8,128)(2,1)S(1)} %convert_element_type.14), channel_id=1, source_target_pairs={{1,0},{2,1},{3,2},{5,4},{6,5},{7,6},{9,8},{10,9},{11,10},{13,12},{... | collective-permute-start | bytes 294920 | tf_op jit(solution)/shard_map/ppermute | solution.py:149
  17.3 12.8 %copy-start.1 = (s32[32,2048]{1,0:T(8,128)S(1)}, s32[32,2048]{1,0:T(8,128)}, u32[]{:S(2)}) copy-start(s32[32,2048]{1,0:T(8,128)} %param.5) | copy-start | bytes 786436
  17.4 62.4 %all-to-all-start = ((bf16[64,32,512]{2,1,0:T(8,128)(2,1)}), bf16[64,32,512]{2,1,0:T(8,128)(2,1)S(1)}, u32[]{:S(2)}, u32[]{:S(2)}) async-start(bf16[64,32,512]{2,1,0:T(8,128)(2,1)} %smooth_edges.1), calls=%async_computation | async-start | bytes 4194304 | tf_op jit(solution)/shard_map/all_to_all | solution.py:309
  30.2 49.6 %copy-start = (f32[1,1,128,512]{3,2,1,0:T(8,128)S(1)}, f32[1,1,128,512]{3,2,1,0:T(8,128)}, u32[]{:S(2)}) copy-start(f32[1,1,128,512]{3,2,1,0:T(8,128)} %param.6) | copy-start | bytes 786436
  83.4 32.6 %copy-start.2 = (f32[1,48,1,128]{3,2,1,0:T(1,128)S(1)}, f32[1,48,1,128]{3,2,1,0:T(1,128)}, u32[]{:S(2)}) copy-start(f32[1,48,1,128]{3,2,1,0:T(1,128)} %constant_dynamic-slice_fusion) | copy-start | bytes 73732
  83.4 3.7 %collective-permute-start.2 = (f32[16,56,128]{2,1,0:T(8,128)S(1)}, f32[16,56,128]{2,1,0:T(8,128)S(1)}, u32[]{:S(2)}, u32[]{:S(2)}) collective-permute-start(f32[16,56,128]{2,1,0:T(8,128)S(1)} %get-tuple-element.25), channel_id=1, source_target_pairs={{0,4},{4,0},{1,5},{5,1},{2,6},{6,2},{3,7},{7,3},{8,12},{12,8},{9,1... | collective-permute-start | bytes 1376264 | tf_op jit(solution)/shard_map/ppermute | solution.py:203
  128.2 5.5 %collective-permute-start.3 = (f32[16,48,128]{2,1,0:T(8,128)S(1)}, f32[16,48,128]{2,1,0:T(8,128)S(1)}, u32[]{:S(2)}, u32[]{:S(2)}) collective-permute-start(f32[16,48,128]{2,1,0:T(8,128)S(1)} %all_to_all.67.own), channel_id=1, source_target_pairs={{0,4},{4,0},{1,5},{5,1},{2,6},{6,2},{3,7},{7,3},{8,12},{12,8},{9,1... | collective-permute-start | bytes 1179656 | tf_op jit(solution)/shard_map/ppermute | solution.py:323
  137.2 1.9 collective-permute-start.4
  175.3 5.5 %collective-permute-start.5 = (f32[16,48,128]{2,1,0:T(8,128)S(1)}, f32[16,48,128]{2,1,0:T(8,128)S(1)}, u32[]{:S(2)}, u32[]{:S(2)}) collective-permute-start(f32[16,48,128]{2,1,0:T(8,128)S(1)} %all_to_all.70.own), channel_id=1, source_target_pairs={{0,4},{4,0},{1,5},{5,1},{2,6},{6,2},{3,7},{7,3},{8,12},{12,8},{9,1... | collective-permute-start | bytes 1179656 | tf_op jit(solution)/shard_map/ppermute | solution.py:323
  184.4 1.9 collective-permute-start.6
  222.5 5.5 %collective-permute-start.7 = (f32[16,48,128]{2,1,0:T(8,128)S(1)}, f32[16,48,128]{2,1,0:T(8,128)S(1)}, u32[]{:S(2)}, u32[]{:S(2)}) collective-permute-start(f32[16,48,128]{2,1,0:T(8,128)S(1)} %all_to_all.73.own), channel_id=1, source_target_pairs={{0,4},{4,0},{1,5},{5,1},{2,6},{6,2},{3,7},{7,3},{8,12},{12,8},{9,1... | collective-permute-start | bytes 1179656 | tf_op jit(solution)/shard_map/ppermute | solution.py:323
  231.5 1.9 collective-permute-start.8
  269.6 5.5 %collective-permute-start.9 = (f32[16,48,128]{2,1,0:T(8,128)S(1)}, f32[16,48,128]{2,1,0:T(8,128)S(1)}, u32[]{:S(2)}, u32[]{:S(2)}) collective-permute-start(f32[16,48,128]{2,1,0:T(8,128)S(1)} %all_to_all.76.own), channel_id=1, source_target_pairs={{0,4},{4,0},{1,5},{5,1},{2,6},{6,2},{3,7},{7,3},{8,12},{12,8},{9,1... | collective-permute-start | bytes 1179656 | tf_op jit(solution)/shard_map/ppermute | solution.py:323

commit v6 on v5

--- a/solution.py
+++ b/solution.py
@@ -17,7 +17,7 @@
 LANES = 128
 DEN_ROWS = 8
 CHUNK = 256
-ROWS = 8
+ROWS = 16
 INNER_MIB = 60
 EDGE_MIB = 53
 TAU = 8.0 / 3.0
@@ -118,12 +118,17 @@
         own, beyond = near[side].astype(jnp.float32), rim[side].astype(jnp.float32)
         pair = (beyond, own) if top else (own, beyond)
         field = jnp.concatenate(pair, axis=0)
-        beside = beside_of(field, sums[...])
+        beside = []
+        for step in range(PASSES):
+            power = sums[:, pl.ds(step * field.shape[-1], field.shape[-1])]
+            part = field[1 + step : 3 * PASSES - 1 - step]
+            flat = part.reshape(-1, part.shape[-1]).astype(jnp.bfloat16)
+            beside.append(jnp.dot(flat, power, preferred_element_type=jnp.float32).reshape(part.shape))
         rows = [field[row] for row in range(3 * PASSES)]
         flag = flags[0] if top else flags[1]
         for step in range(PASSES):
             rows = [
-                TAU * rows[row + 1] + (rows[row] + rows[row + 2]) + beside[step][row + 1 + step]
+                TAU * rows[row + 1] + (rows[row] + rows[row + 2]) + beside[step][row]
                 for row in range(len(rows) - 2)
             ]
             beyond = PASSES - 1 - step

time: 277 us -> 276 us (level)
  no operation moved by 1% of the time
where the time goes in v6:
time: 276 us; the launch traced here: 275 us
  blocking collectives  149 us (54%)
  waiting for transfers between devices  58.5 us (21%)
  starting transfers between devices  38.1 us (14%)
  Pallas kernels  24.9 us (9%)
  local copies, waits for them, and re-layouts  3.5 us (1%)
    all_to_all x8, blocking collectives, to_all(): lax.all_to_all(jnp.broadcast_to(x[None], (count,) + x.shape), axes, 0, 0,...  93.4 us
    all_to_all x4, blocking collectives, summed_block(): plane = jnp.sum(lax.all_to_all(chip, PLANE, 0, 0, tiled=True), axis=0)  55.1 us
    all_to_all x1, waiting for transfers between devices, shards(): lax.all_to_all(smoothed(counts[0]), CHAN, split_axis=0, concat_axis=0, ti...  47.4 us
    ppermute x4, starting transfers between devices, shards(): other = lax.ppermute(own, 'core', [(0, 1), (1, 0)])  16.5 us
    pallas_call x4, Pallas kernels, update(): pl.pallas_call(update_kernel, out_shape=(jax.ShapeDtypeStruct(weights.sha...  14.3 us
    all_to_all x1, starting transfers between devices, shards(): lax.all_to_all(smoothed(counts[0]), CHAN, split_axis=0, concat_axis=0, ti...  12.7 us
    pallas_call x1, Pallas kernels, smoothed(): pl.pallas_call(inner_kernel, out_shape=shape, in_specs=[HBM], out_specs=H...  6.58 us
    ppermute x4, waiting for transfers between devices, summed_block(): chip = kept + lax.ppermute(sent, 'core', [(0, 1), (1, 0)])  5.78 us
  transfers between devices with their start and end apart: 11, of which 9 were waited for; matrix products, arithmetic and copies ran while one was open for 1% of the time, Pallas kernels for 2%

profile of v6, /device:TPU:1, one launch (start us, length us, event | category | flops | bytes accessed | tf_op | source)
XLA Modules:
  0.0 275.4 jit_solution(8085431596957814400)
XLA Ops:
  0.6 1.1 slice_bitcast_fusion
  1.7 4.0 %collective-permute-start = (bf16[3,32,512]{2,1,0:T(8,128)(2,1)S(1)}, bf16[3,32,512]{2,1,0:T(8,128)(2,1)S(1)}, u32[]{:S(2)}, u32[]{:S(2)}) collective-permute-start(bf16[3,32,512]{2,1,0:T(8,128)(2,1)S(1)} %convert_element_type.13), channel_id=1, source_target_pairs={{0,1},{1,2},{2,3},{4,5},{5,6},{6,7},{8,9},{9,10},{10,11},{12,13},{... | collective-permute-start | bytes 294920 | tf_op jit(solution)/shard_map/ppermute | solution.py:153
  5.7 1.3 collective-permute-start.1
  7.0 0.1 add_convert_fusion.flags
  7.1 6.6 %smooth_inner.1.inner = bf16[64,32,512]{2,1,0:T(8,128)(2,1)} custom-call(s32[64,32,512]{2,1,0:T(8,128)} %bitcast.36), custom_call_target="tpu_custom_call" | custom-call | flops 1073741824 | bytes 6291456 | tf_op jit(solution)/shard_map/smooth_inner/pallas_call | solution.py:159
  13.7 0.0 collective-permute-done.before
  13.7 0.0 collective-permute-done.1.after
  13.7 3.0 %smooth_edges.1 = bf16[64,32,512]{2,1,0:T(8,128)(2,1)} custom-call(f32[2]{0:T(128)S(1)} %add_convert_fusion.flags, s32[64,32,512]{2,1,0:T(8,128)} %bitcast.37, bf16[3,32,512]{2,1,0:T(8,128)(2,1)S(1)} %collective-permute-done.before, bf16[3,32,512]{2,1,0:T(8,128)(2,1)S(1)} %collective-permute-done.1.after, ...), custom_call_target="tpu_custom_call", output_to_operand_aliasing={{}: (4, {})} | custom-call | tf_op jit(solution)/shard_map/smooth_edges/pallas_call | solution.py:181
  16.7 0.0 copy-start.1
  16.8 12.7 %all-to-all-start = ((bf16[64,32,512]{2,1,0:T(8,128)(2,1)}), bf16[64,32,512]{2,1,0:T(8,128)(2,1)S(1)}, u32[]{:S(2)}, u32[]{:S(2)}) async-start(bf16[64,32,512]{2,1,0:T(8,128)(2,1)} %smooth_edges.1), calls=%async_computation | async-start | bytes 4194304 | tf_op jit(solution)/shard_map/all_to_all | solution.py:314
  29.5 0.0 copy-done.1
  29.5 0.0 copy-start
  29.5 1.3 copy.13
  30.9 0.6 constant_dynamic-slice_fusion
  31.5 0.1 constant_dynamic-slice_fusion.1
  31.6 0.2 copy_bitcast_fusion
  31.8 47.4 %all-to-all-done = bf16[64,32,512]{2,1,0:T(8,128)(2,1)S(1)} async-done(((bf16[64,32,512]{2,1,0:T(8,128)(2,1)}), bf16[64,32,512]{2,1,0:T(8,128)(2,1)S(1)}, u32[]{:S(2)}, u32[]{:S(2)}) %all-to-all-start) | async-done | bytes 2097184 | tf_op jit(solution)/shard_map/all_to_all | solution.py:314
  79.2 0.0 copy-done
  79.2 3.6 %update.4 = (f32[128,512]{1,0:T(8,128)S(1)}, f32[16,56,128]{2,1,0:T(8,128)S(1)}, f32[16,56,128]{2,1,0:T(8,128)S(1)}) custom-call(s32[1]{0:T(128)} %bitcast.core, bf16[2048,512]{1,0:T(8,128)(2,1)S(1)} %bitcast.31, bf16[32,2048]{1,0:T(8,128)(2,1)S(1)} %convert_element_type.15.template, f32[16,48,128]{2,1,0:T(8,128)S(1)} %get-tuple-element.22.own, ...), custom_call_target="tpu_custom_call" | custom-call | tf_op jit(solution)/shard_map/update/pallas_call | solution.py:281
  82.8 0.0 copy-start.2
  82.8 2.2 collective-permute-start.2
  85.0 1.4 collective-permute-done.2
  86.4 0.1 add.33
  86.5 17.4 %all_to_all.65 = f32[16,56,128]{2,1,0:T(8,128)S(1)} all-to-all(f32[16,56,128]{2,1,0:T(8,128)S(1)} %add.33), channel_id=1, replica_groups=mesh['z'=8,'y'=4,'core'=2,'row'=4] {'y','row'}, dimensions={0} | all-to-all | bytes 917504 | tf_op jit(solution)/shard_map/all_to_all | solution.py:209
  104.0 11.3 %all_to_all.66 = f32[8,56,128]{2,1,0:T(8,128)S(1)} all-to-all(f32[8,56,128]{2,1,0:T(8,128)S(1)} %broadcast_in_dim.21), channel_id=1, replica_groups=mesh['z'=8,'y'=4,'core'=2,'row'=4] {'z'}, dimensions={0} | all-to-all | bytes 458752 | tf_op jit(solution)/shard_map/all_to_all | solution.py:204
  115.3 0.0 copy-done.2
  115.3 0.1 fusion.3
  115.5 12.1 %all_to_all.67.own = f32[16,48,128]{2,1,0:T(8,128)S(1)} all-to-all(f32[16,48,128]{2,1,0:T(8,128)S(1)} %broadcast_in_dim.22), channel_id=1, replica_groups=mesh['z'=8,'y'=4,'core'=2,'row'=4] {'y','row'}, dimensions={0} | all-to-all | bytes 786432 | tf_op jit(solution)/shard_map/all_to_all | solution.py:204
  127.5 4.1 %collective-permute-start.3 = (f32[16,48,128]{2,1,0:T(8,128)S(1)}, f32[16,48,128]{2,1,0:T(8,128)S(1)}, u32[]{:S(2)}, u32[]{:S(2)}) collective-permute-start(f32[16,48,128]{2,1,0:T(8,128)S(1)} %all_to_all.67.own), channel_id=1, source_target_pairs={{0,4},{4,0},{1,5},{5,1},{2,6},{6,2},{3,7},{7,3},{8,12},{12,8},{9,1... | collective-permute-start | bytes 1179656 | tf_op jit(solution)/shard_map/ppermute | solution.py:328
  131.7 1.3 collective-permute-done.3.other
  133.0 3.6 %update.5 = (f32[128,512]{1,0:T(8,128)S(1)}, f32[16,56,128]{2,1,0:T(8,128)S(1)}, f32[16,56,128]{2,1,0:T(8,128)S(1)}) custom-call(s32[1]{0:T(128)} %bitcast.core, bf16[2048,512]{1,0:T(8,128)(2,1)S(1)} %bitcast.32, bf16[32,2048]{1,0:T(8,128)(2,1)S(1)} %convert_element_type.15.template, f32[16,48,128]{2,1,0:T(8,128)S(1)} %all_to_all.67.own, ...), custom_call_target="tpu_custom_call" | custom-call | tf_op jit(solution)/shard_map/update/pallas_call | solution.py:281
  136.6 0.5 collective-permute-start.4
  137.1 1.4 collective-permute-done.4
  138.6 12.5 %all_to_all.68 = f32[16,56,128]{2,1,0:T(8,128)S(1)} all-to-all(f32[16,56,128]{2,1,0:T(8,128)S(1)} %add.34), channel_id=1, replica_groups=mesh['z'=8,'y'=4,'core'=2,'row'=4] {'y','row'}, dimensions={0} | all-to-all | bytes 917504 | tf_op jit(solution)/shard_map/all_to_all | solution.py:209
  151.2 11.3 %all_to_all.69 = f32[8,56,128]{2,1,0:T(8,128)S(1)} all-to-all(f32[8,56,128]{2,1,0:T(8,128)S(1)} %broadcast_in_dim.23), channel_id=1, replica_groups=mesh['z'=8,'y'=4,'core'=2,'row'=4] {'z'}, dimensions={0} | all-to-all | bytes 458752 | tf_op jit(solution)/shard_map/all_to_all | solution.py:204
  162.5 0.1 fusion.2
  162.6 12.1 %all_to_all.70.own = f32[16,48,128]{2,1,0:T(8,128)S(1)} all-to-all(f32[16,48,128]{2,1,0:T(8,128)S(1)} %broadcast_in_dim.24), channel_id=1, replica_groups=mesh['z'=8,'y'=4,'core'=2,'row'=4] {'y','row'}, dimensions={0} | all-to-all | bytes 786432 | tf_op jit(solution)/shard_map/all_to_all | solution.py:204
  174.7 4.1 %collective-permute-start.5 = (f32[16,48,128]{2,1,0:T(8,128)S(1)}, f32[16,48,128]{2,1,0:T(8,128)S(1)}, u32[]{:S(2)}, u32[]{:S(2)}) collective-permute-start(f32[16,48,128]{2,1,0:T(8,128)S(1)} %all_to_all.70.own), channel_id=1, source_target_pairs={{0,4},{4,0},{1,5},{5,1},{2,6},{6,2},{3,7},{7,3},{8,12},{12,8},{9,1... | collective-permute-start | bytes 1179656 | tf_op jit(solution)/shard_map/ppermute | solution.py:328
  178.8 1.3 collective-permute-done.5.other
  180.2 3.6 %update.6 = (f32[128,512]{1,0:T(8,128)S(1)}, f32[16,56,128]{2,1,0:T(8,128)S(1)}, f32[16,56,128]{2,1,0:T(8,128)S(1)}) custom-call(s32[1]{0:T(128)} %bitcast.core, bf16[2048,512]{1,0:T(8,128)(2,1)S(1)} %bitcast.33, bf16[32,2048]{1,0:T(8,128)(2,1)S(1)} %convert_element_type.15.template, f32[16,48,128]{2,1,0:T(8,128)S(1)} %all_to_all.70.own, ...), custom_call_target="tpu_custom_call" | custom-call | tf_op jit(solution)/shard_map/update/pallas_call | solution.py:281
  183.8 0.5 collective-permute-start.6
  184.2 1.4 collective-permute-done.6
  185.7 12.6 %all_to_all.71 = f32[16,56,128]{2,1,0:T(8,128)S(1)} all-to-all(f32[16,56,128]{2,1,0:T(8,128)S(1)} %add.35), channel_id=1, replica_groups=mesh['z'=8,'y'=4,'core'=2,'row'=4] {'y','row'}, dimensions={0} | all-to-all | bytes 917504 | tf_op jit(solution)/shard_map/all_to_all | solution.py:209
  198.4 11.3 %all_to_all.72 = f32[8,56,128]{2,1,0:T(8,128)S(1)} all-to-all(f32[8,56,128]{2,1,0:T(8,128)S(1)} %broadcast_in_dim.25), channel_id=1, replica_groups=mesh['z'=8,'y'=4,'core'=2,'row'=4] {'z'}, dimensions={0} | all-to-all | bytes 458752 | tf_op jit(solution)/shard_map/all_to_all | solution.py:204
  209.7 0.1 fusion.1
  209.8 12.1 %all_to_all.73.own = f32[16,48,128]{2,1,0:T(8,128)S(1)} all-to-all(f32[16,48,128]{2,1,0:T(8,128)S(1)} %broadcast_in_dim.26), channel_id=1, replica_groups=mesh['z'=8,'y'=4,'core'=2,'row'=4] {'y','row'}, dimensions={0} | all-to-all | bytes 786432 | tf_op jit(solution)/shard_map/all_to_all | solution.py:204
  221.9 4.1 %collective-permute-start.7 = (f32[16,48,128]{2,1,0:T(8,128)S(1)}, f32[16,48,128]{2,1,0:T(8,128)S(1)}, u32[]{:S(2)}, u32[]{:S(2)}) collective-permute-start(f32[16,48,128]{2,1,0:T(8,128)S(1)} %all_to_all.73.own), channel_id=1, source_target_pairs={{0,4},{4,0},{1,5},{5,1},{2,6},{6,2},{3,7},{7,3},{8,12},{12,8},{9,1... | collective-permute-start | bytes 1179656 | tf_op jit(solution)/shard_map/ppermute | solution.py:328
  226.0 1.3 collective-permute-done.7.other
  227.3 3.6 %update.7 = (f32[128,512]{1,0:T(8,128)}, f32[16,56,128]{2,1,0:T(8,128)S(1)}, f32[16,56,128]{2,1,0:T(8,128)S(1)}) custom-call(s32[1]{0:T(128)} %bitcast.core, bf16[2048,512]{1,0:T(8,128)(2,1)S(1)} %bitcast.34, bf16[32,2048]{1,0:T(8,128)(2,1)S(1)} %convert_element_type.15.template, f32[16,48,128]{2,1,0:T(8,128)S(1)} %all_to_all.73.own, ...), custom_call_target="tpu_custom_call" | custom-call | tf_op jit(solution)/shard_map/update/pallas_call | solution.py:281
  230.9 0.5 collective-permute-start.8
  231.4 1.4 collective-permute-done.8
  232.9 12.5 %all_to_all.74 = f32[16,56,128]{2,1,0:T(8,128)S(1)} all-to-all(f32[16,56,128]{2,1,0:T(8,128)S(1)} %add.36), channel_id=1, replica_groups=mesh['z'=8,'y'=4,'core'=2,'row'=4] {'y','row'}, dimensions={0} | all-to-all | bytes 917504 | tf_op jit(solution)/shard_map/all_to_all | solution.py:209
  245.5 11.3 %all_to_all.75 = f32[8,56,128]{2,1,0:T(8,128)S(1)} all-to-all(f32[8,56,128]{2,1,0:T(8,128)S(1)} %broadcast_in_dim.28), channel_id=1, replica_groups=mesh['z'=8,'y'=4,'core'=2,'row'=4] {'z'}, dimensions={0} | all-to-all | bytes 458752 | tf_op jit(solution)/shard_map/all_to_all | solution.py:204
  256.8 0.1 fusion
  256.9 12.1 %all_to_all.76.own = f32[16,48,128]{2,1,0:T(8,128)S(1)} all-to-all(f32[16,48,128]{2,1,0:T(8,128)S(1)} %broadcast_in_dim.29), channel_id=1, replica_groups=mesh['z'=8,'y'=4,'core'=2,'row'=4] {'y','row'}, dimensions={0} | all-to-all | bytes 786432 | tf_op jit(solution)/shard_map/all_to_all | solution.py:204
  269.0 4.1 %collective-permute-start.9 = (f32[16,48,128]{2,1,0:T(8,128)S(1)}, f32[16,48,128]{2,1,0:T(8,128)S(1)}, u32[]{:S(2)}, u32[]{:S(2)}) collective-permute-start(f32[16,48,128]{2,1,0:T(8,128)S(1)} %all_to_all.76.own), channel_id=1, source_target_pairs={{0,4},{4,0},{1,5},{5,1},{2,6},{6,2},{3,7},{7,3},{8,12},{12,8},{9,1... | collective-permute-start | bytes 1179656 | tf_op jit(solution)/shard_map/ppermute | solution.py:328
  273.1 1.3 collective-permute-done.9.other
  274.5 0.9 whole.1
  (26 shorter events, 0.6 us)
Async XLA Ops:
  1.7 12.0 %collective-permute-start = (bf16[3,32,512]{2,1,0:T(8,128)(2,1)S(1)}, bf16[3,32,512]{2,1,0:T(8,128)(2,1)S(1)}, u32[]{:S(2)}, u32[]{:S(2)}) collective-permute-start(bf16[3,32,512]{2,1,0:T(8,128)(2,1)S(1)} %convert_element_type.13), channel_id=1, source_target_pairs={{0,1},{1,2},{2,3},{4,5},{5,6},{6,7},{8,9},{9,10},{10,11},{12,13},{... | collective-permute-start | bytes 294920 | tf_op jit(solution)/shard_map/ppermute | solution.py:153
  5.7 8.0 %collective-permute-start.1 = (bf16[3,32,512]{2,1,0:T(8,128)(2,1)S(1)}, bf16[3,32,512]{2,1,0:T(8,128)(2,1)S(1)}, u32[]{:S(2)}, u32[]{:S(2)}) collective-permute-start(bf16[3,32,512]{2,1,0:T(8,128)(2,1)S(1)} %convert_element_type.14), channel_id=1, source_target_pairs={{1,0},{2,1},{3,2},{5,4},{6,5},{7,6},{9,8},{10,9},{11,10},{13,12},{... | collective-permute-start | bytes 294920 | tf_op jit(solution)/shard_map/ppermute | solution.py:154
  16.7 12.8 %copy-start.1 = (s32[32,2048]{1,0:T(8,128)S(1)}, s32[32,2048]{1,0:T(8,128)}, u32[]{:S(2)}) copy-start(s32[32,2048]{1,0:T(8,128)} %param.5) | copy-start | bytes 786436
  16.8 62.4 %all-to-all-start = ((bf16[64,32,512]{2,1,0:T(8,128)(2,1)}), bf16[64,32,512]{2,1,0:T(8,128)(2,1)S(1)}, u32[]{:S(2)}, u32[]{:S(2)}) async-start(bf16[64,32,512]{2,1,0:T(8,128)(2,1)} %smooth_edges.1), calls=%async_computation | async-start | bytes 4194304 | tf_op jit(solution)/shard_map/all_to_all | solution.py:314
  29.5 49.6 %copy-start = (f32[1,1,128,512]{3,2,1,0:T(8,128)S(1)}, f32[1,1,128,512]{3,2,1,0:T(8,128)}, u32[]{:S(2)}) copy-start(f32[1,1,128,512]{3,2,1,0:T(8,128)} %param.6) | copy-start | bytes 786436
  82.8 32.6 %copy-start.2 = (f32[1,48,1,128]{3,2,1,0:T(1,128)S(1)}, f32[1,48,1,128]{3,2,1,0:T(1,128)}, u32[]{:S(2)}) copy-start(f32[1,48,1,128]{3,2,1,0:T(1,128)} %constant_dynamic-slice_fusion) | copy-start | bytes 73732
  82.8 3.7 %collective-permute-start.2 = (f32[16,56,128]{2,1,0:T(8,128)S(1)}, f32[16,56,128]{2,1,0:T(8,128)S(1)}, u32[]{:S(2)}, u32[]{:S(2)}) collective-permute-start(f32[16,56,128]{2,1,0:T(8,128)S(1)} %get-tuple-element.25), channel_id=1, source_target_pairs={{0,4},{4,0},{1,5},{5,1},{2,6},{6,2},{3,7},{7,3},{8,12},{12,8},{9,1... | collective-permute-start | bytes 1376264 | tf_op jit(solution)/shard_map/ppermute | solution.py:208
  127.5 5.5 %collective-permute-start.3 = (f32[16,48,128]{2,1,0:T(8,128)S(1)}, f32[16,48,128]{2,1,0:T(8,128)S(1)}, u32[]{:S(2)}, u32[]{:S(2)}) collective-permute-start(f32[16,48,128]{2,1,0:T(8,128)S(1)} %all_to_all.67.own), channel_id=1, source_target_pairs={{0,4},{4,0},{1,5},{5,1},{2,6},{6,2},{3,7},{7,3},{8,12},{12,8},{9,1... | collective-permute-start | bytes 1179656 | tf_op jit(solution)/shard_map/ppermute | solution.py:328
  136.6 1.9 collective-permute-start.4
  174.7 5.5 %collective-permute-start.5 = (f32[16,48,128]{2,1,0:T(8,128)S(1)}, f32[16,48,128]{2,1,0:T(8,128)S(1)}, u32[]{:S(2)}, u32[]{:S(2)}) collective-permute-start(f32[16,48,128]{2,1,0:T(8,128)S(1)} %all_to_all.70.own), channel_id=1, source_target_pairs={{0,4},{4,0},{1,5},{5,1},{2,6},{6,2},{3,7},{7,3},{8,12},{12,8},{9,1... | collective-permute-start | bytes 1179656 | tf_op jit(solution)/shard_map/ppermute | solution.py:328
  183.8 1.9 collective-permute-start.6
  221.9 5.5 %collective-permute-start.7 = (f32[16,48,128]{2,1,0:T(8,128)S(1)}, f32[16,48,128]{2,1,0:T(8,128)S(1)}, u32[]{:S(2)}, u32[]{:S(2)}) collective-permute-start(f32[16,48,128]{2,1,0:T(8,128)S(1)} %all_to_all.73.own), channel_id=1, source_target_pairs={{0,4},{4,0},{1,5},{5,1},{2,6},{6,2},{3,7},{7,3},{8,12},{12,8},{9,1... | collective-permute-start | bytes 1179656 | tf_op jit(solution)/shard_map/ppermute | solution.py:328
  230.9 1.9 collective-permute-start.8
  269.0 5.5 %collective-permute-start.9 = (f32[16,48,128]{2,1,0:T(8,128)S(1)}, f32[16,48,128]{2,1,0:T(8,128)S(1)}, u32[]{:S(2)}, u32[]{:S(2)}) collective-permute-start(f32[16,48,128]{2,1,0:T(8,128)S(1)} %all_to_all.76.own), channel_id=1, source_target_pairs={{0,4},{4,0},{1,5},{5,1},{2,6},{6,2},{3,7},{7,3},{8,12},{12,8},{9,1... | collective-permute-start | bytes 1179656 | tf_op jit(solution)/shard_map/ppermute | solution.py:328

commit v7 on v5

--- a/solution.py
+++ b/solution.py
@@ -16,7 +16,7 @@
 HALF = FREE // CORES
 LANES = 128
 DEN_ROWS = 8
-CHUNK = 256
+CHUNK = 512
 ROWS = 8
 INNER_MIB = 60
 EDGE_MIB = 53

time: 277 us -> 274 us (0.989)
  no operation moved by 1% of the time
where the time goes in v7:
time: 274 us; the launch traced here: 273 us
  blocking collectives  149 us (54%)
  waiting for transfers between devices  58.5 us (21%)
  starting transfers between devices  38.1 us (14%)
  Pallas kernels  22.8 us (8%)
  local copies, waits for them, and re-layouts  3.5 us (1%)
    all_to_all x8, blocking collectives, to_all(): lax.all_to_all(jnp.broadcast_to(x[None], (count,) + x.shape), axes, 0, 0,...  93.5 us
    all_to_all x4, blocking collectives, summed_block(): plane = jnp.sum(lax.all_to_all(chip, PLANE, 0, 0, tiled=True), axis=0)  55.1 us
    all_to_all x1, waiting for transfers between devices, shards(): lax.all_to_all(smoothed(counts[0]), CHAN, split_axis=0, concat_axis=0, ti...  47.4 us
    ppermute x4, starting transfers between devices, shards(): other = lax.ppermute(own, 'core', [(0, 1), (1, 0)])  16.5 us
    all_to_all x1, starting transfers between devices, shards(): lax.all_to_all(smoothed(counts[0]), CHAN, split_axis=0, concat_axis=0, ti...  12.7 us
    pallas_call x4, Pallas kernels, update(): pl.pallas_call(update_kernel, out_shape=(jax.ShapeDtypeStruct(weights.sha...  11.6 us
    pallas_call x1, Pallas kernels, smoothed(): pl.pallas_call(inner_kernel, out_shape=shape, in_specs=[HBM], out_specs=H...  6.79 us
    ppermute x4, waiting for transfers between devices, summed_block(): chip = kept + lax.ppermute(sent, 'core', [(0, 1), (1, 0)])  5.78 us
  transfers between devices with their start and end apart: 11, of which 9 were waited for; matrix products, arithmetic and copies ran while one was open for 1% of the time, Pallas kernels for 2%

profile of v7, /device:TPU:1, one launch (start us, length us, event | category | flops | bytes accessed | tf_op | source)
XLA Modules:
  0.0 273.3 jit_solution(1919614474082097513)
XLA Ops:
  0.6 1.1 slice_bitcast_fusion
  1.7 4.0 %collective-permute-start = (bf16[3,32,512]{2,1,0:T(8,128)(2,1)S(1)}, bf16[3,32,512]{2,1,0:T(8,128)(2,1)S(1)}, u32[]{:S(2)}, u32[]{:S(2)}) collective-permute-start(bf16[3,32,512]{2,1,0:T(8,128)(2,1)S(1)} %convert_element_type.13), channel_id=1, source_target_pairs={{0,1},{1,2},{2,3},{4,5},{5,6},{6,7},{8,9},{9,10},{10,11},{12,13},{... | collective-permute-start | bytes 294920 | tf_op jit(solution)/shard_map/ppermute | solution.py:148
  5.7 1.3 collective-permute-start.1
  7.0 0.1 add_convert_fusion.flags
  7.1 6.8 %smooth_inner.1.inner = bf16[64,32,512]{2,1,0:T(8,128)(2,1)} custom-call(s32[64,32,512]{2,1,0:T(8,128)} %bitcast.36), custom_call_target="tpu_custom_call" | custom-call | flops 1073741824 | bytes 6291456 | tf_op jit(solution)/shard_map/smooth_inner/pallas_call | solution.py:154
  13.9 0.0 collective-permute-done.before
  13.9 0.0 collective-permute-done.1.after
  13.9 3.4 %smooth_edges.1 = bf16[64,32,512]{2,1,0:T(8,128)(2,1)} custom-call(f32[2]{0:T(128)S(1)} %add_convert_fusion.flags, s32[64,32,512]{2,1,0:T(8,128)} %bitcast.37, bf16[3,32,512]{2,1,0:T(8,128)(2,1)S(1)} %collective-permute-done.before, bf16[3,32,512]{2,1,0:T(8,128)(2,1)S(1)} %collective-permute-done.1.after, ...), custom_call_target="tpu_custom_call", output_to_operand_aliasing={{}: (4, {})} | custom-call | tf_op jit(solution)/shard_map/smooth_edges/pallas_call | solution.py:176
  17.3 0.0 copy-start.1
  17.4 12.7 %all-to-all-start = ((bf16[64,32,512]{2,1,0:T(8,128)(2,1)}), bf16[64,32,512]{2,1,0:T(8,128)(2,1)S(1)}, u32[]{:S(2)}, u32[]{:S(2)}) async-start(bf16[64,32,512]{2,1,0:T(8,128)(2,1)} %smooth_edges.1), calls=%async_computation | async-start | bytes 4194304 | tf_op jit(solution)/shard_map/all_to_all | solution.py:309
  30.1 0.0 copy-done.1
  30.2 0.0 copy-start
  30.2 1.3 copy.13
  31.5 0.6 constant_dynamic-slice_fusion
  32.1 0.1 constant_dynamic-slice_fusion.1
  32.2 0.2 copy_bitcast_fusion
  32.4 47.4 %all-to-all-done = bf16[64,32,512]{2,1,0:T(8,128)(2,1)S(1)} async-done(((bf16[64,32,512]{2,1,0:T(8,128)(2,1)}), bf16[64,32,512]{2,1,0:T(8,128)(2,1)S(1)}, u32[]{:S(2)}, u32[]{:S(2)}) %all-to-all-start) | async-done | bytes 2097184 | tf_op jit(solution)/shard_map/all_to_all | solution.py:309
  79.8 0.0 copy-done
  79.8 2.9 %update.4 = (f32[128,512]{1,0:T(8,128)S(1)}, f32[16,56,128]{2,1,0:T(8,128)S(1)}, f32[16,56,128]{2,1,0:T(8,128)S(1)}) custom-call(s32[1]{0:T(128)} %bitcast.core, bf16[2048,512]{1,0:T(8,128)(2,1)S(1)} %bitcast.31, bf16[32,2048]{1,0:T(8,128)(2,1)S(1)} %convert_element_type.15.template, f32[16,48,128]{2,1,0:T(8,128)S(1)} %get-tuple-element.22.own, ...), custom_call_target="tpu_custom_call" | custom-call | tf_op jit(solution)/shard_map/update/pallas_call | solution.py:276
  82.7 0.0 copy-start.2
  82.7 2.2 collective-permute-start.2
  85.0 1.4 collective-permute-done.2
  86.4 0.1 add.33
  86.5 17.4 %all_to_all.65 = f32[16,56,128]{2,1,0:T(8,128)S(1)} all-to-all(f32[16,56,128]{2,1,0:T(8,128)S(1)} %add.33), channel_id=1, replica_groups=mesh['z'=8,'y'=4,'core'=2,'row'=4] {'y','row'}, dimensions={0} | all-to-all | bytes 917504 | tf_op jit(solution)/shard_map/all_to_all | solution.py:204
  104.0 11.3 %all_to_all.66 = f32[8,56,128]{2,1,0:T(8,128)S(1)} all-to-all(f32[8,56,128]{2,1,0:T(8,128)S(1)} %broadcast_in_dim.21), channel_id=1, replica_groups=mesh['z'=8,'y'=4,'core'=2,'row'=4] {'z'}, dimensions={0} | all-to-all | bytes 458752 | tf_op jit(solution)/shard_map/all_to_all | solution.py:199
  115.3 0.0 copy-done.2
  115.3 0.1 fusion.3
  115.4 12.1 %all_to_all.67.own = f32[16,48,128]{2,1,0:T(8,128)S(1)} all-to-all(f32[16,48,128]{2,1,0:T(8,128)S(1)} %broadcast_in_dim.22), channel_id=1, replica_groups=mesh['z'=8,'y'=4,'core'=2,'row'=4] {'y','row'}, dimensions={0} | all-to-all | bytes 786432 | tf_op jit(solution)/shard_map/all_to_all | solution.py:199
  127.5 4.1 %collective-permute-start.3 = (f32[16,48,128]{2,1,0:T(8,128)S(1)}, f32[16,48,128]{2,1,0:T(8,128)S(1)}, u32[]{:S(2)}, u32[]{:S(2)}) collective-permute-start(f32[16,48,128]{2,1,0:T(8,128)S(1)} %all_to_all.67.own), channel_id=1, source_target_pairs={{0,4},{4,0},{1,5},{5,1},{2,6},{6,2},{3,7},{7,3},{8,12},{12,8},{9,1... | collective-permute-start | bytes 1179656 | tf_op jit(solution)/shard_map/ppermute | solution.py:323
  131.6 1.3 collective-permute-done.3.other
  133.0 2.9 %update.5 = (f32[128,512]{1,0:T(8,128)S(1)}, f32[16,56,128]{2,1,0:T(8,128)S(1)}, f32[16,56,128]{2,1,0:T(8,128)S(1)}) custom-call(s32[1]{0:T(128)} %bitcast.core, bf16[2048,512]{1,0:T(8,128)(2,1)S(1)} %bitcast.32, bf16[32,2048]{1,0:T(8,128)(2,1)S(1)} %convert_element_type.15.template, f32[16,48,128]{2,1,0:T(8,128)S(1)} %all_to_all.67.own, ...), custom_call_target="tpu_custom_call" | custom-call | tf_op jit(solution)/shard_map/update/pallas_call | solution.py:276
  135.9 0.5 collective-permute-start.4
  136.3 1.4 collective-permute-done.4
  137.8 12.6 %all_to_all.68 = f32[16,56,128]{2,1,0:T(8,128)S(1)} all-to-all(f32[16,56,128]{2,1,0:T(8,128)S(1)} %add.34), channel_id=1, replica_groups=mesh['z'=8,'y'=4,'core'=2,'row'=4] {'y','row'}, dimensions={0} | all-to-all | bytes 917504 | tf_op jit(solution)/shard_map/all_to_all | solution.py:204
  150.4 11.3 %all_to_all.69 = f32[8,56,128]{2,1,0:T(8,128)S(1)} all-to-all(f32[8,56,128]{2,1,0:T(8,128)S(1)} %broadcast_in_dim.23), channel_id=1, replica_groups=mesh['z'=8,'y'=4,'core'=2,'row'=4] {'z'}, dimensions={0} | all-to-all | bytes 458752 | tf_op jit(solution)/shard_map/all_to_all | solution.py:199
  161.8 0.1 fusion.2
  161.9 12.1 %all_to_all.70.own = f32[16,48,128]{2,1,0:T(8,128)S(1)} all-to-all(f32[16,48,128]{2,1,0:T(8,128)S(1)} %broadcast_in_dim.24), channel_id=1, replica_groups=mesh['z'=8,'y'=4,'core'=2,'row'=4] {'y','row'}, dimensions={0} | all-to-all | bytes 786432 | tf_op jit(solution)/shard_map/all_to_all | solution.py:199
  173.9 4.1 %collective-permute-start.5 = (f32[16,48,128]{2,1,0:T(8,128)S(1)}, f32[16,48,128]{2,1,0:T(8,128)S(1)}, u32[]{:S(2)}, u32[]{:S(2)}) collective-permute-start(f32[16,48,128]{2,1,0:T(8,128)S(1)} %all_to_all.70.own), channel_id=1, source_target_pairs={{0,4},{4,0},{1,5},{5,1},{2,6},{6,2},{3,7},{7,3},{8,12},{12,8},{9,1... | collective-permute-start | bytes 1179656 | tf_op jit(solution)/shard_map/ppermute | solution.py:323
  178.1 1.3 collective-permute-done.5.other
  179.4 2.9 %update.6 = (f32[128,512]{1,0:T(8,128)S(1)}, f32[16,56,128]{2,1,0:T(8,128)S(1)}, f32[16,56,128]{2,1,0:T(8,128)S(1)}) custom-call(s32[1]{0:T(128)} %bitcast.core, bf16[2048,512]{1,0:T(8,128)(2,1)S(1)} %bitcast.33, bf16[32,2048]{1,0:T(8,128)(2,1)S(1)} %convert_element_type.15.template, f32[16,48,128]{2,1,0:T(8,128)S(1)} %all_to_all.70.own, ...), custom_call_target="tpu_custom_call" | custom-call | tf_op jit(solution)/shard_map/update/pallas_call | solution.py:276
  182.3 0.5 collective-permute-start.6
  182.8 1.4 collective-permute-done.6
  184.3 12.5 %all_to_all.71 = f32[16,56,128]{2,1,0:T(8,128)S(1)} all-to-all(f32[16,56,128]{2,1,0:T(8,128)S(1)} %add.35), channel_id=1, replica_groups=mesh['z'=8,'y'=4,'core'=2,'row'=4] {'y','row'}, dimensions={0} | all-to-all | bytes 917504 | tf_op jit(solution)/shard_map/all_to_all | solution.py:204
  196.9 11.3 %all_to_all.72 = f32[8,56,128]{2,1,0:T(8,128)S(1)} all-to-all(f32[8,56,128]{2,1,0:T(8,128)S(1)} %broadcast_in_dim.25), channel_id=1, replica_groups=mesh['z'=8,'y'=4,'core'=2,'row'=4] {'z'}, dimensions={0} | all-to-all | bytes 458752 | tf_op jit(solution)/shard_map/all_to_all | solution.py:199
  208.2 0.1 fusion.1
  208.3 12.1 %all_to_all.73.own = f32[16,48,128]{2,1,0:T(8,128)S(1)} all-to-all(f32[16,48,128]{2,1,0:T(8,128)S(1)} %broadcast_in_dim.26), channel_id=1, replica_groups=mesh['z'=8,'y'=4,'core'=2,'row'=4] {'y','row'}, dimensions={0} | all-to-all | bytes 786432 | tf_op jit(solution)/shard_map/all_to_all | solution.py:199
  220.4 4.1 %collective-permute-start.7 = (f32[16,48,128]{2,1,0:T(8,128)S(1)}, f32[16,48,128]{2,1,0:T(8,128)S(1)}, u32[]{:S(2)}, u32[]{:S(2)}) collective-permute-start(f32[16,48,128]{2,1,0:T(8,128)S(1)} %all_to_all.73.own), channel_id=1, source_target_pairs={{0,4},{4,0},{1,5},{5,1},{2,6},{6,2},{3,7},{7,3},{8,12},{12,8},{9,1... | collective-permute-start | bytes 1179656 | tf_op jit(solution)/shard_map/ppermute | solution.py:323
  224.5 1.3 collective-permute-done.7.other
  225.9 2.9 %update.7 = (f32[128,512]{1,0:T(8,128)}, f32[16,56,128]{2,1,0:T(8,128)S(1)}, f32[16,56,128]{2,1,0:T(8,128)S(1)}) custom-call(s32[1]{0:T(128)} %bitcast.core, bf16[2048,512]{1,0:T(8,128)(2,1)S(1)} %bitcast.34, bf16[32,2048]{1,0:T(8,128)(2,1)S(1)} %convert_element_type.15.template, f32[16,48,128]{2,1,0:T(8,128)S(1)} %all_to_all.73.own, ...), custom_call_target="tpu_custom_call" | custom-call | tf_op jit(solution)/shard_map/update/pallas_call | solution.py:276
  228.8 0.5 collective-permute-start.8
  229.3 1.4 collective-permute-done.8
  230.8 12.6 %all_to_all.74 = f32[16,56,128]{2,1,0:T(8,128)S(1)} all-to-all(f32[16,56,128]{2,1,0:T(8,128)S(1)} %add.36), channel_id=1, replica_groups=mesh['z'=8,'y'=4,'core'=2,'row'=4] {'y','row'}, dimensions={0} | all-to-all | bytes 917504 | tf_op jit(solution)/shard_map/all_to_all | solution.py:204
  243.4 11.3 %all_to_all.75 = f32[8,56,128]{2,1,0:T(8,128)S(1)} all-to-all(f32[8,56,128]{2,1,0:T(8,128)S(1)} %broadcast_in_dim.28), channel_id=1, replica_groups=mesh['z'=8,'y'=4,'core'=2,'row'=4] {'z'}, dimensions={0} | all-to-all | bytes 458752 | tf_op jit(solution)/shard_map/all_to_all | solution.py:199
  254.7 0.1 fusion
  254.8 12.1 %all_to_all.76.own = f32[16,48,128]{2,1,0:T(8,128)S(1)} all-to-all(f32[16,48,128]{2,1,0:T(8,128)S(1)} %broadcast_in_dim.29), channel_id=1, replica_groups=mesh['z'=8,'y'=4,'core'=2,'row'=4] {'y','row'}, dimensions={0} | all-to-all | bytes 786432 | tf_op jit(solution)/shard_map/all_to_all | solution.py:199
  266.9 4.1 %collective-permute-start.9 = (f32[16,48,128]{2,1,0:T(8,128)S(1)}, f32[16,48,128]{2,1,0:T(8,128)S(1)}, u32[]{:S(2)}, u32[]{:S(2)}) collective-permute-start(f32[16,48,128]{2,1,0:T(8,128)S(1)} %all_to_all.76.own), channel_id=1, source_target_pairs={{0,4},{4,0},{1,5},{5,1},{2,6},{6,2},{3,7},{7,3},{8,12},{12,8},{9,1... | collective-permute-start | bytes 1179656 | tf_op jit(solution)/shard_map/ppermute | solution.py:323
  271.0 1.3 collective-permute-done.9.other
  272.4 0.9 whole.1
  (26 shorter events, 0.6 us)
Async XLA Ops:
  1.7 12.2 %collective-permute-start = (bf16[3,32,512]{2,1,0:T(8,128)(2,1)S(1)}, bf16[3,32,512]{2,1,0:T(8,128)(2,1)S(1)}, u32[]{:S(2)}, u32[]{:S(2)}) collective-permute-start(bf16[3,32,512]{2,1,0:T(8,128)(2,1)S(1)} %convert_element_type.13), channel_id=1, source_target_pairs={{0,1},{1,2},{2,3},{4,5},{5,6},{6,7},{8,9},{9,10},{10,11},{12,13},{... | collective-permute-start | bytes 294920 | tf_op jit(solution)/shard_map/ppermute | solution.py:148
  5.7 8.2 %collective-permute-start.1 = (bf16[3,32,512]{2,1,0:T(8,128)(2,1)S(1)}, bf16[3,32,512]{2,1,0:T(8,128)(2,1)S(1)}, u32[]{:S(2)}, u32[]{:S(2)}) collective-permute-start(bf16[3,32,512]{2,1,0:T(8,128)(2,1)S(1)} %convert_element_type.14), channel_id=1, source_target_pairs={{1,0},{2,1},{3,2},{5,4},{6,5},{7,6},{9,8},{10,9},{11,10},{13,12},{... | collective-permute-start | bytes 294920 | tf_op jit(solution)/shard_map/ppermute | solution.py:149
  17.3 12.8 %copy-start.1 = (s32[32,2048]{1,0:T(8,128)S(1)}, s32[32,2048]{1,0:T(8,128)}, u32[]{:S(2)}) copy-start(s32[32,2048]{1,0:T(8,128)} %param.5) | copy-start | bytes 786436
  17.4 62.4 %all-to-all-start = ((bf16[64,32,512]{2,1,0:T(8,128)(2,1)}), bf16[64,32,512]{2,1,0:T(8,128)(2,1)S(1)}, u32[]{:S(2)}, u32[]{:S(2)}) async-start(bf16[64,32,512]{2,1,0:T(8,128)(2,1)} %smooth_edges.1), calls=%async_computation | async-start | bytes 4194304 | tf_op jit(solution)/shard_map/all_to_all | solution.py:309
  30.2 49.6 %copy-start = (f32[1,1,128,512]{3,2,1,0:T(8,128)S(1)}, f32[1,1,128,512]{3,2,1,0:T(8,128)}, u32[]{:S(2)}) copy-start(f32[1,1,128,512]{3,2,1,0:T(8,128)} %param.6) | copy-start | bytes 786436
  82.7 32.6 %copy-start.2 = (f32[1,48,1,128]{3,2,1,0:T(1,128)S(1)}, f32[1,48,1,128]{3,2,1,0:T(1,128)}, u32[]{:S(2)}) copy-start(f32[1,48,1,128]{3,2,1,0:T(1,128)} %constant_dynamic-slice_fusion) | copy-start | bytes 73732
  82.7 3.7 %collective-permute-start.2 = (f32[16,56,128]{2,1,0:T(8,128)S(1)}, f32[16,56,128]{2,1,0:T(8,128)S(1)}, u32[]{:S(2)}, u32[]{:S(2)}) collective-permute-start(f32[16,56,128]{2,1,0:T(8,128)S(1)} %get-tuple-element.25), channel_id=1, source_target_pairs={{0,4},{4,0},{1,5},{5,1},{2,6},{6,2},{3,7},{7,3},{8,12},{12,8},{9,1... | collective-permute-start | bytes 1376264 | tf_op jit(solution)/shard_map/ppermute | solution.py:203
  127.5 5.5 %collective-permute-start.3 = (f32[16,48,128]{2,1,0:T(8,128)S(1)}, f32[16,48,128]{2,1,0:T(8,128)S(1)}, u32[]{:S(2)}, u32[]{:S(2)}) collective-permute-start(f32[16,48,128]{2,1,0:T(8,128)S(1)} %all_to_all.67.own), channel_id=1, source_target_pairs={{0,4},{4,0},{1,5},{5,1},{2,6},{6,2},{3,7},{7,3},{8,12},{12,8},{9,1... | collective-permute-start | bytes 1179656 | tf_op jit(solution)/shard_map/ppermute | solution.py:323
  135.9 1.9 collective-permute-start.4
  173.9 5.5 %collective-permute-start.5 = (f32[16,48,128]{2,1,0:T(8,128)S(1)}, f32[16,48,128]{2,1,0:T(8,128)S(1)}, u32[]{:S(2)}, u32[]{:S(2)}) collective-permute-start(f32[16,48,128]{2,1,0:T(8,128)S(1)} %all_to_all.70.own), channel_id=1, source_target_pairs={{0,4},{4,0},{1,5},{5,1},{2,6},{6,2},{3,7},{7,3},{8,12},{12,8},{9,1... | collective-permute-start | bytes 1179656 | tf_op jit(solution)/shard_map/ppermute | solution.py:323
  182.3 1.9 collective-permute-start.6
  220.4 5.5 %collective-permute-start.7 = (f32[16,48,128]{2,1,0:T(8,128)S(1)}, f32[16,48,128]{2,1,0:T(8,128)S(1)}, u32[]{:S(2)}, u32[]{:S(2)}) collective-permute-start(f32[16,48,128]{2,1,0:T(8,128)S(1)} %all_to_all.73.own), channel_id=1, source_target_pairs={{0,4},{4,0},{1,5},{5,1},{2,6},{6,2},{3,7},{7,3},{8,12},{12,8},{9,1... | collective-permute-start | bytes 1179656 | tf_op jit(solution)/shard_map/ppermute | solution.py:323
  228.8 1.9 collective-permute-start.8
  266.9 5.5 %collective-permute-start.9 = (f32[16,48,128]{2,1,0:T(8,128)S(1)}, f32[16,48,128]{2,1,0:T(8,128)S(1)}, u32[]{:S(2)}, u32[]{:S(2)}) collective-permute-start(f32[16,48,128]{2,1,0:T(8,128)S(1)} %all_to_all.76.own), channel_id=1, source_target_pairs={{0,4},{4,0},{1,5},{5,1},{2,6},{6,2},{3,7},{7,3},{8,12},{12,8},{9,1... | collective-permute-start | bytes 1179656 | tf_op jit(solution)/shard_map/ppermute | solution.py:323
